TPU v7x, 32 devices: a whole 2x2x4 slice. The times are simulated.
32 devices in a mesh: blk: 4 (over y, x), uly: 8 (over z, core).
Axes of the slice: x: 2, y: 2, z: 4, core: 2. Of those that a mesh axis runs over, the one named last changes fastest.
Arguments:
- queries: bfloat16 [4096, 4096], P(('blk', 'uly')), may hold values from -1.5 to 1.5
- keys: bfloat16 [4096, 1024], P(('blk', 'uly')), may hold values from -1.5 to 1.5
- values: bfloat16 [4096, 1024], P(('blk', 'uly')), may hold values from -6 to 6
- grad_out: bfloat16 [4096, 4096], P(('blk', 'uly')), may hold values from -96 to 96
- row_lse: float32 [4096, 32], P('blk', 'uly'), may hold values from 6 to 7.5
- row_delta: float32 [4096, 32], P('blk', 'uly'), may hold values from -960 to 960
- pattern: int32 [32, 2], replicated, may hold values from 0 to 31, as said below
- memory_keys: bfloat16 [128, 4096], P(None, 'uly'), may hold values from -1.5 to 1.5
- memory_values: bfloat16 [128, 4096], P(None, 'uly'), may hold values from -6 to 6
Outputs:
- grad_queries: bfloat16 [4096, 4096], P(('blk', 'uly'))
- grad_keys: float32 [4096, 1024], P(('blk', 'uly'))
- grad_values: float32 [4096, 1024], P(('blk', 'uly'))
- grad_memory_keys: float32 [128, 4096], P(None, 'uly')
- grad_memory_values: float32 [128, 4096], P(None, 'uly')
Inputs may be any that keep to these rules, and one draw needn't show every extreme that they name: `pattern`: query block b lies in span b // 8. The rows of one span name exactly one block of every span that is neither that span nor beside it; all their other named blocks lie in the span itself.
All inputs are finite; a program needn't handle non-finite values.
Results may differ from a plain program's by a relative error of at most 0.0085.
Values may be sent and summed in bfloat16 or wider, within the bound.
No kernel may reach another device: no remote copies, remote signals or barrier semaphores. Data moves between devices by JAX's collectives and lax.ppermute only.
A program may use at most 64 MiB of HBM per device.

v0:
```python
import math

import jax
import jax.numpy as jnp
from jax import lax
from jax.sharding import PartitionSpec as P

QUERY_HEADS = 32
KEY_HEADS = 8
HEAD_FEATURES = 128
BLOCK = 128
RANDOM = 2


def shards(
    queries, keys, values, grad_out, row_lse, row_delta, pattern, memory_keys, memory_values
):
    span_count = lax.axis_size("blk")
    head_ways = lax.axis_size("uly")
    my_span = lax.axis_index("blk")
    present_rows = queries.shape[0]
    span_rows = present_rows * head_ways
    block_count = span_rows // BLOCK
    local_heads = QUERY_HEADS // head_ways
    group_width = QUERY_HEADS // KEY_HEADS
    entries = block_count * RANDOM
    score_scale = HEAD_FEATURES ** (-0.5)
    step_blocks = math.gcd(block_count, max(1, 512 // BLOCK))
    step_count = block_count // step_blocks
    pool_blocks = block_count + span_count + 1

    def widen_heads(key_value_rows):
        spread_rows = jnp.broadcast_to(
            key_value_rows.reshape(present_rows, KEY_HEADS, 1, HEAD_FEATURES),
            (present_rows, KEY_HEADS, group_width, HEAD_FEATURES),
        )
        return spread_rows.reshape(present_rows, QUERY_HEADS * HEAD_FEATURES)

    query_x, dout_x = (
        lax.all_to_all(queries, "uly", split_axis=1, concat_axis=0, tiled=True),
        lax.all_to_all(grad_out, "uly", split_axis=1, concat_axis=0, tiled=True),
    )
    key_x, value_x = (
        lax.all_to_all(widen_heads(keys), "uly", split_axis=1, concat_axis=0, tiled=True),
        lax.all_to_all(widen_heads(values), "uly", split_axis=1, concat_axis=0, tiled=True),
    )

    def by_head(wide_rows):
        return wide_rows.reshape(block_count, BLOCK, local_heads, HEAD_FEATURES).transpose(
            2, 0, 1, 3
        )

    def stat_head(stat_rows):
        return stat_rows.reshape(block_count, BLOCK, local_heads).transpose(2, 0, 1)

    query_heads = by_head(query_x)
    key_heads = by_head(key_x)
    value_heads = by_head(value_x)
    dout_heads = by_head(dout_x)
    lse_heads = stat_head(row_lse)
    delta_heads = stat_head(row_delta)
    flat_pattern = pattern.reshape(span_count, entries)
    owner_all = flat_pattern // block_count
    local_all = flat_pattern % block_count
    span_ids = jnp.arange(span_count, dtype=jnp.int32)
    near_span = jnp.abs(span_ids - my_span) == 1
    other_span = span_ids != my_span
    from_me = (owner_all == my_span) & other_span[:, None]
    named_block = jnp.sum(jnp.where(from_me, local_all, 0), axis=1)
    edge_block = jnp.where(span_ids > my_span, block_count - 1, 0)
    send_block = jnp.where(near_span, edge_block, named_block)
    my_pattern = lax.dynamic_slice_in_dim(flat_pattern, my_span, 1, 0)[0]
    my_owner = my_pattern // block_count
    random_index = jnp.where(my_owner == my_span, my_pattern % block_count, block_count + my_owner)
    random_index = random_index.reshape(block_count, RANDOM)
    block_ids = jnp.arange(block_count, dtype=jnp.int32)
    left_index = jnp.where(block_ids > 0, block_ids - 1, block_count + jnp.maximum(my_span - 1, 0))
    right_index = jnp.where(
        block_ids < block_count - 1,
        block_ids + 1,
        block_count + jnp.minimum(my_span + 1, span_count - 1),
    )
    memory_index = jnp.full((block_count, 1), block_count + span_count, jnp.int32)
    pair_index = jnp.concatenate(
        [left_index[:, None], block_ids[:, None], right_index[:, None], random_index, memory_index],
        axis=1,
    )
    left_ok = (block_ids > 0) | (my_span > 0)
    right_ok = (block_ids < block_count - 1) | (my_span < span_count - 1)
    pair_ok = jnp.concatenate(
        [
            left_ok[:, None],
            jnp.ones((block_count, 1), bool),
            right_ok[:, None],
            jnp.ones((block_count, RANDOM + 1), bool),
        ],
        axis=1,
    ).astype(jnp.float32)
    key_send = key_heads[:, send_block]
    value_send = value_heads[:, send_block]
    key_in, value_in = (
        lax.all_to_all(key_send, "blk", split_axis=1, concat_axis=1, tiled=True),
        lax.all_to_all(value_send, "blk", split_axis=1, concat_axis=1, tiled=True),
    )

    def memory_block(memory):
        return memory.reshape(BLOCK, local_heads, HEAD_FEATURES).transpose(1, 0, 2)[:, None]

    key_pool = jnp.concatenate([key_heads, key_in, memory_block(memory_keys)], axis=1)
    value_pool = jnp.concatenate([value_heads, value_in, memory_block(memory_values)], axis=1)

    def one_step(totals, step_id):
        key_acc, value_acc = totals
        first_block = step_id * step_blocks

        def take_part(array):
            return lax.dynamic_slice_in_dim(array, first_block, step_blocks, 1)

        query_part = take_part(query_heads)
        dout_part = take_part(dout_heads)
        lse_part = take_part(lse_heads)
        delta_part = take_part(delta_heads)
        index_part = lax.dynamic_slice_in_dim(pair_index, first_block, step_blocks, 0)
        valid_part = lax.dynamic_slice_in_dim(pair_ok, first_block, step_blocks, 0)
        key_sets = key_pool[:, index_part]
        value_sets = value_pool[:, index_part]
        scores = (
            jnp.einsum(
                "hnad,hnskd->hnsak", query_part, key_sets, preferred_element_type=jnp.float32
            )
            * score_scale
        )
        weights = (
            jnp.exp(scores - lse_part[:, :, None, :, None]) * valid_part[None, :, :, None, None]
        )
        dweights = jnp.einsum(
            "hnad,hnskd->hnsak", dout_part, value_sets, preferred_element_type=jnp.float32
        )
        dscores = weights * (dweights - delta_part[:, :, None, :, None])
        weight_bf = weights.astype(jnp.bfloat16)
        dscore_bf = dscores.astype(jnp.bfloat16)
        grad_q_part = (
            jnp.einsum("hnsak,hnskd->hnad", dscore_bf, key_sets, preferred_element_type=jnp.float32)
            * score_scale
        ).astype(jnp.bfloat16)
        key_term = (
            jnp.einsum(
                "hnsak,hnad->hnskd", dscore_bf, query_part, preferred_element_type=jnp.float32
            )
            * score_scale
        ).astype(jnp.bfloat16)
        value_term = jnp.einsum(
            "hnsak,hnad->hnskd", weight_bf, dout_part, preferred_element_type=jnp.float32
        ).astype(jnp.bfloat16)
        key_acc = key_acc.at[:, index_part].add(key_term.astype(jnp.float32))
        value_acc = value_acc.at[:, index_part].add(value_term.astype(jnp.float32))
        return ((key_acc, value_acc), grad_q_part)

    empty_pool = jnp.zeros((local_heads, pool_blocks, BLOCK, HEAD_FEATURES), jnp.float32)
    (key_acc, value_acc), grad_q_steps = lax.scan(
        one_step, (empty_pool, empty_pool), jnp.arange(step_count, dtype=jnp.int32)
    )
    grad_q = grad_q_steps.transpose(1, 0, 2, 3, 4).reshape(
        local_heads, block_count, BLOCK, HEAD_FEATURES
    )
    grad_k_local = key_acc[:, :block_count]
    grad_v_local = value_acc[:, :block_count]
    memory_dk = key_acc[:, block_count + span_count]
    memory_dv = value_acc[:, block_count + span_count]
    key_slots = key_acc[:, block_count : block_count + span_count].astype(jnp.bfloat16)
    value_slots = value_acc[:, block_count : block_count + span_count].astype(jnp.bfloat16)
    key_back, value_back = (
        lax.all_to_all(key_slots, "blk", split_axis=1, concat_axis=1, tiled=True),
        lax.all_to_all(value_slots, "blk", split_axis=1, concat_axis=1, tiled=True),
    )
    grad_k_local = grad_k_local.at[:, send_block].add(key_back.astype(jnp.float32))
    grad_v_local = grad_v_local.at[:, send_block].add(value_back.astype(jnp.float32))

    def to_rows(head_blocks):
        return head_blocks.transpose(1, 2, 0, 3).reshape(span_rows, local_heads * HEAD_FEATURES)

    grad_q_rows = lax.all_to_all(to_rows(grad_q), "uly", split_axis=0, concat_axis=1, tiled=True)
    grad_k_rows, grad_v_rows = (
        lax.all_to_all(
            to_rows(grad_k_local.astype(jnp.bfloat16)),
            "uly",
            split_axis=0,
            concat_axis=1,
            tiled=True,
        ),
        lax.all_to_all(
            to_rows(grad_v_local.astype(jnp.bfloat16)),
            "uly",
            split_axis=0,
            concat_axis=1,
            tiled=True,
        ),
    )

    def group_sum(rows_by_head):
        summed_terms = jnp.sum(
            rows_by_head.astype(jnp.float32).reshape(
                present_rows, KEY_HEADS, group_width, HEAD_FEATURES
            ),
            axis=2,
        )
        return summed_terms.reshape(present_rows, KEY_HEADS * HEAD_FEATURES)

    def memory_rows(memory_terms):
        return memory_terms.transpose(1, 0, 2).reshape(BLOCK, local_heads * HEAD_FEATURES)

    memory_keys_total, memory_values_total = lax.psum(
        (memory_rows(memory_dk), memory_rows(memory_dv)), "blk"
    )
    return (
        grad_q_rows,
        group_sum(grad_k_rows),
        group_sum(grad_v_rows),
        memory_keys_total,
        memory_values_total,
    )


def solution(mesh):
    in_specs = (
        P(("blk", "uly"), None),
        P(("blk", "uly"), None),
        P(("blk", "uly"), None),
        P(("blk", "uly"), None),
        P("blk", "uly"),
        P("blk", "uly"),
        P(),
        P(None, "uly"),
        P(None, "uly"),
    )
    out_specs = (
        P(("blk", "uly"), None),
        P(("blk", "uly"), None),
        P(("blk", "uly"), None),
        P(None, "uly"),
        P(None, "uly"),
    )
    return jax.shard_map(shards, mesh=mesh, in_specs=in_specs, out_specs=out_specs, check_vma=False)
```

profile of v0, /device:TPU:0, one launch (start us, length us, event | category | flops | bytes accessed | tf_op | source)
XLA Modules:
  0.0 418.6 jit_solution(17839844307571903224)
XLA Ops:
  9.6 6.3 %all-to-all-start.3 = ((bf16[128,8,512]{0,2,1:T(8,128)(2,1)}), bf16[128,8,512]{0,2,1:T(8,128)(2,1)S(1)}, u32[]{:S(2)}, u32[]{:S(2)}) async-start(bf16[128,8,512]{0,2,1:T(8,128)(2,1)} %bitcast.36), calls=%async_computation.3 | async-start | bytes 2097152 | tf_op jit(solution)/shard_map/all_to_all | solution.py:45
  16.1 26.4 %all-to-all-done.3 = bf16[128,8,512]{0,2,1:T(8,128)(2,1)S(1)} async-done(((bf16[128,8,512]{0,2,1:T(8,128)(2,1)}), bf16[128,8,512]{0,2,1:T(8,128)(2,1)S(1)}, u32[]{:S(2)}, u32[]{:S(2)}) %all-to-all-start.3) | async-done | bytes 1048608 | tf_op jit(solution)/shard_map/all_to_all | solution.py:45
  49.7 24.3 %all-to-all-done = bf16[128,8,512]{0,2,1:T(8,128)(2,1)S(1)} async-done(((bf16[128,8,512]{0,2,1:T(8,128)(2,1)}), bf16[128,8,512]{0,2,1:T(8,128)(2,1)S(1)}, u32[]{:S(2)}, u32[]{:S(2)}) %all-to-all-start) | async-done | bytes 1048608 | tf_op jit(solution)/shard_map/all_to_all | solution.py:44
  73.9 4.2 %all-to-all-start.2 = ((bf16[128,8,512]{0,2,1:T(8,128)(2,1)}), bf16[128,8,512]{0,2,1:T(8,128)(2,1)}, u32[]{:S(2)}, u32[]{:S(2)}) async-start(bf16[128,8,512]{0,2,1:T(8,128)(2,1)} %bitcast.30), calls=%async_computation.2 | async-start | bytes 2097152 | tf_op jit(solution)/shard_map/all_to_all | solution.py:40
  81.2 23.6 %all-to-all-done.2 = bf16[128,8,512]{0,2,1:T(8,128)(2,1)} async-done(((bf16[128,8,512]{0,2,1:T(8,128)(2,1)}), bf16[128,8,512]{0,2,1:T(8,128)(2,1)}, u32[]{:S(2)}, u32[]{:S(2)}) %all-to-all-start.2) | async-done | bytes 1048608 | tf_op jit(solution)/shard_map/all_to_all | solution.py:40
  111.0 6.1 %all-to-all-done.4 = bf16[4,4,128,128]{3,2,0,1:T(8,128)(2,1)} async-done(((bf16[4,4,128,128]{3,2,0,1:T(8,128)(2,1)}), bf16[4,4,128,128]{3,2,0,1:T(8,128)(2,1)}, u32[]{:S(2)}, u32[]{:S(2)}) %all-to-all-start.4) | async-done | bytes 524320 | tf_op jit(solution)/shard_map/all_to_all | solution.py:103
  122.8 5.0 %all-to-all-done.1 = bf16[4,4,128,128]{3,2,0,1:T(8,128)(2,1)S(1)} async-done(((bf16[4,4,128,128]{3,2,0,1:T(8,128)(2,1)}), bf16[4,4,128,128]{3,2,0,1:T(8,128)(2,1)S(1)}, u32[]{:S(2)}, u32[]{:S(2)}) %all-to-all-start.1) | async-done | bytes 524320 | tf_op jit(solution)/shard_map/all_to_all | solution.py:102
  127.7 4.4 %all-to-all-start.5 = ((bf16[128,8,512]{0,2,1:T(8,128)(2,1)}), bf16[128,8,512]{0,2,1:T(8,128)(2,1)}, u32[]{:S(2)}, u32[]{:S(2)}) async-start(bf16[128,8,512]{0,2,1:T(8,128)(2,1)} %bitcast.44), calls=%async_computation.5 | async-start | bytes 2097152 | tf_op jit(solution)/shard_map/all_to_all | solution.py:41
  137.1 21.5 %all-to-all-done.5 = bf16[128,8,512]{0,2,1:T(8,128)(2,1)} async-done(((bf16[128,8,512]{0,2,1:T(8,128)(2,1)}), bf16[128,8,512]{0,2,1:T(8,128)(2,1)}, u32[]{:S(2)}, u32[]{:S(2)}) %all-to-all-start.5) | async-done | bytes 1048608 | tf_op jit(solution)/shard_map/all_to_all | solution.py:41
  163.0 102.1 %while.14 = (s32[]{:T(128)}, f32[4,13,128,128]{3,2,1,0:T(8,128)}, f32[4,13,128,128]{3,2,1,0:T(8,128)}, bf16[2,4,4,128,128]{4,3,2,0,1:T(8,128)(2,1)}, s32[2]{0:T(...) while((s32[]{:T(128)}, f32[4,13,128,128]{3,2,1,0:T(8,128)}, ...), condition=%wide.region_5.6_spmd, body=%wide.region_2.5_spmd.sunk | while | flops 2040529920 | bytes 222885584 | solution.py:160
  186.4 9.2 %scatter_fusion.1 = f32[4,13,128,128]{3,2,1,0:T(8,128)S(1)} fusion(f32[4,13,128,128]{3,2,1,0:T(8,128)S(1)} %copy-done, s32[24]{0:T(128)S(1)} %reshape.306, f32[24,4,128,128]{3,2,1,0:T(8,128)} %copy.168), kind=kCustom, calls=%fused_computation.5.clone.1 | custom fusion | flops 1572864 | bytes 18874464 | tf_op jit(solution)/shard_map/while/body/eval_jaxpr/scatter-add | solution.py:156
  195.6 4.2 fusion.78
  203.1 9.2 %scatter_fusion = f32[4,13,128,128]{3,2,1,0:T(8,128)S(1)} fusion(f32[4,13,128,128]{3,2,1,0:T(8,128)S(1)} %copy-done.3, s32[24]{0:T(128)S(1)} %reshape.306, f32[24,4,128,128]{3,2,1,0:T(8,128)} %copy.167), kind=kCustom, calls=%fused_computation.4.clone.1 | custom fusion | flops 1572864 | bytes 18874464 | tf_op jit(solution)/shard_map/while/body/eval_jaxpr/scatter-add | solution.py:155
  237.5 9.1 %scatter_fusion.1 = f32[4,13,128,128]{3,2,1,0:T(8,128)S(1)} fusion(f32[4,13,128,128]{3,2,1,0:T(8,128)S(1)} %copy-done, s32[24]{0:T(128)S(1)} %reshape.306, f32[24,4,128,128]{3,2,1,0:T(8,128)} %copy.168), kind=kCustom, calls=%fused_computation.5.clone.1 | custom fusion | flops 1572864 | bytes 18874464 | tf_op jit(solution)/shard_map/while/body/eval_jaxpr/scatter-add | solution.py:156
  254.2 9.1 %scatter_fusion = f32[4,13,128,128]{3,2,1,0:T(8,128)S(1)} fusion(f32[4,13,128,128]{3,2,1,0:T(8,128)S(1)} %copy-done.3, s32[24]{0:T(128)S(1)} %reshape.306, f32[24,4,128,128]{3,2,1,0:T(8,128)} %copy.167), kind=kCustom, calls=%fused_computation.4.clone.1 | custom fusion | flops 1572864 | bytes 18874464 | tf_op jit(solution)/shard_map/while/body/eval_jaxpr/scatter-add | solution.py:155
  273.6 7.0 %all-to-all-done.7 = bf16[4,4,128,128]{3,2,0,1:T(8,128)(2,1)} async-done(((bf16[4,4,128,128]{3,2,0,1:T(8,128)(2,1)}), bf16[4,4,128,128]{3,2,0,1:T(8,128)(2,1)}, u32[]{:S(2)}, u32[]{:S(2)}) %all-to-all-start.7) | async-done | bytes 524320 | tf_op jit(solution)/shard_map/all_to_all | solution.py:173
  287.1 5.0 %all-to-all-done.9 = bf16[4,4,128,128]{3,2,0,1:T(8,128)(2,1)} async-done(((bf16[4,4,128,128]{3,2,0,1:T(8,128)(2,1)}), bf16[4,4,128,128]{3,2,0,1:T(8,128)(2,1)}, u32[]{:S(2)}, u32[]{:S(2)}) %all-to-all-start.9) | async-done | bytes 524320 | tf_op jit(solution)/shard_map/all_to_all | solution.py:174
  292.1 4.4 %all-to-all-start.6 = ((bf16[8,128,512]{1,2,0:T(8,128)(2,1)}), bf16[8,128,512]{1,2,0:T(8,128)(2,1)}, u32[]{:S(2)}, u32[]{:S(2)}) async-start(bf16[8,128,512]{1,2,0:T(8,128)(2,1)} %bitcast.218), calls=%async_computation.6 | async-start | bytes 2097152 | tf_op jit(solution)/shard_map/all_to_all | solution.py:182
  310.2 12.8 %all-to-all-done.6 = bf16[8,128,512]{1,2,0:T(8,128)(2,1)} async-done(((bf16[8,128,512]{1,2,0:T(8,128)(2,1)}), bf16[8,128,512]{1,2,0:T(8,128)(2,1)}, u32[]{:S(2)}, u32[]{:S(2)}) %all-to-all-start.6) | async-done | bytes 1048608 | tf_op jit(solution)/shard_map/all_to_all | solution.py:182
  323.1 4.2 %all-to-all-start.8 = ((bf16[8,128,512]{1,2,0:T(8,128)(2,1)}), bf16[8,128,512]{1,2,0:T(8,128)(2,1)}, u32[]{:S(2)}, u32[]{:S(2)}) async-start(bf16[8,128,512]{1,2,0:T(8,128)(2,1)} %bitcast.217), calls=%async_computation.8 | async-start | bytes 2097152 | tf_op jit(solution)/shard_map/all_to_all | solution.py:184
  339.4 14.5 %all-to-all-done.8 = bf16[8,128,512]{1,2,0:T(8,128)(2,1)} async-done(((bf16[8,128,512]{1,2,0:T(8,128)(2,1)}), bf16[8,128,512]{1,2,0:T(8,128)(2,1)}, u32[]{:S(2)}, u32[]{:S(2)}) %all-to-all-start.8) | async-done | bytes 1048608 | tf_op jit(solution)/shard_map/all_to_all | solution.py:184
  353.9 4.2 %all-to-all-start.10 = ((bf16[8,128,512]{1,2,0:T(8,128)(2,1)}), bf16[8,128,512]{1,2,0:T(8,128)(2,1)}, u32[]{:S(2)}, u32[]{:S(2)}) async-start(bf16[8,128,512]{1,2,0:T(8,128)(2,1)} %bitcast.216), calls=%async_computation.10 | async-start | bytes 2097152 | tf_op jit(solution)/shard_map/all_to_all | solution.py:191
  365.4 19.3 %all-to-all-done.10 = bf16[8,128,512]{1,2,0:T(8,128)(2,1)} async-done(((bf16[8,128,512]{1,2,0:T(8,128)(2,1)}), bf16[8,128,512]{1,2,0:T(8,128)(2,1)}, u32[]{:S(2)}, u32[]{:S(2)}) %all-to-all-start.10) | async-done | bytes 1048608 | tf_op jit(solution)/shard_map/all_to_all | solution.py:191
  387.3 21.2 %all-reduce.3.cloned.1.call-done = (f32[128,512]{1,0:T(8,128)}, f32[128,512]{1,0:T(8,128)}) async-done(((f32[128,512]{1,0:T(8,128)}, f32[128,512]{1,0:T(8,128)}), (f32[128,512]{1,0:T(8,128)}, f32[128,512]{1,0:T(8,128)})) %all-reduce.3.cloned.1.call-update) | async-done | bytes 524304 | tf_op jit(solution)/shard_map/psum | solution.py:212
  (165 shorter events, 147.4 us)
Async XLA Ops:
  7.2 8.7 %copy-start.10 = (bf16[128,1024]{1,0:T(8,128)(2,1)S(1)}, bf16[128,1024]{1,0:T(8,128)(2,1)}, u32[]{:S(2)}) copy-start(bf16[128,1024]{1,0:T(8,128)(2,1)} %param.12) | copy-start | bytes 786436
  9.6 32.9 %all-to-all-start.3 = ((bf16[128,8,512]{0,2,1:T(8,128)(2,1)}), bf16[128,8,512]{0,2,1:T(8,128)(2,1)S(1)}, u32[]{:S(2)}, u32[]{:S(2)}) async-start(bf16[128,8,512]{0,2,1:T(8,128)(2,1)} %bitcast.36), calls=%async_computation.3 | async-start | bytes 2097152 | tf_op jit(solution)/shard_map/all_to_all | solution.py:45
  43.7 34.6 %copy-start.17 = (s32[32,2]{0,1:T(2,128)S(1)}, s32[32,2]{0,1:T(2,128)}, u32[]{:S(2)}) copy-start(s32[32,2]{0,1:T(2,128)} %param.17) | copy-start | bytes 772
  43.7 30.2 %all-to-all-start = ((bf16[128,8,512]{0,2,1:T(8,128)(2,1)}), bf16[128,8,512]{0,2,1:T(8,128)(2,1)S(1)}, u32[]{:S(2)}, u32[]{:S(2)}) async-start(bf16[128,8,512]{0,2,1:T(8,128)(2,1)} %bitcast.20), calls=%async_computation | async-start | bytes 2097152 | tf_op jit(solution)/shard_map/all_to_all | solution.py:44
  73.9 30.8 %all-to-all-start.2 = ((bf16[128,8,512]{0,2,1:T(8,128)(2,1)}), bf16[128,8,512]{0,2,1:T(8,128)(2,1)}, u32[]{:S(2)}, u32[]{:S(2)}) async-start(bf16[128,8,512]{0,2,1:T(8,128)(2,1)} %bitcast.30), calls=%async_computation.2 | async-start | bytes 2097152 | tf_op jit(solution)/shard_map/all_to_all | solution.py:40
  104.7 12.3 %all-to-all-start.4 = ((bf16[4,4,128,128]{3,2,0,1:T(8,128)(2,1)}), bf16[4,4,128,128]{3,2,0,1:T(8,128)(2,1)}, u32[]{:S(2)}, u32[]{:S(2)}) async-start(bf16[4,4,128,128]{3,2,0,1:T(8,128)(2,1)} %bitcast.40), calls=%async_computation.4 | async-start | bytes 1048576 | tf_op jit(solution)/shard_map/all_to_all | solution.py:103
  109.6 23.0 %copy-start.11 = (bf16[128,512]{1,0:T(8,128)(2,1)S(1)}, bf16[128,512]{1,0:T(8,128)(2,1)}, u32[]{:S(2)}) copy-start(bf16[128,512]{1,0:T(8,128)(2,1)} %param.18) | copy-start | bytes 393220
  109.6 23.3 %copy-start.12 = (bf16[128,512]{1,0:T(8,128)(2,1)S(1)}, bf16[128,512]{1,0:T(8,128)(2,1)}, u32[]{:S(2)}) copy-start(bf16[128,512]{1,0:T(8,128)(2,1)} %param.19) | copy-start | bytes 393220
  111.0 22.4 %copy-start.13 = (f32[1024,4]{0,1:T(4,128)S(1)}, f32[1024,4]{0,1:T(4,128)}, u32[]{:S(2)}) copy-start(f32[1024,4]{0,1:T(4,128)} %param.16) | copy-start | bytes 49156
  111.0 22.4 %copy-start.14 = (f32[1024,4]{0,1:T(4,128)S(1)}, f32[1024,4]{0,1:T(4,128)}, u32[]{:S(2)}) copy-start(f32[1024,4]{0,1:T(4,128)} %param.15) | copy-start | bytes 49156
  117.0 10.7 %all-to-all-start.1 = ((bf16[4,4,128,128]{3,2,0,1:T(8,128)(2,1)}), bf16[4,4,128,128]{3,2,0,1:T(8,128)(2,1)S(1)}, u32[]{:S(2)}, u32[]{:S(2)}) async-start(bf16[4,4,128,128]{3,2,0,1:T(8,128)(2,1)} %bitcast.26), calls=%async_computation.1 | async-start | bytes 1048576 | tf_op jit(solution)/shard_map/all_to_all | solution.py:102
  127.7 30.8 %all-to-all-start.5 = ((bf16[128,8,512]{0,2,1:T(8,128)(2,1)}), bf16[128,8,512]{0,2,1:T(8,128)(2,1)}, u32[]{:S(2)}, u32[]{:S(2)}) async-start(bf16[128,8,512]{0,2,1:T(8,128)(2,1)} %bitcast.44), calls=%async_computation.5 | async-start | bytes 2097152 | tf_op jit(solution)/shard_map/all_to_all | solution.py:41
  176.7 3.6 copy-start.8
  195.5 4.2 %copy-start.1 = (f32[4,13,128,128]{3,2,1,0:T(8,128)}, f32[4,13,128,128]{3,2,1,0:T(8,128)S(1)}, u32[]{:S(2)}) copy-start(f32[4,13,128,128]{3,2,1,0:T(8,128)S(1)} %scatter_fusion.1) | copy-start | bytes 10223620 | tf_op jit(solution)/shard_map/while
  227.8 3.6 copy-start.8
  246.6 4.2 %copy-start.1 = (f32[4,13,128,128]{3,2,1,0:T(8,128)}, f32[4,13,128,128]{3,2,1,0:T(8,128)S(1)}, u32[]{:S(2)}) copy-start(f32[4,13,128,128]{3,2,1,0:T(8,128)S(1)} %scatter_fusion.1) | copy-start | bytes 10223620 | tf_op jit(solution)/shard_map/while
  265.1 7.4 %copy-start.2 = (f32[4,13,128,128]{3,2,1,0:T(8,128)S(1)}, f32[4,13,128,128]{3,2,1,0:T(8,128)}, u32[]{:S(2)}) copy-start(f32[4,13,128,128]{3,2,1,0:T(8,128)} %get-tuple-element.76) | copy-start | bytes 10223620
  268.3 12.3 %all-to-all-start.7 = ((bf16[4,4,128,128]{3,2,0,1:T(8,128)(2,1)}), bf16[4,4,128,128]{3,2,0,1:T(8,128)(2,1)}, u32[]{:S(2)}, u32[]{:S(2)}) async-start(bf16[4,4,128,128]{3,2,0,1:T(8,128)(2,1)} %slice.41), calls=%async_computation.7 | async-start | bytes 1048576 | tf_op jit(solution)/shard_map/all_to_all | solution.py:173
  280.6 11.4 %all-to-all-start.9 = ((bf16[4,4,128,128]{3,2,0,1:T(8,128)(2,1)}), bf16[4,4,128,128]{3,2,0,1:T(8,128)(2,1)}, u32[]{:S(2)}, u32[]{:S(2)}) async-start(bf16[4,4,128,128]{3,2,0,1:T(8,128)(2,1)} %slice.40), calls=%async_computation.9 | async-start | bytes 1048576 | tf_op jit(solution)/shard_map/all_to_all | solution.py:174
  292.1 9.7 %copy-start.16 = (s32[4]{0:T(128)S(1)}, s32[4]{0:T(128)}, u32[]{:S(2)}) copy-start(s32[4]{0:T(128)} %copy-done.15) | copy-start | bytes 52
  292.1 31.0 %all-to-all-start.6 = ((bf16[8,128,512]{1,2,0:T(8,128)(2,1)}), bf16[8,128,512]{1,2,0:T(8,128)(2,1)}, u32[]{:S(2)}, u32[]{:S(2)}) async-start(bf16[8,128,512]{1,2,0:T(8,128)(2,1)} %bitcast.218), calls=%async_computation.6 | async-start | bytes 2097152 | tf_op jit(solution)/shard_map/all_to_all | solution.py:182
  323.1 30.8 %all-to-all-start.8 = ((bf16[8,128,512]{1,2,0:T(8,128)(2,1)}), bf16[8,128,512]{1,2,0:T(8,128)(2,1)}, u32[]{:S(2)}, u32[]{:S(2)}) async-start(bf16[8,128,512]{1,2,0:T(8,128)(2,1)} %bitcast.217), calls=%async_computation.8 | async-start | bytes 2097152 | tf_op jit(solution)/shard_map/all_to_all | solution.py:184
  353.9 30.8 %all-to-all-start.10 = ((bf16[8,128,512]{1,2,0:T(8,128)(2,1)}), bf16[8,128,512]{1,2,0:T(8,128)(2,1)}, u32[]{:S(2)}, u32[]{:S(2)}) async-start(bf16[8,128,512]{1,2,0:T(8,128)(2,1)} %bitcast.216), calls=%async_computation.10 | async-start | bytes 2097152 | tf_op jit(solution)/shard_map/all_to_all | solution.py:191
  358.1 50.3 %all-reduce.3.cloned.1.call-start = ((), (), s32[]{:S(2)}) async-start(), calls=%async_computation.11 | async-start | bytes 1048576 | tf_op jit(solution)/shard_map/psum | solution.py:212
  (15 other events, 32.3 us)
Sparse Core Ops, SparseCore 0:
  362.5 45.8 all-reduce.2
where the time goes:
time: 421 us; the launch traced here: 419 us
  waiting for transfers between devices  187 us (44%)
  local copies, waits for them, and re-layouts  86.3 us (20%)
  other arithmetic  60.3 us (14%)
  starting transfers between devices  47.4 us (11%)
  matrix products  22 us (5%)
  between operations  14.3 us (3%)
    all_to_all x1, waiting for transfers between devices, shards(): lax.all_to_all(widen_heads(values), 'uly', split_axis=1, concat_axis=0, t...  26.4 us
    all_to_all x1, waiting for transfers between devices, shards(): lax.all_to_all(widen_heads(keys), 'uly', split_axis=1, concat_axis=0, til...  24.3 us
    all_to_all x1, waiting for transfers between devices, shards(): lax.all_to_all(queries, 'uly', split_axis=1, concat_axis=0, tiled=True)  23.6 us
    all_to_all x1, waiting for transfers between devices, shards(): lax.all_to_all(grad_out, 'uly', split_axis=1, concat_axis=0, tiled=True)  21.5 us
    psum x1, waiting for transfers between devices, shards(): lax.psum((memory_rows(memory_dk), memory_rows(memory_dv)), 'blk')  21.2 us
    all_to_all x1, waiting for transfers between devices, shards(): lax.all_to_all(to_rows(grad_v_local.astype(jnp.bfloat16)), 'uly', split_a...  19.3 us
    scatter-add x2, other arithmetic, one_step(): key_acc = key_acc.at[:, index_part].add(key_term.astype(jnp.float32))  18.3 us
    scatter-add x2, other arithmetic, one_step(): value_acc = value_acc.at[:, index_part].add(value_term.astype(jnp.float32))  18.3 us
  transfers between devices with their start and end apart: 12, of which 12 were waited for; matrix products, arithmetic and copies ran while one was open for 13% of the time, Pallas kernels for 0%

commit v1 on v0

v1 whole, which is shorter than its diff:
```python
import functools
import math

import jax
import jax.numpy as jnp
from jax import lax
from jax.experimental import pallas as pl
from jax.experimental.pallas import tpu as pltpu
from jax.sharding import PartitionSpec as P

QUERY_HEADS = 32
KEY_HEADS = 8
HEAD_FEATURES = 128
BLOCK = 128
RANDOM = 2
SEQ_PAIRS = RANDOM + 3
GROUP = QUERY_HEADS // KEY_HEADS
SCALE = HEAD_FEATURES ** (-0.5)
LOG2E = math.log2(math.e)
FAR = 1e30
NN = (((1,), (0,)), ((), ()))
NT = (((1,), (1,)), ((), ()))


def dot(left, right, dims=NN):
    return lax.dot_general(left, right, dims, preferred_element_type=jnp.float32)


def attention_kernel(
    index_ref,
    far_ref,
    qd_ref,
    kv_ref,
    slot_ref,
    stat_ref,
    mk_ref,
    mv_ref,
    dq_ref,
    acc_ref,
    dmk_ref,
    dmv_ref,
    kt_ref,
    mkt_ref,
):
    step = pl.program_id(0)
    block_count = kv_ref.shape[0]
    span_count = slot_ref.shape[0]
    heads = mk_ref.shape[1] // HEAD_FEATURES

    def col(head):
        return pl.ds(head * HEAD_FEATURES, HEAD_FEATURES)

    @pl.when(step == 0)
    def _():
        acc_ref[...] = jnp.zeros_like(acc_ref)
        dmk_ref[...] = jnp.zeros_like(dmk_ref)
        dmv_ref[...] = jnp.zeros_like(dmv_ref)
        for b in range(block_count):
            kt_ref[0, b] = kv_ref[b, 0]
            kt_ref[1, b] = kv_ref[b, 1]
            kt_ref[2, b] = kv_ref[b, 0].T
        for s in range(span_count):
            kt_ref[0, block_count + s] = slot_ref[s, 0]
            kt_ref[1, block_count + s] = slot_ref[s, 1]
            kt_ref[2, block_count + s] = slot_ref[s, 0].T
        for h in range(heads):
            mkt_ref[h] = mk_ref[:, col(h)].T

    index = [index_ref[step, j] for j in range(SEQ_PAIRS)]
    lse = stat_ref[0, 0:1, :] * LOG2E
    delta = stat_ref[0, 1:2, :]
    q_heads = [qd_ref[0, 0, :, col(h)] for h in range(heads)]
    do_heads = [qd_ref[0, 1, :, col(h)] for h in range(heads)]
    q_all = jnp.concatenate(q_heads, axis=0)
    do_all = jnp.concatenate(do_heads, axis=0)
    keys = jnp.concatenate([kt_ref[0, i] for i in index], axis=0)
    values = jnp.concatenate([kt_ref[1, i] for i in index], axis=0)
    keys_t = jnp.concatenate([kt_ref[2, i] for i in index], axis=1)

    def weigh(scores, dweights, lse_row):
        weights = jnp.exp2(scores * (SCALE * LOG2E) - lse_row)
        dscores = weights * (dweights - delta)
        return weights.astype(jnp.bfloat16), dscores.astype(jnp.bfloat16)

    scores = dot(keys, q_all, NT)
    dweights = dot(values, do_all, NT)
    parts = [
        weigh(
            scores[j * BLOCK : (j + 1) * BLOCK],
            dweights[j * BLOCK : (j + 1) * BLOCK],
            lse + far_ref[step, j],
        )
        for j in range(SEQ_PAIRS)
    ]
    weights = jnp.concatenate([w for w, _ in parts], axis=0)
    dscores = jnp.concatenate([d for _, d in parts], axis=0)
    dq_t = dot(keys_t, dscores)
    dk = dot(dscores, q_all)
    dv = dot(weights, do_all)
    for j, i in enumerate(index):
        rows = slice(j * BLOCK, (j + 1) * BLOCK)
        acc_ref[0, i] += dk[rows]
        acc_ref[1, i] += dv[rows]

    mem_scores = jnp.concatenate(
        [dot(mk_ref[:, col(h)], q_heads[h], NT) for h in range(heads)], axis=1
    )
    mem_dweights = jnp.concatenate(
        [dot(mv_ref[:, col(h)], do_heads[h], NT) for h in range(heads)], axis=1
    )
    mem_w, mem_d = weigh(mem_scores, mem_dweights, lse)
    for h in range(heads):
        lanes = slice(h * HEAD_FEATURES, (h + 1) * HEAD_FEATURES)
        dmk_ref[:, col(h)] += dot(mem_d[:, lanes], q_heads[h]) * SCALE
        dmv_ref[:, col(h)] += dot(mem_w[:, lanes], do_heads[h])
        head_dq = dq_t[:, lanes] + dot(mkt_ref[h], mem_d[:, lanes])
        dq_ref[0, :, col(h)] = (head_dq * SCALE).T.astype(jnp.bfloat16)


def attention(index, far, qd, kv, slots, stats, memory_keys, memory_values):
    block_count = qd.shape[0]
    width = qd.shape[3]
    pool = kv.shape[0] + slots.shape[0]
    whole = lambda shape: pl.BlockSpec(shape, lambda n, *_: (0,) * len(shape))
    pairs = block_count * (SEQ_PAIRS + 1) * width // HEAD_FEATURES
    return pl.pallas_call(
        attention_kernel,
        grid_spec=pltpu.PrefetchScalarGridSpec(
            num_scalar_prefetch=2,
            grid=(block_count,),
            in_specs=[
                pl.BlockSpec((1, 2, BLOCK, width), lambda n, *_: (n, 0, 0, 0)),
                whole(kv.shape),
                whole(slots.shape),
                pl.BlockSpec((1, 2, width), lambda n, *_: (n, 0, 0)),
                whole(memory_keys.shape),
                whole(memory_values.shape),
            ],
            out_specs=[
                pl.BlockSpec((1, BLOCK, width), lambda n, *_: (n, 0, 0)),
                whole((2, pool, BLOCK, HEAD_FEATURES)),
                whole((BLOCK, width)),
                whole((BLOCK, width)),
            ],
            scratch_shapes=[
                pltpu.VMEM((3, pool, BLOCK, HEAD_FEATURES), jnp.bfloat16),
                pltpu.VMEM((width // HEAD_FEATURES, BLOCK, HEAD_FEATURES), jnp.bfloat16),
            ],
        ),
        out_shape=[
            jax.ShapeDtypeStruct((block_count, BLOCK, width), jnp.bfloat16),
            jax.ShapeDtypeStruct((2, pool, BLOCK, HEAD_FEATURES), jnp.float32),
            jax.ShapeDtypeStruct((BLOCK, width), jnp.float32),
            jax.ShapeDtypeStruct((BLOCK, width), jnp.float32),
        ],
        compiler_params=pltpu.CompilerParams(vmem_limit_bytes=48 * 1024 * 1024),
        cost_estimate=pl.CostEstimate(
            flops=pairs * 10 * BLOCK * BLOCK * HEAD_FEATURES,
            bytes_accessed=8 * 1024 * 1024,
            transcendentals=pairs * BLOCK * BLOCK,
        ),
    )(index, far, qd, kv, slots, stats, memory_keys, memory_values)


def pair_tables(pattern, span_count, block_count, my_span):
    entries = block_count * RANDOM
    flat_pattern = pattern.reshape(span_count, entries)
    owner_all = flat_pattern // block_count
    local_all = flat_pattern % block_count
    span_ids = jnp.arange(span_count, dtype=jnp.int32)
    near_span = jnp.abs(span_ids - my_span) == 1
    from_me = (owner_all == my_span) & (span_ids != my_span)[:, None]
    named_block = jnp.sum(jnp.where(from_me, local_all, 0), axis=1)
    edge_block = jnp.where(span_ids > my_span, block_count - 1, 0)
    send_block = jnp.where(near_span, edge_block, named_block)
    my_pattern = lax.dynamic_slice_in_dim(flat_pattern, my_span, 1, 0)[0]
    my_owner = my_pattern // block_count
    random_index = jnp.where(my_owner == my_span, my_pattern % block_count, block_count + my_owner)
    random_index = random_index.reshape(block_count, RANDOM)
    block_ids = jnp.arange(block_count, dtype=jnp.int32)
    left_index = jnp.where(block_ids > 0, block_ids - 1, block_count + jnp.maximum(my_span - 1, 0))
    right_index = jnp.where(
        block_ids < block_count - 1,
        block_ids + 1,
        block_count + jnp.minimum(my_span + 1, span_count - 1),
    )
    pair_index = jnp.concatenate(
        [left_index[:, None], block_ids[:, None], right_index[:, None], random_index], axis=1
    )
    left_far = jnp.where((block_ids > 0) | (my_span > 0), 0.0, FAR)
    right_far = jnp.where((block_ids < block_count - 1) | (my_span < span_count - 1), 0.0, FAR)
    none = jnp.zeros((block_count,), jnp.float32)
    pair_far = jnp.stack([left_far, none, right_far, none, none], axis=1).astype(jnp.float32)
    return send_block, pair_index, pair_far


def shards(
    queries, keys, values, grad_out, row_lse, row_delta, pattern, memory_keys, memory_values
):
    span_count = lax.axis_size("blk")
    head_ways = lax.axis_size("uly")
    my_span = lax.axis_index("blk")
    present_rows = queries.shape[0]
    span_rows = present_rows * head_ways
    block_count = span_rows // BLOCK
    local_heads = QUERY_HEADS // head_ways
    width = local_heads * HEAD_FEATURES
    copies = GROUP // local_heads

    send_block, pair_index, pair_far = pair_tables(pattern, span_count, block_count, my_span)

    def pieces(rows, piece_width):
        return rows.reshape(present_rows, -1, piece_width).transpose(1, 0, 2)

    def key_pieces(rows):
        return jnp.repeat(pieces(rows, HEAD_FEATURES), copies, axis=0)

    kv_send = jnp.stack([key_pieces(keys), key_pieces(values)], axis=1)
    kv = lax.all_to_all(kv_send, "uly", 0, 0, tiled=True)
    qd_send = jnp.stack([pieces(queries, width), pieces(grad_out, width)], axis=1)
    qd = lax.all_to_all(qd_send, "uly", 0, 0, tiled=True)
    slots = lax.all_to_all(kv[send_block], "blk", 0, 0, tiled=True)

    def stat_rows(stat):
        return (
            stat.reshape(block_count, BLOCK, local_heads)
            .transpose(0, 2, 1)
            .reshape(block_count, 1, width)
        )

    stats = jnp.concatenate([stat_rows(row_lse), stat_rows(row_delta)], axis=1)
    grad_q, acc, memory_dk, memory_dv = attention(
        pair_index, pair_far, qd, kv, slots, stats, memory_keys, memory_values
    )
    back = acc[:, block_count:].transpose(1, 0, 2, 3).astype(jnp.bfloat16)
    back = lax.all_to_all(back, "blk", 0, 0, tiled=True)
    chosen = jax.nn.one_hot(send_block, block_count, dtype=jnp.float32)
    total = acc[:, :block_count].transpose(1, 0, 2, 3)
    total = total + jnp.einsum(
        "sb,strd->btrd", chosen, back.astype(jnp.float32), precision=lax.Precision.HIGHEST
    )
    scale = jnp.array([SCALE, 1.0], jnp.float32)[None, :, None, None]
    total = (total * scale).astype(jnp.bfloat16)
    grad_q = lax.all_to_all(grad_q, "uly", 0, 0, tiled=True)
    grad_kv = lax.all_to_all(total, "uly", 0, 0, tiled=True)
    grad_kv = jnp.sum(
        grad_kv.astype(jnp.float32).reshape(KEY_HEADS, copies, 2, present_rows, HEAD_FEATURES),
        axis=1,
    )
    grad_k = grad_kv[:, 0].transpose(1, 0, 2).reshape(present_rows, KEY_HEADS * HEAD_FEATURES)
    grad_v = grad_kv[:, 1].transpose(1, 0, 2).reshape(present_rows, KEY_HEADS * HEAD_FEATURES)
    grad_q = grad_q.transpose(1, 0, 2).reshape(present_rows, QUERY_HEADS * HEAD_FEATURES)
    memory_dk, memory_dv = lax.psum((memory_dk, memory_dv), "blk")
    return grad_q, grad_k, grad_v, memory_dk, memory_dv


def solution(mesh):
    in_specs = (
        P(("blk", "uly"), None),
        P(("blk", "uly"), None),
        P(("blk", "uly"), None),
        P(("blk", "uly"), None),
        P("blk", "uly"),
        P("blk", "uly"),
        P(),
        P(None, "uly"),
        P(None, "uly"),
    )
    out_specs = (
        P(("blk", "uly"), None),
        P(("blk", "uly"), None),
        P(("blk", "uly"), None),
        P(None, "uly"),
        P(None, "uly"),
    )
    return jax.shard_map(shards, mesh=mesh, in_specs=in_specs, out_specs=out_specs, check_vma=False)
```

time: 421 us -> 206 us (0.49)
  waiting for transfers between devices: 187 us -> 114 us
  local copies, waits for them, and re-layouts: 86.3 us -> 17.2 us
  other arithmetic: 60.3 us -> 4.27 us
  starting transfers between devices: 47.4 us -> 22.3 us
  matrix products: 22 us -> 0.41 us
  blocking collectives: 0 us -> 17.9 us
  Pallas kernels: 0 us -> 14.5 us
    all_to_all x11 -> x5, waiting for transfers between devices: 165 us -> 92.1 us  [the longest x1 48.4 us: shards(): qd = lax.all_to_all(qd_send, 'uly', 0, 0, tiled=True)]
    scatter-add x6 -> x0, other arithmetic: 43.6 us -> none  [the longest x2 18.3 us: one_step(): key_acc = key_acc.at[:, index_part].add(key_term.astype(jnp.float32))]
    all_to_all x11 -> x5, starting transfers between devices: 47.4 us -> 22.3 us  [the longest x1 6.33 us: shards(): kv = lax.all_to_all(kv_send, 'uly', 0, 0, tiled=True)]
    dot_general x10 -> x1, matrix products: 22 us -> 0.41 us  [shards(): jnp.einsum('sb,strd->btrd', chosen, back.astype(jnp.float32), precision=l...]
    all_to_all x0 -> x1, blocking collectives: none -> 17.9 us  [shards(): grad_kv = lax.all_to_all(total, 'uly', 0, 0, tiled=True)]
    gather x6 -> x1, local copies, waits for them, and re-layouts: 16.3 us -> 1.28 us  [shards(): slots = lax.all_to_all(kv[send_block], 'blk', 0, 0, tiled=True)]
    pallas_call x0 -> x1, Pallas kernels: none -> 14.5 us  [attention(): pl.pallas_call(attention_kernel, grid_spec=pltpu.PrefetchScalarGridSpec(n...]
    convert_element_type x4 -> x3, local copies, waits for them, and re-layouts: 12.9 us -> 0.8 us  [the longest x2 0.76 us: shards(): back = acc[:, block_count:].transpose(1, 0, 2, 3).astype(jnp.bfloat16)]
  transfers between devices with their start and end apart: 12 -> 6, of which waited for: 12 -> 5; matrix products, arithmetic and copies ran while one was open for 13% -> 6% of each run, Pallas kernels for 0% -> 0%
where the time goes in v1:
time: 206 us; the launch traced here: 205 us
  waiting for transfers between devices  114 us (55%)
  starting transfers between devices  22.3 us (11%)
  blocking collectives  17.9 us (9%)
  local copies, waits for them, and re-layouts  17.2 us (8%)
  Pallas kernels  14.5 us (7%)
  between operations  14.3 us (7%)
  other arithmetic  4.27 us (2%)
    all_to_all x1, waiting for transfers between devices, shards(): qd = lax.all_to_all(qd_send, 'uly', 0, 0, tiled=True)  48.4 us
    all_to_all x1, waiting for transfers between devices, shards(): grad_q = lax.all_to_all(grad_q, 'uly', 0, 0, tiled=True)  23.4 us
    psum x1, waiting for transfers between devices, shards(): memory_dk, memory_dv = lax.psum((memory_dk, memory_dv), 'blk')  21.6 us
    all_to_all x1, blocking collectives, shards(): grad_kv = lax.all_to_all(total, 'uly', 0, 0, tiled=True)  17.9 us
    all_to_all x1, waiting for transfers between devices, shards(): kv = lax.all_to_all(kv_send, 'uly', 0, 0, tiled=True)  14.9 us
    pallas_call x1, Pallas kernels, attention(): pl.pallas_call(attention_kernel, grid_spec=pltpu.PrefetchScalarGridSpec(n...  14.5 us
    unnamed x24, local copies, waits for them, and re-layouts  11.4 us
    all_to_all x1, starting transfers between devices, shards(): kv = lax.all_to_all(kv_send, 'uly', 0, 0, tiled=True)  6.33 us
  transfers between devices with their start and end apart: 6, of which 5 were waited for; matrix products, arithmetic and copies ran while one was open for 6% of the time, Pallas kernels for 0%

profile of v1, /device:TPU:0, one launch (start us, length us, event | category | flops | bytes accessed | tf_op | source)
XLA Modules:
  0.0 205.2 jit_solution(17778745596775441410)
XLA Ops:
  7.2 1.1 copy.44
  8.5 1.2 copy.46
  9.9 0.8 pad_maximum_fusion.1
  10.8 6.3 %all-to-all-start.1 = ((bf16[8,2,128,128]{3,2,1,0:T(8,128)(2,1)}), bf16[8,2,128,128]{3,2,1,0:T(8,128)(2,1)S(1)}, u32[]{:S(2)}, u32[]{:S(2)}) async-start(bf16[8,2,128,128]{3,2,1,0:T(8,128)(2,1)} %pad_maximum_fusion.1), calls=%async_computation.1 | async-start | bytes 1048576 | tf_op jit(solution)/shard_map/all_to_all | solution.py:219
  17.5 14.9 %all-to-all-done.1.kv_ref = bf16[8,2,128,128]{3,2,1,0:T(8,128)(2,1)S(1)} async-done(((bf16[8,2,128,128]{3,2,1,0:T(8,128)(2,1)}), bf16[8,2,128,128]{3,2,1,0:T(8,128)(2,1)S(1)}, u32[]{:S(2)}, u32[]{:S(2)}) %all-to-all-start.1) | async-done | bytes 524320 | tf_op jit(solution)/shard_map/all_to_all | solution.py:219
  32.4 1.3 gather_fusion
  33.7 3.7 %all-to-all-start.2 = ((bf16[4,2,128,128]{3,2,1,0:T(8,128)(2,1)}), bf16[4,2,128,128]{3,2,1,0:T(8,128)(2,1)S(1)}, u32[]{:S(2)}, u32[]{:S(2)}) async-start(bf16[4,2,128,128]{3,2,1,0:T(8,128)(2,1)} %gather_fusion), calls=%async_computation.2 | async-start | bytes 524288 | tf_op jit(solution)/shard_map/all_to_all | solution.py:222
  38.6 1.6 copy.42
  40.3 1.3 copy.43
  41.6 2.7 %pad_maximum_fusion = bf16[8,2,128,512]{3,2,1,0:T(8,128)(2,1)} fusion(bf16[8,1,128,512]{3,2,1,0:T(8,128)(2,1)} %bitcast.62, bf16[8,1,128,512]{3,2,1,0:T(8,128)(2,1)S(1)} %bitcast.61), kind=kLoop, calls=%fused_computation.1 | loop fusion | flops 1048576 | bytes 4194304 | tf_op jit(solution)/shard_map/stack | solution.py:220
  44.3 4.5 %all-to-all-start = ((bf16[8,2,128,512]{3,2,1,0:T(8,128)(2,1)}), bf16[8,2,128,512]{3,2,1,0:T(8,128)(2,1)}, u32[]{:S(2)}, u32[]{:S(2)}) async-start(bf16[8,2,128,512]{3,2,1,0:T(8,128)(2,1)} %pad_maximum_fusion), calls=%async_computation | async-start | bytes 4194304 | tf_op jit(solution)/shard_map/all_to_all | solution.py:221
  49.5 48.4 %all-to-all-done.qd_ref = bf16[8,2,128,512]{3,2,1,0:T(8,128)(2,1)} async-done(((bf16[8,2,128,512]{3,2,1,0:T(8,128)(2,1)}), bf16[8,2,128,512]{3,2,1,0:T(8,128)(2,1)}, u32[]{:S(2)}, u32[]{:S(2)}) %all-to-all-start) | async-done | bytes 2097184 | tf_op jit(solution)/shard_map/all_to_all | solution.py:221
  97.9 14.5 %shard_map.137 = (bf16[8,128,512]{2,1,0:T(8,128)(2,1)}, f32[2,12,128,128]{3,2,1,0:T(8,128)S(1)}, f32[128,512]{1,0:T(8,128)}, f32[128,512]{1,0:T(8,128)}) custom-call(s32[8,5]{1,0:T(8,128)S(1)} %pad_add_fusion.index_ref, f32[8,5]{1,0:T(8,128)S(1)} %maximum_maximum_fusion.far_ref, bf16[8,2,128,512]{3,2,1,0:T(8,128)(2,1)} %all-to-all-done.qd_ref, ...), custom_call_target="tpu_custom_call" | custom-call | flops 4026531840 | bytes 8388608 | tf_op jit(solution)/shard_map/pallas_call | solution.py:126
  113.1 4.2 %all-to-all-start.4 = ((bf16[4,2,128,128]{3,2,1,0:T(8,128)(2,1)}), bf16[4,2,128,128]{3,2,1,0:T(8,128)(2,1)S(1)}, u32[]{:S(2)}, u32[]{:S(2)}) async-start(bf16[4,2,128,128]{3,2,1,0:T(8,128)(2,1)} %copy.51), calls=%async_computation.4 | async-start | bytes 524288 | tf_op jit(solution)/shard_map/all_to_all | solution.py:236
  117.3 5.4 %all-to-all-done.4 = bf16[4,2,128,128]{3,2,1,0:T(8,128)(2,1)S(1)} async-done(((bf16[4,2,128,128]{3,2,1,0:T(8,128)(2,1)}), bf16[4,2,128,128]{3,2,1,0:T(8,128)(2,1)S(1)}, u32[]{:S(2)}, u32[]{:S(2)}) %all-to-all-start.4) | async-done | bytes 262176 | tf_op jit(solution)/shard_map/all_to_all | solution.py:236
  123.5 17.9 %all_to_all.30 = bf16[8,2,128,128]{3,2,1,0:T(8,128)(2,1)S(1)} all-to-all(bf16[8,2,128,128]{3,2,1,0:T(8,128)(2,1)S(1)} %copy.54), channel_id=1, replica_groups=mesh['blk'=4,'uly'=8] {'uly'}, dimensions={0} | all-to-all | bytes 1048576 | tf_op jit(solution)/shard_map/all_to_all | solution.py:245
  141.4 3.6 %all-to-all-start.3 = ((bf16[8,128,512]{2,1,0:T(8,128)(2,1)}), bf16[8,128,512]{2,1,0:T(8,128)(2,1)S(1)}, u32[]{:S(2)}, u32[]{:S(2)}) async-start(bf16[8,128,512]{2,1,0:T(8,128)(2,1)} %get-tuple-element.9), calls=%async_computation.3 | async-start | bytes 2097152 | tf_op jit(solution)/shard_map/all_to_all | solution.py:244
  146.1 1.0 copy.58
  147.1 1.0 copy.57
  148.1 23.4 %all-to-all-done.3 = bf16[8,128,512]{2,1,0:T(8,128)(2,1)S(1)} async-done(((bf16[8,128,512]{2,1,0:T(8,128)(2,1)}), bf16[8,128,512]{2,1,0:T(8,128)(2,1)S(1)}, u32[]{:S(2)}, u32[]{:S(2)}) %all-to-all-start.3) | async-done | bytes 1048608 | tf_op jit(solution)/shard_map/all_to_all | solution.py:244
  172.1 1.3 copy.56
  173.4 21.6 %all-reduce.3.cloned.1.call-done = (f32[128,512]{1,0:T(8,128)}, f32[128,512]{1,0:T(8,128)}) async-done(((f32[128,512]{1,0:T(8,128)}, f32[128,512]{1,0:T(8,128)}), (f32[128,512]{1,0:T(8,128)}, f32[128,512]{1,0:T(8,128)})) %all-reduce.3.cloned.1.call-update) | async-done | bytes 524304 | tf_op jit(solution)/shard_map/psum | solution.py:253
  195.1 1.7 copy.65
  196.7 1.7 copy.66
  (52 shorter events, 5.8 us)
Async XLA Ops:
  7.2 10.1 %copy-start.5 = (s32[32,2]{0,1:T(2,128)S(1)}, s32[32,2]{0,1:T(2,128)}, u32[]{:S(2)}) copy-start(s32[32,2]{0,1:T(2,128)} %param.16) | copy-start | bytes 772
  8.5 28.9 %copy-start.2 = (bf16[128,4096]{1,0:T(8,128)(2,1)S(1)}, bf16[128,4096]{1,0:T(8,128)(2,1)}, u32[]{:S(2)}) copy-start(bf16[128,4096]{1,0:T(8,128)(2,1)} %param.10) | copy-start | bytes 3145732
  10.8 21.7 %all-to-all-start.1 = ((bf16[8,2,128,128]{3,2,1,0:T(8,128)(2,1)}), bf16[8,2,128,128]{3,2,1,0:T(8,128)(2,1)S(1)}, u32[]{:S(2)}, u32[]{:S(2)}) async-start(bf16[8,2,128,128]{3,2,1,0:T(8,128)(2,1)} %pad_maximum_fusion.1), calls=%async_computation.1 | async-start | bytes 1048576 | tf_op jit(solution)/shard_map/all_to_all | solution.py:219
  33.7 10.6 %all-to-all-start.2 = ((bf16[4,2,128,128]{3,2,1,0:T(8,128)(2,1)}), bf16[4,2,128,128]{3,2,1,0:T(8,128)(2,1)S(1)}, u32[]{:S(2)}, u32[]{:S(2)}) async-start(bf16[4,2,128,128]{3,2,1,0:T(8,128)(2,1)} %gather_fusion), calls=%async_computation.2 | async-start | bytes 524288 | tf_op jit(solution)/shard_map/all_to_all | solution.py:222
  44.3 5.0 %copy-start.3 = (f32[1024,4]{0,1:T(4,128)S(1)}, f32[1024,4]{0,1:T(4,128)}, u32[]{:S(2)}) copy-start(f32[1024,4]{0,1:T(4,128)} %param.15) | copy-start | bytes 49156
  44.3 5.0 %copy-start.4 = (f32[1024,4]{0,1:T(4,128)S(1)}, f32[1024,4]{0,1:T(4,128)}, u32[]{:S(2)}) copy-start(f32[1024,4]{0,1:T(4,128)} %param.14) | copy-start | bytes 49156
  44.3 53.6 %copy-start = (bf16[128,512]{1,0:T(8,128)(2,1)S(1)}, bf16[128,512]{1,0:T(8,128)(2,1)}, u32[]{:S(2)}) copy-start(bf16[128,512]{1,0:T(8,128)(2,1)} %mk_ref.1) | copy-start | bytes 393220
  44.3 53.6 %copy-start.1 = (bf16[128,512]{1,0:T(8,128)(2,1)S(1)}, bf16[128,512]{1,0:T(8,128)(2,1)}, u32[]{:S(2)}) copy-start(bf16[128,512]{1,0:T(8,128)(2,1)} %mv_ref.1) | copy-start | bytes 393220
  44.3 53.6 %all-to-all-start = ((bf16[8,2,128,512]{3,2,1,0:T(8,128)(2,1)}), bf16[8,2,128,512]{3,2,1,0:T(8,128)(2,1)}, u32[]{:S(2)}, u32[]{:S(2)}) async-start(bf16[8,2,128,512]{3,2,1,0:T(8,128)(2,1)} %pad_maximum_fusion), calls=%async_computation | async-start | bytes 4194304 | tf_op jit(solution)/shard_map/all_to_all | solution.py:221
  112.4 10.8 %copy-start.6 = (f32[2]{0:T(128)S(1)}, f32[2]{0:T(128)}, u32[]{:S(2)}) copy-start(f32[2]{0:T(128)} %constant.73.clone) | copy-start | bytes 28
  113.1 9.6 %all-to-all-start.4 = ((bf16[4,2,128,128]{3,2,1,0:T(8,128)(2,1)}), bf16[4,2,128,128]{3,2,1,0:T(8,128)(2,1)S(1)}, u32[]{:S(2)}, u32[]{:S(2)}) async-start(bf16[4,2,128,128]{3,2,1,0:T(8,128)(2,1)} %copy.51), calls=%async_computation.4 | async-start | bytes 524288 | tf_op jit(solution)/shard_map/all_to_all | solution.py:236
  141.4 30.1 %all-to-all-start.3 = ((bf16[8,128,512]{2,1,0:T(8,128)(2,1)}), bf16[8,128,512]{2,1,0:T(8,128)(2,1)S(1)}, u32[]{:S(2)}, u32[]{:S(2)}) async-start(bf16[8,128,512]{2,1,0:T(8,128)(2,1)} %get-tuple-element.9), calls=%async_computation.3 | async-start | bytes 2097152 | tf_op jit(solution)/shard_map/all_to_all | solution.py:244
  144.9 50.1 %all-reduce.3.cloned.1.call-start = ((), (), s32[]{:S(2)}) async-start(), calls=%async_computation.6 | async-start | bytes 1048576 | tf_op jit(solution)/shard_map/psum | solution.py:253
Sparse Core Ops, SparseCore 0:
  149.3 45.6 all-reduce.2

commit v2 on v0

v2 whole, which is shorter than its diff:
```python
import functools
import math

import jax
import jax.numpy as jnp
from jax import lax
from jax.experimental import pallas as pl
from jax.experimental.pallas import tpu as pltpu
from jax.sharding import PartitionSpec as P

QUERY_HEADS = 32
KEY_HEADS = 8
HEAD_FEATURES = 128
BLOCK = 128
RANDOM = 2
SEQ_PAIRS = RANDOM + 3
GROUP = QUERY_HEADS // KEY_HEADS
SCALE = HEAD_FEATURES ** (-0.5)
LOG2E = math.log2(math.e)
FAR = 1e30
MAX_PERMUTES = 8
VMEM_LIMIT = 24 * 1024 * 1024
NN = (((1,), (0,)), ((), ()))
NT = (((1,), (1,)), ((), ()))
SMEM_SPEC = pl.BlockSpec(memory_space=pltpu.SMEM)
VMEM_SPEC = pl.BlockSpec(memory_space=pltpu.VMEM)


def dot(left, right, dims=NN):
    return lax.dot_general(left, right, dims, preferred_element_type=jnp.float32)


def col(at, width=HEAD_FEATURES):
    if isinstance(at, int):
        return pl.ds(at * width, width)
    return pl.ds(pl.multiple_of(at * width, width), width)


def even(n):
    return n & (n - 1) == 0


def partner(me, k, n):
    return me ^ k if even(n) else lax.rem(k - me + n, n)


def skipped(k, n):
    return even(n) and k == 0


def exchange(pieces, axis):
    n = lax.axis_size(axis)
    if even(n) and n <= MAX_PERMUTES:
        return [pieces[0]] + [
            lax.ppermute(pieces[k], axis, [(i, i ^ k) for i in range(n)]) for k in range(1, n)
        ]
    order = partner(lax.axis_index(axis), jnp.arange(n, dtype=jnp.int32), n)
    sent = jnp.stack(pieces)[order]
    return list(lax.all_to_all(sent, axis, 0, 0, tiled=True)[order])


def call(kernel, outs, ctl, *operands, scratch=(), flops=0, trans=0):
    moved = sum(math.prod(x.shape) * x.dtype.itemsize for x in [*operands, *outs])
    return pl.pallas_call(
        kernel,
        in_specs=[SMEM_SPEC] + [VMEM_SPEC] * len(operands),
        out_specs=[VMEM_SPEC] * len(outs),
        out_shape=[jax.ShapeDtypeStruct(x.shape, x.dtype) for x in outs],
        scratch_shapes=list(scratch),
        compiler_params=pltpu.CompilerParams(vmem_limit_bytes=VMEM_LIMIT),
        cost_estimate=pl.CostEstimate(flops=flops, bytes_accessed=moved, transcendentals=trans),
    )(ctl, *operands)


def array(shape, dtype=jnp.bfloat16):
    return jax.ShapeDtypeStruct(shape, dtype)


class Layout:
    def __init__(self, ways, spans):
        self.ways = ways
        self.spans = spans
        self.heads = QUERY_HEADS // ways
        self.width = self.heads * HEAD_FEATURES
        self.mem_rows = BLOCK // spans if BLOCK % spans == 0 else 0

    def key_head(self, device):
        return lax.div(device * self.heads, GROUP)

    def pool_index(self, ctl, block):
        me, span = ctl[0], ctl[1]
        owner = lax.div(block, self.ways)
        local = lax.rem(block, self.ways)
        mine = partner(me, local, self.ways)
        slot = self.ways + partner(span, owner, self.spans)
        return jnp.where(owner == span, mine, slot)

    def pairs(self, ctl, k):
        me, span = ctl[0], ctl[1]
        block = span * self.ways + partner(me, k, self.ways)
        last = self.ways * self.spans - 1
        index = [
            self.pool_index(ctl, jnp.maximum(block - 1, 0)),
            self.pool_index(ctl, block),
            self.pool_index(ctl, jnp.minimum(block + 1, last)),
        ]
        index += [self.pool_index(ctl, ctl[2 + block * RANDOM + r]) for r in range(RANDOM)]
        far = [jnp.where(block == 0, FAR, 0.0), 0.0, jnp.where(block == last, FAR, 0.0)]
        return index, far + [0.0] * RANDOM

    def send_index(self, ctl, k):
        me, span = ctl[0], ctl[1]
        other = partner(span, k, self.spans)
        entries = self.ways * RANDOM

        def look(e, found):
            block = ctl[2 + other * entries + e]
            return jnp.where(lax.div(block, self.ways) == span, lax.rem(block, self.ways), found)

        named = lax.fori_loop(0, entries, look, jnp.int32(0))
        local = jnp.where(
            other == span + 1, self.ways - 1, jnp.where(other == span - 1, 0, named)
        )
        return partner(me, local, self.ways)


def cut_kernel(lay, column, ctl, *refs):
    first, second, *pieces = refs
    for k, piece in enumerate(pieces):
        at = col(column(partner(ctl[0], k, lay.ways)), piece.shape[2])
        piece[0] = first[:, at]
        piece[1] = second[:, at]


def cut(lay, column, ctl, first, second, width):
    return call(
        functools.partial(cut_kernel, lay, column),
        [array((2, BLOCK, width))] * lay.ways,
        ctl,
        first,
        second,
    )


def pool_kernel(lay, ctl, *refs):
    pieces = refs[: lay.ways]
    pool, *slots = refs[lay.ways :]
    for k, piece in enumerate(pieces):
        pool[k, 0] = piece[0]
        pool[k, 1] = piece[1]
        pool[k, 2] = piece[0].T
    for k, slot in enumerate(slots):
        if not skipped(k, lay.spans):
            at = lay.send_index(ctl, k)
            slot[0] = pool[at, 0]
            slot[1] = pool[at, 1]
        else:
            slot[...] = pieces[0][...]


def attention_kernel(lay, ks, first, last, ctl, *refs):
    refs = list(refs)
    take = lambda n: [refs.pop(0) for _ in range(n)]
    looped = len(ks) > MAX_PERMUTES // 2
    qds = take(1 if looped else len(ks))
    (pool,) = take(1)
    slots = take(lay.spans)
    stats, mk, mv = take(3)
    if not first:
        prev = take(3)
    dqs = take(1 if looped else len(ks))
    if last:
        local, own_mem = take(2)
        backs = take(lay.spans)
        acc, dmk, dmv, slot_pool, mkt = take(5)
    else:
        acc, dmk, dmv = take(3)
        slot_pool, mkt = take(2)
    heads = range(lay.heads)
    ways = lay.ways
    if first:
        for total in (acc, dmk, dmv):
            total[...] = jnp.zeros_like(total)
    else:
        for total, before in zip((acc, dmk, dmv), prev):
            total[...] = before[...]
    slot_pool[:ways] = pool[...]
    for s, slot in enumerate(slots):
        slot_pool[ways + s, 0] = slot[0]
        slot_pool[ways + s, 1] = slot[1]
        slot_pool[ways + s, 2] = slot[0].T
    for h in heads:
        mkt[h] = mk[:, col(h)].T

    def one_block(k, qd, dq):
        index, far = lay.pairs(ctl, k)
        stat = stats[partner(ctl[0], k, ways)]
        lse = jnp.concatenate([stat[h : h + 1] for h in heads], axis=1) * LOG2E
        delta = jnp.concatenate([stat[lay.heads + h : lay.heads + h + 1] for h in heads], axis=1)
        q_heads = [qd[0, :, col(h)] for h in heads]
        do_heads = [qd[1, :, col(h)] for h in heads]
        q_all = jnp.concatenate(q_heads, axis=0)
        do_all = jnp.concatenate(do_heads, axis=0)
        keys = jnp.concatenate([slot_pool[i, 0] for i in index], axis=0)
        values = jnp.concatenate([slot_pool[i, 1] for i in index], axis=0)
        keys_t = jnp.concatenate([slot_pool[i, 2] for i in index], axis=1)

        def weigh(scores, dweights, lse_row):
            weights = jnp.exp2(scores * (SCALE * LOG2E) - lse_row)
            dscores = weights * (dweights - delta)
            return weights.astype(jnp.bfloat16), dscores.astype(jnp.bfloat16)

        scores = dot(keys, q_all, NT)
        dweights = dot(values, do_all, NT)
        parts = []
        for j in range(SEQ_PAIRS):
            rows = slice(j * BLOCK, (j + 1) * BLOCK)
            parts.append(weigh(scores[rows], dweights[rows], lse + far[j]))
        weights = jnp.concatenate([w for w, _ in parts], axis=0)
        dscores = jnp.concatenate([d for _, d in parts], axis=0)
        dq_t = dot(keys_t, dscores)
        dk = dot(dscores, q_all)
        dv = dot(weights, do_all)
        for j, i in enumerate(index):
            rows = slice(j * BLOCK, (j + 1) * BLOCK)
            acc[i, 0] += dk[rows]
            acc[i, 1] += dv[rows]

        mem_scores = jnp.concatenate([dot(mk[:, col(h)], q_heads[h], NT) for h in heads], axis=1)
        mem_dweights = jnp.concatenate(
            [dot(mv[:, col(h)], do_heads[h], NT) for h in heads], axis=1
        )
        mem_w, mem_d = weigh(mem_scores, mem_dweights, lse)
        for h in heads:
            lanes = slice(h * HEAD_FEATURES, (h + 1) * HEAD_FEATURES)
            dmk[:, col(h)] += dot(mem_d[:, lanes], q_heads[h])
            dmv[:, col(h)] += dot(mem_w[:, lanes], do_heads[h])
            head_dq = dq_t[:, lanes] + dot(mkt[h], mem_d[:, lanes])
            dq[:, col(h)] = (head_dq * SCALE).T.astype(jnp.bfloat16)

    if looped:

        @pl.loop(0, len(ks))
        def _(i):
            one_block(ks[0] + i, qds[0].at[i], dqs[0].at[i])
    else:
        for k, qd, dq in zip(ks, qds, dqs):
            one_block(k, qd, dq)

    if last:
        local[...] = acc[:ways]
        for s, back in enumerate(backs):
            back[0] = (acc[ways + s, 0] * SCALE).astype(jnp.bfloat16)
            back[1] = acc[ways + s, 1].astype(jnp.bfloat16)
            if lay.mem_rows:
                rows = mem_part(lay, ctl, s)
                for h in heads:
                    at = pl.ds(h * lay.mem_rows, lay.mem_rows)
                    back[2, at] = (dmk[rows, col(h)] * SCALE).astype(jnp.bfloat16)
                    back[3, at] = dmv[rows, col(h)].astype(jnp.bfloat16)
        if lay.mem_rows:
            rows = mem_part(lay, ctl, 0)
            own_mem[0] = dmk[rows] * SCALE
            own_mem[1] = dmv[rows]
        else:
            own_mem[0] = dmk[...] * SCALE
            own_mem[1] = dmv[...]


def mem_part(lay, ctl, k):
    at = partner(ctl[1], k, lay.spans) * lay.mem_rows
    return pl.ds(pl.multiple_of(at, lay.mem_rows), lay.mem_rows)


def attention(lay, ks, ctl, qds, pool, slots, stats, mk, mv, before, last):
    blocks = lay.ways + lay.spans
    totals = [
        array((blocks, 2, BLOCK, HEAD_FEATURES), jnp.float32),
        array((BLOCK, lay.width), jnp.float32),
        array((BLOCK, lay.width), jnp.float32),
    ]
    scratch = [
        pltpu.VMEM((blocks, 3, BLOCK, HEAD_FEATURES), jnp.bfloat16),
        pltpu.VMEM((lay.heads, BLOCK, HEAD_FEATURES), jnp.bfloat16),
    ]
    pieces = [qds[k] for k in ks]
    outs = [array((BLOCK, lay.width))] * len(ks)
    looped = len(ks) > MAX_PERMUTES // 2
    if looped:
        pieces = [jnp.stack(pieces)]
        outs = [array((len(ks), BLOCK, lay.width))]
    if last:
        outs += [
            array((lay.ways, 2, BLOCK, HEAD_FEATURES), jnp.float32),
            array((2, lay.mem_rows or BLOCK, lay.width), jnp.float32),
        ]
        outs += [array((4 if lay.mem_rows else 2, BLOCK, HEAD_FEATURES))] * lay.spans
        scratch = [pltpu.VMEM(t.shape, t.dtype) for t in totals] + scratch
    else:
        outs += totals
    pairs = len(ks) * lay.heads * (SEQ_PAIRS + 1)
    done = call(
        functools.partial(attention_kernel, lay, ks, before is None, last),
        outs,
        ctl,
        *pieces,
        pool,
        *slots,
        stats,
        mk,
        mv,
        *(before or []),
        scratch=scratch,
        flops=pairs * 10 * BLOCK * BLOCK * HEAD_FEATURES,
        trans=pairs * BLOCK * BLOCK,
    )
    return [*done[0], *done[1:]] if looped else done


def merge_kernel(lay, ctl, *refs):
    local, own_mem = refs[:2]
    backs = refs[2 : 2 + lay.spans]
    pieces = refs[2 + lay.spans : 2 + lay.spans + lay.ways]
    mem_sum, total = refs[2 + lay.spans + lay.ways :]
    for k in range(lay.ways):
        total[k, 0] = local[k, 0] * SCALE
        total[k, 1] = local[k, 1]
    mem_sum[...] = own_mem[...]
    for s, back in enumerate(backs):
        if skipped(s, lay.spans):
            continue
        at = lay.send_index(ctl, s)
        for i in range(2):
            total[at, i] += back[i].astype(jnp.float32)
            for h in range(lay.heads if lay.mem_rows else 0):
                rows = pl.ds(h * lay.mem_rows, lay.mem_rows)
                mem_sum[i, :, col(h)] += back[2 + i, rows].astype(jnp.float32)
    for k, piece in enumerate(pieces):
        piece[...] = total[k].astype(jnp.bfloat16)


def join_kernel(lay, ctl, *refs):
    *pieces, out = refs
    for k, piece in enumerate(pieces):
        out[:, col(partner(ctl[0], k, lay.ways), lay.width)] = piece[...]


def finish_kernel(lay, ctl, *refs):
    pieces = refs[: lay.ways]
    parts = refs[lay.ways : -4]
    out_k, out_v, out_mk, out_mv = refs[-4:]
    shared = lay.heads < GROUP
    if shared:
        out_k[...] = jnp.zeros_like(out_k)
        out_v[...] = jnp.zeros_like(out_v)
    for k, piece in enumerate(pieces):
        at = col(lay.key_head(partner(ctl[0], k, lay.ways)))
        for i, out in enumerate((out_k, out_v)):
            term = piece[i].astype(jnp.float32)
            out[:, at] = out[:, at] + term if shared else term
    for s, part in enumerate(parts):
        rows = mem_part(lay, ctl, s) if lay.mem_rows else slice(None)
        out_mk[rows, :] = part[0]
        out_mv[rows, :] = part[1]


def shards(
    queries, keys, values, grad_out, row_lse, row_delta, pattern, memory_keys, memory_values
):
    lay = Layout(lax.axis_size("uly"), lax.axis_size("blk"))
    place = jnp.stack([lax.axis_index("uly"), lax.axis_index("blk")]).astype(jnp.int32)
    ctl = jnp.concatenate([place, pattern.reshape(-1)])

    kv = exchange(cut(lay, lay.key_head, ctl, keys, values, HEAD_FEATURES), "uly")
    qd = exchange(cut(lay, lambda device: device, ctl, queries, grad_out, lay.width), "uly")
    stats = jnp.concatenate([row_lse, row_delta], axis=1)
    stats = stats.reshape(lay.ways, BLOCK, 2 * lay.heads).transpose(0, 2, 1)

    pool, *slots = call(
        functools.partial(pool_kernel, lay),
        [array((lay.ways, 3, BLOCK, HEAD_FEATURES))]
        + [array((2, BLOCK, HEAD_FEATURES))] * lay.spans,
        ctl,
        *kv,
    )
    slots = exchange(slots, "blk")

    half = max(1, lay.ways // 4)
    steps = [range(0, 2 * half), range(2 * half, 3 * half), range(3 * half, lay.ways)]
    totals, dq = None, []
    for step in steps:
        last = step is steps[-1]
        ks = list(step)
        done = attention(
            lay, ks, ctl, qd, pool, slots, stats, memory_keys, memory_values, totals, last
        )
        dq += done[: len(ks)]
        totals = done[len(ks) :]
    local, own_mem, *backs = totals
    backs = exchange(backs, "blk")
    dq = exchange(dq, "uly")
    *dkv, mem = call(
        functools.partial(merge_kernel, lay),
        [array((2, BLOCK, HEAD_FEATURES))] * lay.ways + [array(own_mem.shape, jnp.float32)],
        ctl,
        local,
        own_mem,
        *backs,
        scratch=[pltpu.VMEM((lay.ways, 2, BLOCK, HEAD_FEATURES), jnp.float32)],
    )
    dkv = exchange(dkv, "uly")
    mem = exchange([mem] * lay.spans, "blk") if lay.mem_rows else [lax.psum(mem, "blk")]
    (grad_q,) = call(
        functools.partial(join_kernel, lay),
        [array(queries.shape)],
        ctl,
        *dq,
    )
    grad_k, grad_v, grad_mk, grad_mv = call(
        functools.partial(finish_kernel, lay),
        [array(keys.shape, jnp.float32)] * 2 + [array(memory_keys.shape, jnp.float32)] * 2,
        ctl,
        *dkv,
        *mem,
    )
    return grad_q, grad_k, grad_v, grad_mk, grad_mv


def solution(mesh):
    in_specs = (
        P(("blk", "uly"), None),
        P(("blk", "uly"), None),
        P(("blk", "uly"), None),
        P(("blk", "uly"), None),
        P("blk", "uly"),
        P("blk", "uly"),
        P(),
        P(None, "uly"),
        P(None, "uly"),
    )
    out_specs = (
        P(("blk", "uly"), None),
        P(("blk", "uly"), None),
        P(("blk", "uly"), None),
        P(None, "uly"),
        P(None, "uly"),
    )
    return jax.shard_map(shards, mesh=mesh, in_specs=in_specs, out_specs=out_specs, check_vma=False)
```

time: 421 us -> 126 us (0.30)
  waiting for transfers between devices: 187 us -> 39.2 us
  local copies, waits for them, and re-layouts: 86.3 us -> 5.23 us
  other arithmetic: 60.3 us -> 0.09 us
  matrix products: 22 us -> 0 us
  Pallas kernels: 0 us -> 19.9 us
  between operations: 14.3 us -> 0.79 us
  starting transfers between devices: 47.4 us -> 60.3 us
    all_to_all x11 -> x0, waiting for transfers between devices: 165 us -> none  [the longest x1 26.4 us: shards(): lax.all_to_all(widen_heads(values), 'uly', split_axis=1, concat_axis=0, t...]
    ppermute x0 -> x37, starting transfers between devices: none -> 60.3 us  [exchange(): lax.ppermute(pieces[k], axis, [(i, i ^ k) for i in range(n)])]
    all_to_all x11 -> x0, starting transfers between devices: 47.4 us -> none  [the longest x1 6.33 us: shards(): lax.all_to_all(widen_heads(values), 'uly', split_axis=1, concat_axis=0, t...]
    scatter-add x6 -> x0, other arithmetic: 43.6 us -> none  [the longest x2 18.3 us: one_step(): key_acc = key_acc.at[:, index_part].add(key_term.astype(jnp.float32))]
    ppermute x0 -> x37, waiting for transfers between devices: none -> 39.2 us  [exchange(): lax.ppermute(pieces[k], axis, [(i, i ^ k) for i in range(n)])]
    dot_general x10 -> x0, matrix products: 22 us -> none  [the longest x2 8.36 us: one_step(): jnp.einsum('hnsak,hnad->hnskd', dscore_bf, query_part, preferred_element_...]
    psum x1 -> x0, waiting for transfers between devices: 21.2 us -> none  [shards(): lax.psum((memory_rows(memory_dk), memory_rows(memory_dv)), 'blk')]
    pallas_call x0 -> x9, Pallas kernels: none -> 19.9 us  [call(): pl.pallas_call(kernel, in_specs=[SMEM_SPEC] + [VMEM_SPEC] * len(operands)...]
  transfers between devices with their start and end apart: 12 -> 37, of which waited for: 12 -> 8; matrix products, arithmetic and copies ran while one was open for 13% -> 0% of each run, Pallas kernels for 0% -> 14%
where the time goes in v2:
time: 126 us; the launch traced here: 125 us
  starting transfers between devices  60.3 us (48%)
  waiting for transfers between devices  39.2 us (31%)
  Pallas kernels  19.9 us (16%)
  local copies, waits for them, and re-layouts  5.23 us (4%)
    ppermute x37, starting transfers between devices, exchange(): lax.ppermute(pieces[k], axis, [(i, i ^ k) for i in range(n)])  60.3 us
    ppermute x37, waiting for transfers between devices, exchange(): lax.ppermute(pieces[k], axis, [(i, i ^ k) for i in range(n)])  39.2 us
    pallas_call x9, Pallas kernels, call(): pl.pallas_call(kernel, in_specs=[SMEM_SPEC] + [VMEM_SPEC] * len(operands)...  19.9 us
    unnamed x17, local copies, waits for them, and re-layouts  5.13 us
  transfers between devices with their start and end apart: 37, of which 8 were waited for; matrix products, arithmetic and copies ran while one was open for 0% of the time, Pallas kernels for 14%

profile of v2, /device:TPU:0, one launch (start us, length us, event | category | flops | bytes accessed | tf_op | source)
XLA Modules:
  0.0 125.5 jit_solution(10352538284616075804)
XLA Ops:
  4.7 2.6 %collective-permute-start.4 = (bf16[2,128,128]{2,1,0:T(8,128)(2,1)S(1)}, bf16[2,128,128]{2,1,0:T(8,128)(2,1)S(1)}, u32[]{:S(2)}, u32[]{:S(2)}) collective-permute-start(bf16[2,128,128]{2,1,0:T(8,128)(2,1)S(1)} %get-tuple-element.65), channel_id=1, source_target_pairs={{0,2},{1,3},{2,0},{3,1},{4,6},{5,7},{6,4},{7,5},{8,10},{9,11},{10,... | collective-permute-start | bytes 196616 | tf_op jit(solution)/shard_map/ppermute | solution.py:55
  7.4 2.8 %collective-permute-start.6 = (bf16[2,128,128]{2,1,0:T(8,128)(2,1)S(1)}, bf16[2,128,128]{2,1,0:T(8,128)(2,1)S(1)}, u32[]{:S(2)}, u32[]{:S(2)}) collective-permute-start(bf16[2,128,128]{2,1,0:T(8,128)(2,1)S(1)} %get-tuple-element.67), channel_id=1, source_target_pairs={{0,4},{1,5},{2,6},{3,7},{4,0},{5,1},{6,2},{7,3},{8,12},{9,13},{10,... | collective-permute-start | bytes 196616 | tf_op jit(solution)/shard_map/ppermute | solution.py:55
  10.2 3.6 %collective-permute-start.8 = (bf16[2,128,128]{2,1,0:T(8,128)(2,1)S(1)}, bf16[2,128,128]{2,1,0:T(8,128)(2,1)S(1)}, u32[]{:S(2)}, u32[]{:S(2)}) collective-permute-start(bf16[2,128,128]{2,1,0:T(8,128)(2,1)S(1)} %get-tuple-element.69), channel_id=1, source_target_pairs={{0,6},{1,7},{2,4},{3,5},{4,2},{5,3},{6,0},{7,1},{8,14},{9,15},{10,... | collective-permute-start | bytes 196616 | tf_op jit(solution)/shard_map/ppermute | solution.py:55
  17.6 1.6 %collective-permute-start.1 = (bf16[2,128,512]{2,1,0:T(8,128)(2,1)S(1)}, bf16[2,128,512]{2,1,0:T(8,128)(2,1)S(1)}, u32[]{:S(2)}, u32[]{:S(2)}) collective-permute-start(bf16[2,128,512]{2,1,0:T(8,128)(2,1)S(1)} %get-tuple-element.61), channel_id=1, source_target_pairs={{0,2},{1,3},{2,0},{3,1},{4,6},{5,7},{6,4},{7,5},{8,10},{9,11},{10,... | collective-permute-start | bytes 786440 | tf_op jit(solution)/shard_map/ppermute | solution.py:55
  26.3 2.4 %collective-permute-start.12 = (bf16[2,128,128]{2,1,0:T(8,128)(2,1)S(1)}, bf16[2,128,128]{2,1,0:T(8,128)(2,1)S(1)}, u32[]{:S(2)}, u32[]{:S(2)}) collective-permute-start(bf16[2,128,128]{2,1,0:T(8,128)(2,1)S(1)} %get-tuple-element.75), channel_id=1, source_target_pairs={{0,24},{8,16},{16,8},{24,0},{1,25},{9,17},{17,9},{25,1},{2,26},{10... | collective-permute-start | bytes 196616 | tf_op jit(solution)/shard_map/ppermute | solution.py:55
  28.7 4.5 %collective-permute-start.16 = (bf16[2,128,512]{2,1,0:T(8,128)(2,1)S(1)}, bf16[2,128,512]{2,1,0:T(8,128)(2,1)S(1)}, u32[]{:S(2)}, u32[]{:S(2)}) collective-permute-start(bf16[2,128,512]{2,1,0:T(8,128)(2,1)S(1)} %get-tuple-element.80), channel_id=1, source_target_pairs={{0,4},{1,5},{2,6},{3,7},{4,0},{5,1},{6,2},{7,3},{8,12},{9,13},{10,... | collective-permute-start | bytes 786440 | tf_op jit(solution)/shard_map/ppermute | solution.py:55
  35.0 4.3 %collective-permute-start.21 = (bf16[2,128,512]{2,1,0:T(8,128)(2,1)S(1)}, bf16[2,128,512]{2,1,0:T(8,128)(2,1)S(1)}, u32[]{:S(2)}, u32[]{:S(2)}) collective-permute-start(bf16[2,128,512]{2,1,0:T(8,128)(2,1)S(1)} %get-tuple-element.88), channel_id=1, source_target_pairs={{0,7},{1,6},{2,5},{3,4},{4,3},{5,2},{6,1},{7,0},{8,15},{9,14},{10,... | collective-permute-start | bytes 786440 | tf_op jit(solution)/shard_map/ppermute | solution.py:55
  39.3 5.8 %shard_map.131 = (bf16[128,512]{1,0:T(8,128)(2,1)S(1)}, bf16[128,512]{1,0:T(8,128)(2,1)S(1)}, bf16[128,512]{1,0:T(8,128)(2,1)S(1)}, bf16[128,512]{1,0:T(8,128)(2...) custom-call(s32[66]{0:T(128)S(1)} %pad_add_fusion.ctl, ...), custom_call_target="tpu_custom_call" | custom-call | flops 2013265920 | bytes 5013504 | tf_op jit(solution)/shard_map/pallas_call | solution.py:64
  45.2 17.2 %collective-permute-done.16.refs_0_ = bf16[2,128,512]{2,1,0:T(8,128)(2,1)S(1)} collective-permute-done((bf16[2,128,512]{2,1,0:T(8,128)(2,1)S(1)}, bf16[2,128,512]{2,1,0:T(8,128)(2,1)S(1)}, u32[]{:S(2)}, u32[]{:S(2)}) %collective-permute-start.16) | collective-permute-done | bytes 262176 | tf_op jit(solution)/shard_map/ppermute | solution.py:55
  62.4 3.5 %collective-permute-done.17.refs_1_ = bf16[2,128,512]{2,1,0:T(8,128)(2,1)S(1)} collective-permute-done((bf16[2,128,512]{2,1,0:T(8,128)(2,1)S(1)}, bf16[2,128,512]{2,1,0:T(8,128)(2,1)S(1)}, u32[]{:S(2)}, u32[]{:S(2)}) %collective-permute-start.17) | collective-permute-done | bytes 262176 | tf_op jit(solution)/shard_map/ppermute | solution.py:55
  65.9 3.3 %shard_map.132 = (bf16[128,512]{1,0:T(8,128)(2,1)S(1)}, bf16[128,512]{1,0:T(8,128)(2,1)S(1)}, f32[12,2,128,128]{3,2,1,0:T(8,128)S(1)}, f32[128,512]{1,0:T(8,128)S(1)}, f32[128,512]{1,0:T(8,128)S(1)}) custom-call(s32[66]{0:T(128)S(1)} %pad_add_fusion.ctl, bf16[2,128,512]{2,1,0:T(8,128)(2,1)S(1)} %collective-permute-done.16.refs_0_, ...), custom_call_target="tpu_custom_call" | custom-call | flops 1006632960 | bytes 6324224 | tf_op jit(solution)/shard_map/pallas_call | solution.py:64
  69.2 3.5 %shard_map.133 = (bf16[128,512]{1,0:T(8,128)(2,1)S(1)}, bf16[128,512]{1,0:T(8,128)(2,1)S(1)}, f32[8,2,128,128]{3,2,1,0:T(8,128)S(1)}, f32[2,32,512]{2,1,0:T(8,12...) custom-call(s32[66]{0:T(128)S(1)} %pad_add_fusion.ctl, ...), custom_call_target="tpu_custom_call" | custom-call | flops 1006632960 | bytes 5931008 | tf_op jit(solution)/shard_map/pallas_call | solution.py:64
  73.4 2.8 %collective-permute-start.26 = (bf16[4,128,128]{2,1,0:T(8,128)(2,1)S(1)}, bf16[4,128,128]{2,1,0:T(8,128)(2,1)S(1)}, u32[]{:S(2)}, u32[]{:S(2)}) collective-permute-start(bf16[4,128,128]{2,1,0:T(8,128)(2,1)S(1)} %get-tuple-element.99), channel_id=1, source_target_pairs={{0,24},{8,16},{16,8},{24,0},{1,25},{9,17},{17,9},{25,1},{2,26},{10... | collective-permute-start | bytes 393224 | tf_op jit(solution)/shard_map/ppermute | solution.py:55
  76.3 8.1 %collective-permute-start.15 = (bf16[128,512]{1,0:T(8,128)(2,1)S(1)}, bf16[128,512]{1,0:T(8,128)(2,1)S(1)}, u32[]{:S(2)}, u32[]{:S(2)}) collective-permute-start(bf16[128,512]{1,0:T(8,128)(2,1)S(1)} %get-tuple-element.79), channel_id=1, source_target_pairs={{0,3},{1,2},{2,1},{3,0},{4,7},{5,6},{6,5},{7,4},{8,11},{9,10},{10,... | collective-permute-start | bytes 393224 | tf_op jit(solution)/shard_map/ppermute | solution.py:55
  85.3 2.5 %collective-permute-start.19 = (bf16[128,512]{1,0:T(8,128)(2,1)S(1)}, bf16[128,512]{1,0:T(8,128)(2,1)S(1)}, u32[]{:S(2)}, u32[]{:S(2)}) collective-permute-start(bf16[128,512]{1,0:T(8,128)(2,1)S(1)} %get-tuple-element.86), channel_id=1, source_target_pairs={{0,5},{1,4},{2,7},{3,6},{4,1},{5,0},{6,3},{7,2},{8,13},{9,12},{10,... | collective-permute-start | bytes 393224 | tf_op jit(solution)/shard_map/ppermute | solution.py:55
  87.9 1.7 %collective-permute-start.22 = (bf16[128,512]{1,0:T(8,128)(2,1)S(1)}, bf16[128,512]{1,0:T(8,128)(2,1)S(1)}, u32[]{:S(2)}, u32[]{:S(2)}) collective-permute-start(bf16[128,512]{1,0:T(8,128)(2,1)S(1)} %get-tuple-element.92), channel_id=1, source_target_pairs={{0,6},{1,7},{2,4},{3,5},{4,2},{5,3},{6,0},{7,1},{8,14},{9,15},{10,... | collective-permute-start | bytes 393224 | tf_op jit(solution)/shard_map/ppermute | solution.py:55
  89.6 1.8 %collective-permute-start.23 = (bf16[128,512]{1,0:T(8,128)(2,1)S(1)}, bf16[128,512]{1,0:T(8,128)(2,1)S(1)}, u32[]{:S(2)}, u32[]{:S(2)}) collective-permute-start(bf16[128,512]{1,0:T(8,128)(2,1)S(1)} %get-tuple-element.93), channel_id=1, source_target_pairs={{0,7},{1,6},{2,5},{3,4},{4,3},{5,2},{6,1},{7,0},{8,15},{9,14},{10,... | collective-permute-start | bytes 393224 | tf_op jit(solution)/shard_map/ppermute | solution.py:55
  93.2 9.6 %collective-permute-done.18.refs_4_ = bf16[128,512]{1,0:T(8,128)(2,1)S(1)} collective-permute-done((bf16[128,512]{1,0:T(8,128)(2,1)S(1)}, bf16[128,512]{1,0:T(8,128)(2,1)S(1)}, u32[]{:S(2)}, u32[]{:S(2)}) %collective-permute-start.18) | collective-permute-done | bytes 131104 | tf_op jit(solution)/shard_map/ppermute | solution.py:55
  102.8 1.9 %collective-permute-done.19.refs_5_ = bf16[128,512]{1,0:T(8,128)(2,1)S(1)} collective-permute-done((bf16[128,512]{1,0:T(8,128)(2,1)S(1)}, bf16[128,512]{1,0:T(8,128)(2,1)S(1)}, u32[]{:S(2)}, u32[]{:S(2)}) %collective-permute-start.19) | collective-permute-done | bytes 131104 | tf_op jit(solution)/shard_map/ppermute | solution.py:55
  104.7 5.0 %collective-permute-start.30 = (bf16[2,128,128]{2,1,0:T(8,128)(2,1)S(1)}, bf16[2,128,128]{2,1,0:T(8,128)(2,1)S(1)}, u32[]{:S(2)}, u32[]{:S(2)}) collective-permute-start(bf16[2,128,128]{2,1,0:T(8,128)(2,1)S(1)} %get-tuple-element.104), channel_id=1, source_target_pairs={{0,4},{1,5},{2,6},{3,7},{4,0},{5,1},{6,2},{7,3},{8,12},{9,13},{10,... | collective-permute-start | bytes 196616 | tf_op jit(solution)/shard_map/ppermute | solution.py:55
  109.7 2.9 %collective-permute-start.31 = (bf16[2,128,128]{2,1,0:T(8,128)(2,1)S(1)}, bf16[2,128,128]{2,1,0:T(8,128)(2,1)S(1)}, u32[]{:S(2)}, u32[]{:S(2)}) collective-permute-start(bf16[2,128,128]{2,1,0:T(8,128)(2,1)S(1)} %get-tuple-element.105), channel_id=1, source_target_pairs={{0,5},{1,4},{2,7},{3,6},{4,1},{5,0},{6,3},{7,2},{8,13},{9,12},{10,... | collective-permute-start | bytes 196616 | tf_op jit(solution)/shard_map/ppermute | solution.py:55
  116.1 1.7 %collective-permute-start.32 = (bf16[2,128,128]{2,1,0:T(8,128)(2,1)S(1)}, bf16[2,128,128]{2,1,0:T(8,128)(2,1)S(1)}, u32[]{:S(2)}, u32[]{:S(2)}) collective-permute-start(bf16[2,128,128]{2,1,0:T(8,128)(2,1)S(1)} %get-tuple-element.106), channel_id=1, source_target_pairs={{0,6},{1,7},{2,4},{3,5},{4,2},{5,3},{6,0},{7,1},{8,14},{9,15},{10,... | collective-permute-start | bytes 196616 | tf_op jit(solution)/shard_map/ppermute | solution.py:55
  119.4 2.8 %collective-permute-done.32.refs_6_ = bf16[2,128,128]{2,1,0:T(8,128)(2,1)S(1)} collective-permute-done((bf16[2,128,128]{2,1,0:T(8,128)(2,1)S(1)}, bf16[2,128,128]{2,1,0:T(8,128)(2,1)S(1)}, u32[]{:S(2)}, u32[]{:S(2)}) %collective-permute-start.32) | collective-permute-done | bytes 65568 | tf_op jit(solution)/shard_map/ppermute | solution.py:55
  123.6 1.8 %shard_map.136 = (f32[128,1024]{1,0:T(8,128)}, f32[128,1024]{1,0:T(8,128)}, f32[128,512]{1,0:T(8,128)}, f32[128,512]{1,0:T(8,128)}) custom-call(s32[66]{0:T(128)S(1)} %pad_add_fusion.ctl, bf16[2,128,128]{2,1,0:T(8,128)(2,1)S(1)} %get-tuple-element.100.refs_0_, bf16[2,128,128]{2,1,0:T(8,128)(2,1)S(1)} %collective-permute-done.27.refs_1_, ...), custom_call_target="tpu_custom_call" | custom-call | bytes 2621440 | tf_op jit(solution)/shard_map/pallas_call | solution.py:64
  (79 shorter events, 26.9 us)
Async XLA Ops:
  10.2 10.5 %collective-permute-start.7 = (bf16[2,128,128]{2,1,0:T(8,128)(2,1)S(1)}, bf16[2,128,128]{2,1,0:T(8,128)(2,1)S(1)}, u32[]{:S(2)}, u32[]{:S(2)}) collective-permute-start(bf16[2,128,128]{2,1,0:T(8,128)(2,1)S(1)} %get-tuple-element.68), channel_id=1, source_target_pairs={{0,5},{1,4},{2,7},{3,6},{4,1},{5,0},{6,3},{7,2},{8,13},{9,12},{10,... | collective-permute-start | bytes 196616 | tf_op jit(solution)/shard_map/ppermute | solution.py:55
  10.2 10.5 %collective-permute-start.8 = (bf16[2,128,128]{2,1,0:T(8,128)(2,1)S(1)}, bf16[2,128,128]{2,1,0:T(8,128)(2,1)S(1)}, u32[]{:S(2)}, u32[]{:S(2)}) collective-permute-start(bf16[2,128,128]{2,1,0:T(8,128)(2,1)S(1)} %get-tuple-element.69), channel_id=1, source_target_pairs={{0,6},{1,7},{2,4},{3,5},{4,2},{5,3},{6,0},{7,1},{8,14},{9,15},{10,... | collective-permute-start | bytes 196616 | tf_op jit(solution)/shard_map/ppermute | solution.py:55
  17.1 16.7 %collective-permute-start = (bf16[2,128,512]{2,1,0:T(8,128)(2,1)S(1)}, bf16[2,128,512]{2,1,0:T(8,128)(2,1)S(1)}, u32[]{:S(2)}, u32[]{:S(2)}) collective-permute-start(bf16[2,128,512]{2,1,0:T(8,128)(2,1)S(1)} %get-tuple-element.60), channel_id=1, source_target_pairs={{0,1},{1,0},{2,3},{3,2},{4,5},{5,4},{6,7},{7,6},{8,9},{9,8},{10,11... | collective-permute-start | bytes 786440 | tf_op jit(solution)/shard_map/ppermute | solution.py:55
  17.6 17.4 %collective-permute-start.1 = (bf16[2,128,512]{2,1,0:T(8,128)(2,1)S(1)}, bf16[2,128,512]{2,1,0:T(8,128)(2,1)S(1)}, u32[]{:S(2)}, u32[]{:S(2)}) collective-permute-start(bf16[2,128,512]{2,1,0:T(8,128)(2,1)S(1)} %get-tuple-element.61), channel_id=1, source_target_pairs={{0,2},{1,3},{2,0},{3,1},{4,6},{5,7},{6,4},{7,5},{8,10},{9,11},{10,... | collective-permute-start | bytes 786440 | tf_op jit(solution)/shard_map/ppermute | solution.py:55
  20.7 18.6 %collective-permute-start.2 = (bf16[2,128,512]{2,1,0:T(8,128)(2,1)S(1)}, bf16[2,128,512]{2,1,0:T(8,128)(2,1)S(1)}, u32[]{:S(2)}, u32[]{:S(2)}) collective-permute-start(bf16[2,128,512]{2,1,0:T(8,128)(2,1)S(1)} %get-tuple-element.62), channel_id=1, source_target_pairs={{0,3},{1,2},{2,1},{3,0},{4,7},{5,6},{6,5},{7,4},{8,11},{9,10},{10,... | collective-permute-start | bytes 786440 | tf_op jit(solution)/shard_map/ppermute | solution.py:55
  28.7 33.7 %collective-permute-start.16 = (bf16[2,128,512]{2,1,0:T(8,128)(2,1)S(1)}, bf16[2,128,512]{2,1,0:T(8,128)(2,1)S(1)}, u32[]{:S(2)}, u32[]{:S(2)}) collective-permute-start(bf16[2,128,512]{2,1,0:T(8,128)(2,1)S(1)} %get-tuple-element.80), channel_id=1, source_target_pairs={{0,4},{1,5},{2,6},{3,7},{4,0},{5,1},{6,2},{7,3},{8,12},{9,13},{10,... | collective-permute-start | bytes 786440 | tf_op jit(solution)/shard_map/ppermute | solution.py:55
  33.2 32.6 %collective-permute-start.17 = (bf16[2,128,512]{2,1,0:T(8,128)(2,1)S(1)}, bf16[2,128,512]{2,1,0:T(8,128)(2,1)S(1)}, u32[]{:S(2)}, u32[]{:S(2)}) collective-permute-start(bf16[2,128,512]{2,1,0:T(8,128)(2,1)S(1)} %get-tuple-element.81), channel_id=1, source_target_pairs={{0,5},{1,4},{2,7},{3,6},{4,1},{5,0},{6,3},{7,2},{8,13},{9,12},{10,... | collective-permute-start | bytes 786440 | tf_op jit(solution)/shard_map/ppermute | solution.py:55
  33.8 35.4 %collective-permute-start.20 = (bf16[2,128,512]{2,1,0:T(8,128)(2,1)S(1)}, bf16[2,128,512]{2,1,0:T(8,128)(2,1)S(1)}, u32[]{:S(2)}, u32[]{:S(2)}) collective-permute-start(bf16[2,128,512]{2,1,0:T(8,128)(2,1)S(1)} %get-tuple-element.87), channel_id=1, source_target_pairs={{0,6},{1,7},{2,4},{3,5},{4,2},{5,3},{6,0},{7,1},{8,14},{9,15},{10,... | collective-permute-start | bytes 786440 | tf_op jit(solution)/shard_map/ppermute | solution.py:55
  35.0 34.1 %collective-permute-start.21 = (bf16[2,128,512]{2,1,0:T(8,128)(2,1)S(1)}, bf16[2,128,512]{2,1,0:T(8,128)(2,1)S(1)}, u32[]{:S(2)}, u32[]{:S(2)}) collective-permute-start(bf16[2,128,512]{2,1,0:T(8,128)(2,1)S(1)} %get-tuple-element.88), channel_id=1, source_target_pairs={{0,7},{1,6},{2,5},{3,4},{4,3},{5,2},{6,1},{7,0},{8,15},{9,14},{10,... | collective-permute-start | bytes 786440 | tf_op jit(solution)/shard_map/ppermute | solution.py:55
  45.1 31.1 %collective-permute-start.13 = (bf16[128,512]{1,0:T(8,128)(2,1)S(1)}, bf16[128,512]{1,0:T(8,128)(2,1)S(1)}, u32[]{:S(2)}, u32[]{:S(2)}) collective-permute-start(bf16[128,512]{1,0:T(8,128)(2,1)S(1)} %get-tuple-element.77), channel_id=1, source_target_pairs={{0,1},{1,0},{2,3},{3,2},{4,5},{5,4},{6,7},{7,6},{8,9},{9,8},{10,11... | collective-permute-start | bytes 393224 | tf_op jit(solution)/shard_map/ppermute | solution.py:55
  62.4 22.0 %collective-permute-start.14 = (bf16[128,512]{1,0:T(8,128)(2,1)S(1)}, bf16[128,512]{1,0:T(8,128)(2,1)S(1)}, u32[]{:S(2)}, u32[]{:S(2)}) collective-permute-start(bf16[128,512]{1,0:T(8,128)(2,1)S(1)} %get-tuple-element.78), channel_id=1, source_target_pairs={{0,2},{1,3},{2,0},{3,1},{4,6},{5,7},{6,4},{7,5},{8,10},{9,11},{10,... | collective-permute-start | bytes 393224 | tf_op jit(solution)/shard_map/ppermute | solution.py:55
  72.7 12.6 %collective-permute-start.24 = (bf16[4,128,128]{2,1,0:T(8,128)(2,1)S(1)}, bf16[4,128,128]{2,1,0:T(8,128)(2,1)S(1)}, u32[]{:S(2)}, u32[]{:S(2)}) collective-permute-start(bf16[4,128,128]{2,1,0:T(8,128)(2,1)S(1)} %get-tuple-element.97), channel_id=1, source_target_pairs={{0,8},{8,0},{16,24},{24,16},{1,9},{9,1},{17,25},{25,17},{2,10},{10... | collective-permute-start | bytes 393224 | tf_op jit(solution)/shard_map/ppermute | solution.py:55
  73.0 14.9 %collective-permute-start.25 = (bf16[4,128,128]{2,1,0:T(8,128)(2,1)S(1)}, bf16[4,128,128]{2,1,0:T(8,128)(2,1)S(1)}, u32[]{:S(2)}, u32[]{:S(2)}) collective-permute-start(bf16[4,128,128]{2,1,0:T(8,128)(2,1)S(1)} %get-tuple-element.98), channel_id=1, source_target_pairs={{0,16},{8,24},{16,0},{24,8},{1,17},{9,25},{17,1},{25,9},{2,18},{10... | collective-permute-start | bytes 393224 | tf_op jit(solution)/shard_map/ppermute | solution.py:55
  73.4 16.1 %collective-permute-start.26 = (bf16[4,128,128]{2,1,0:T(8,128)(2,1)S(1)}, bf16[4,128,128]{2,1,0:T(8,128)(2,1)S(1)}, u32[]{:S(2)}, u32[]{:S(2)}) collective-permute-start(bf16[4,128,128]{2,1,0:T(8,128)(2,1)S(1)} %get-tuple-element.99), channel_id=1, source_target_pairs={{0,24},{8,16},{16,8},{24,0},{1,25},{9,17},{17,9},{25,1},{2,26},{10... | collective-permute-start | bytes 393224 | tf_op jit(solution)/shard_map/ppermute | solution.py:55
  76.3 16.4 %collective-permute-start.15 = (bf16[128,512]{1,0:T(8,128)(2,1)S(1)}, bf16[128,512]{1,0:T(8,128)(2,1)S(1)}, u32[]{:S(2)}, u32[]{:S(2)}) collective-permute-start(bf16[128,512]{1,0:T(8,128)(2,1)S(1)} %get-tuple-element.79), channel_id=1, source_target_pairs={{0,3},{1,2},{2,1},{3,0},{4,7},{5,6},{6,5},{7,4},{8,11},{9,10},{10,... | collective-permute-start | bytes 393224 | tf_op jit(solution)/shard_map/ppermute | solution.py:55
  84.4 18.5 %collective-permute-start.18 = (bf16[128,512]{1,0:T(8,128)(2,1)S(1)}, bf16[128,512]{1,0:T(8,128)(2,1)S(1)}, u32[]{:S(2)}, u32[]{:S(2)}) collective-permute-start(bf16[128,512]{1,0:T(8,128)(2,1)S(1)} %get-tuple-element.85), channel_id=1, source_target_pairs={{0,4},{1,5},{2,6},{3,7},{4,0},{5,1},{6,2},{7,3},{8,12},{9,13},{10,... | collective-permute-start | bytes 393224 | tf_op jit(solution)/shard_map/ppermute | solution.py:55
  85.3 19.4 %collective-permute-start.19 = (bf16[128,512]{1,0:T(8,128)(2,1)S(1)}, bf16[128,512]{1,0:T(8,128)(2,1)S(1)}, u32[]{:S(2)}, u32[]{:S(2)}) collective-permute-start(bf16[128,512]{1,0:T(8,128)(2,1)S(1)} %get-tuple-element.86), channel_id=1, source_target_pairs={{0,5},{1,4},{2,7},{3,6},{4,1},{5,0},{6,3},{7,2},{8,13},{9,12},{10,... | collective-permute-start | bytes 393224 | tf_op jit(solution)/shard_map/ppermute | solution.py:55
  87.9 16.9 %collective-permute-start.22 = (bf16[128,512]{1,0:T(8,128)(2,1)S(1)}, bf16[128,512]{1,0:T(8,128)(2,1)S(1)}, u32[]{:S(2)}, u32[]{:S(2)}) collective-permute-start(bf16[128,512]{1,0:T(8,128)(2,1)S(1)} %get-tuple-element.92), channel_id=1, source_target_pairs={{0,6},{1,7},{2,4},{3,5},{4,2},{5,3},{6,0},{7,1},{8,14},{9,15},{10,... | collective-permute-start | bytes 393224 | tf_op jit(solution)/shard_map/ppermute | solution.py:55
  89.6 20.1 %collective-permute-start.23 = (bf16[128,512]{1,0:T(8,128)(2,1)S(1)}, bf16[128,512]{1,0:T(8,128)(2,1)S(1)}, u32[]{:S(2)}, u32[]{:S(2)}) collective-permute-start(bf16[128,512]{1,0:T(8,128)(2,1)S(1)} %get-tuple-element.93), channel_id=1, source_target_pairs={{0,7},{1,6},{2,5},{3,4},{4,3},{5,2},{6,1},{7,0},{8,15},{9,14},{10,... | collective-permute-start | bytes 393224 | tf_op jit(solution)/shard_map/ppermute | solution.py:55
  92.7 19.9 %collective-permute-start.27 = (bf16[2,128,128]{2,1,0:T(8,128)(2,1)S(1)}, bf16[2,128,128]{2,1,0:T(8,128)(2,1)S(1)}, u32[]{:S(2)}, u32[]{:S(2)}) collective-permute-start(bf16[2,128,128]{2,1,0:T(8,128)(2,1)S(1)} %get-tuple-element.101), channel_id=1, source_target_pairs={{0,1},{1,0},{2,3},{3,2},{4,5},{5,4},{6,7},{7,6},{8,9},{9,8},{10,11... | collective-permute-start | bytes 196616 | tf_op jit(solution)/shard_map/ppermute | solution.py:55
  102.8 10.3 %collective-permute-start.28 = (bf16[2,128,128]{2,1,0:T(8,128)(2,1)S(1)}, bf16[2,128,128]{2,1,0:T(8,128)(2,1)S(1)}, u32[]{:S(2)}, u32[]{:S(2)}) collective-permute-start(bf16[2,128,128]{2,1,0:T(8,128)(2,1)S(1)} %get-tuple-element.102), channel_id=1, source_target_pairs={{0,2},{1,3},{2,0},{3,1},{4,6},{5,7},{6,4},{7,5},{8,10},{9,11},{10,... | collective-permute-start | bytes 196616 | tf_op jit(solution)/shard_map/ppermute | solution.py:55
  104.7 11.4 %collective-permute-start.30 = (bf16[2,128,128]{2,1,0:T(8,128)(2,1)S(1)}, bf16[2,128,128]{2,1,0:T(8,128)(2,1)S(1)}, u32[]{:S(2)}, u32[]{:S(2)}) collective-permute-start(bf16[2,128,128]{2,1,0:T(8,128)(2,1)S(1)} %get-tuple-element.104), channel_id=1, source_target_pairs={{0,4},{1,5},{2,6},{3,7},{4,0},{5,1},{6,2},{7,3},{8,12},{9,13},{10,... | collective-permute-start | bytes 196616 | tf_op jit(solution)/shard_map/ppermute | solution.py:55
  112.6 11.0 %collective-permute-start.36 = (f32[2,32,512]{2,1,0:T(8,128)S(1)}, f32[2,32,512]{2,1,0:T(8,128)S(1)}, u32[]{:S(2)}, u32[]{:S(2)}) collective-permute-start(f32[2,32,512]{2,1,0:T(8,128)S(1)} %get-tuple-element.108.refs_8_), channel_id=1, source_target_pairs={{0,24},{8,16},{16,8},{24,0},{1,25},{9,17},{17,9},{25,1},{2,26},{10... | collective-permute-start | bytes 393224 | tf_op jit(solution)/shard_map/ppermute | solution.py:55
  113.1 10.5 %collective-permute-start.35 = (f32[2,32,512]{2,1,0:T(8,128)S(1)}, f32[2,32,512]{2,1,0:T(8,128)S(1)}, u32[]{:S(2)}, u32[]{:S(2)}) collective-permute-start(f32[2,32,512]{2,1,0:T(8,128)S(1)} %get-tuple-element.108.refs_8_), channel_id=1, source_target_pairs={{0,16},{8,24},{16,0},{24,8},{1,17},{9,25},{17,1},{25,9},{2,18},{10... | collective-permute-start | bytes 393224 | tf_op jit(solution)/shard_map/ppermute | solution.py:55
  (21 other events, 233.8 us)

commit v3 on v2

v3 whole, which is shorter than its diff:
```python
import functools
import math

import jax
import jax.numpy as jnp
from jax import lax
from jax.experimental import pallas as pl
from jax.experimental.pallas import tpu as pltpu
from jax.sharding import PartitionSpec as P

QUERY_HEADS = 32
KEY_HEADS = 8
HEAD_FEATURES = 128
BLOCK = 128
RANDOM = 2
SEQ_PAIRS = RANDOM + 3
GROUP = QUERY_HEADS // KEY_HEADS
SCALE = HEAD_FEATURES ** (-0.5)
LOG2E = math.log2(math.e)
FAR = 1e30
MAX_PERMUTES = 8
VMEM_LIMIT = 24 * 1024 * 1024
WIDE_LIMIT = 60 * 1024 * 1024
NN = (((1,), (0,)), ((), ()))
NT = (((1,), (1,)), ((), ()))
SMEM_SPEC = pl.BlockSpec(memory_space=pltpu.SMEM)


def dot(left, right, dims=NN):
    return lax.dot_general(left, right, dims, preferred_element_type=jnp.float32)


def col(at, width=HEAD_FEATURES):
    if isinstance(at, int):
        return pl.ds(at * width, width)
    return pl.ds(pl.multiple_of(at * width, width), width)


def even(n):
    return n & (n - 1) == 0


def partner(me, k, n):
    return me ^ k if even(n) else lax.rem(k - me + n, n)


def staged(n):
    return even(n) and n <= MAX_PERMUTES


def swap(piece, k):
    return lax.ppermute(piece, "uly", [(i, i ^ k) for i in range(lax.axis_size("uly"))])


def to_spans(stacked):
    return lax.all_to_all(stacked, "blk", 0, 0, tiled=True)


def after(early, late):
    early, late = lax.optimization_barrier((early, late))
    return early, late


def call(kernel, outs, ctl, *operands, scratch=(), limit=VMEM_LIMIT):
    outputs = pl.pallas_call(
        kernel,
        in_specs=[SMEM_SPEC] + [pl.BlockSpec(memory_space=pltpu.VMEM)] * len(operands),
        out_specs=[pl.BlockSpec(memory_space=pltpu.VMEM)] * len(outs),
        out_shape=[jax.ShapeDtypeStruct(x.shape, x.dtype) for x in outs],
        scratch_shapes=list(scratch),
        compiler_params=pltpu.CompilerParams(vmem_limit_bytes=limit),
        cost_estimate=pl.CostEstimate(flops=0, bytes_accessed=0, transcendentals=0),
    )(ctl, *operands)
    return list(outputs)


def array(shape, dtype=jnp.bfloat16):
    return jax.ShapeDtypeStruct(shape, dtype)


class Layout:
    def __init__(self, ways, spans):
        self.ways = ways
        self.spans = spans
        self.heads = QUERY_HEADS // ways
        self.width = self.heads * HEAD_FEATURES
        self.mem_rows = BLOCK // spans if BLOCK % spans == 0 else 0

    def key_head(self, device):
        return lax.div(device * self.heads, GROUP)

    def pool_index(self, ctl, block):
        me, span = ctl[0], ctl[1]
        owner = lax.div(block, self.ways)
        local = lax.rem(block, self.ways)
        mine = partner(me, local, self.ways)
        return jnp.where(owner == span, mine, self.ways + owner)

    def pairs(self, ctl, k):
        me, span = ctl[0], ctl[1]
        block = span * self.ways + partner(me, k, self.ways)
        last = self.ways * self.spans - 1
        index = [
            self.pool_index(ctl, jnp.maximum(block - 1, 0)),
            self.pool_index(ctl, block),
            self.pool_index(ctl, jnp.minimum(block + 1, last)),
        ]
        index += [self.pool_index(ctl, ctl[2 + block * RANDOM + r]) for r in range(RANDOM)]
        far = [jnp.where(block == 0, FAR, 0.0), 0.0, jnp.where(block == last, FAR, 0.0)]
        return index, far + [0.0] * RANDOM

    def send_index(self, ctl, other):
        me, span = ctl[0], ctl[1]
        entries = self.ways * RANDOM

        def look(e, found):
            block = ctl[2 + other * entries + e]
            return jnp.where(lax.div(block, self.ways) == span, lax.rem(block, self.ways), found)

        named = lax.fori_loop(0, entries, look, jnp.int32(0))
        local = jnp.where(
            other == span + 1, self.ways - 1, jnp.where(other == span - 1, 0, named)
        )
        return partner(me, local, self.ways)


def cut_kernel(column, ks, ctl, first, second, out):
    for n, k in enumerate(ks):
        at = col(column(partner(ctl[0], k, lax.axis_size("uly"))), out.shape[3])
        out[n, 0] = first[:, at]
        out[n, 1] = second[:, at]


def cut(column, ks, ctl, first, second, width):
    out = array((len(ks), 2, BLOCK, width))
    return call(functools.partial(cut_kernel, column, ks), [out], ctl, first, second)[0]


def pack_kernel(column, ctl, first, second, got, *outs):
    for j, out in enumerate(outs):
        at = col(column(partner(ctl[0], 2 * j, lax.axis_size("uly"))), out.shape[3])
        out[0, 0] = first[:, at]
        out[0, 1] = second[:, at]
        out[1] = got[j]


def by_chip(column, ctl, first, second, width):
    ways = lax.axis_size("uly")
    chips = ways // 2
    if staged(ways):
        got = swap(cut(column, range(1, ways, 2), ctl, first, second, width), 1)
        return call(
            functools.partial(pack_kernel, column),
            [array((2, 2, BLOCK, width))] * chips,
            ctl,
            first,
            second,
            got,
        )
    order = partner(lax.axis_index("uly"), jnp.arange(ways, dtype=jnp.int32), ways)
    sent = cut(column, range(ways), ctl, first, second, width)[order]
    got = lax.all_to_all(sent, "uly", 0, 0, tiled=True)[order]
    return list(got.reshape(chips, 2, 2, BLOCK, width))


def pick_kernel(ctl, *refs):
    *pieces, out = refs
    for j, piece in enumerate(pieces):
        out[j] = piece[1]


def to_blocks(pieces):
    out = array((len(pieces), *pieces[0].shape[1:]), pieces[0].dtype)
    (other,) = call(pick_kernel, [out], jnp.zeros((1,), jnp.int32), *pieces)
    return swap(other, 1)


def pool_kernel(lay, ctl, *refs):
    *pieces, pool, slots = refs
    for j, piece in enumerate(pieces):
        for i in range(2):
            pool[2 * j + i, 0] = piece[i, 0]
            pool[2 * j + i, 1] = piece[i, 1]
            pool[2 * j + i, 2] = piece[i, 0].T
    for s in range(lay.spans):
        at = lay.send_index(ctl, s)
        slots[s, 0] = pool[at, 0]
        slots[s, 1] = pool[at, 1]


def attention_kernel(lay, js, first, last, ctl, *refs):
    refs = list(refs)
    take = lambda n: [refs.pop(0) for _ in range(n)]
    looped = len(js) > MAX_PERMUTES // 2
    qds = take(1 if looped else len(js))
    pool, slots, stats, mk, mv = take(5)
    if not first:
        prev = take(3)
    dqs = take(1 if looped else len(js))
    if last:
        local, own_mem, backs = take(3)
        acc, dmk, dmv, slot_pool, mkt = take(5)
    else:
        acc, dmk, dmv = take(3)
        slot_pool, mkt = take(2)
    heads = range(lay.heads)
    ways = lay.ways
    if first:
        for total in (acc, dmk, dmv):
            total[...] = jnp.zeros_like(total)
    else:
        for total, before in zip((acc, dmk, dmv), prev):
            total[...] = before[...]
    slot_pool[:ways] = pool[...]
    for s in range(lay.spans):
        slot_pool[ways + s, 0] = slots[s, 0]
        slot_pool[ways + s, 1] = slots[s, 1]
        slot_pool[ways + s, 2] = slots[s, 0].T
    for h in heads:
        mkt[h] = mk[:, col(h)].T

    def one_block(k, qd, dq):
        index, far = lay.pairs(ctl, k)
        stat = stats[partner(ctl[0], k, ways)]
        lse = jnp.concatenate([stat[h : h + 1] for h in heads], axis=1) * LOG2E
        delta = jnp.concatenate([stat[lay.heads + h : lay.heads + h + 1] for h in heads], axis=1)
        q_heads = [qd[0, :, col(h)] for h in heads]
        do_heads = [qd[1, :, col(h)] for h in heads]
        q_all = jnp.concatenate(q_heads, axis=0)
        do_all = jnp.concatenate(do_heads, axis=0)
        keys = jnp.concatenate([slot_pool[i, 0] for i in index], axis=0)
        values = jnp.concatenate([slot_pool[i, 1] for i in index], axis=0)
        keys_t = jnp.concatenate([slot_pool[i, 2] for i in index], axis=1)

        def weigh(scores, dweights, lse_row):
            weights = jnp.exp2(scores * (SCALE * LOG2E) - lse_row)
            dscores = weights * (dweights - delta)
            return weights.astype(jnp.bfloat16), dscores.astype(jnp.bfloat16)

        scores = dot(keys, q_all, NT)
        dweights = dot(values, do_all, NT)
        parts = []
        for j in range(SEQ_PAIRS):
            rows = slice(j * BLOCK, (j + 1) * BLOCK)
            parts.append(weigh(scores[rows], dweights[rows], lse + far[j]))
        weights = jnp.concatenate([w for w, _ in parts], axis=0)
        dscores = jnp.concatenate([d for _, d in parts], axis=0)
        dq_t = dot(keys_t, dscores)
        dk = dot(dscores, q_all)
        dv = dot(weights, do_all)
        for j, i in enumerate(index):
            rows = slice(j * BLOCK, (j + 1) * BLOCK)
            acc[i, 0] += dk[rows]
            acc[i, 1] += dv[rows]

        mem_scores = jnp.concatenate([dot(mk[:, col(h)], q_heads[h], NT) for h in heads], axis=1)
        mem_dweights = jnp.concatenate(
            [dot(mv[:, col(h)], do_heads[h], NT) for h in heads], axis=1
        )
        mem_w, mem_d = weigh(mem_scores, mem_dweights, lse)
        for h in heads:
            lanes = slice(h * HEAD_FEATURES, (h + 1) * HEAD_FEATURES)
            dmk[:, col(h)] += dot(mem_d[:, lanes], q_heads[h])
            dmv[:, col(h)] += dot(mem_w[:, lanes], do_heads[h])
            head_dq = dq_t[:, lanes] + dot(mkt[h], mem_d[:, lanes])
            dq[:, col(h)] = (head_dq * SCALE).T.astype(jnp.bfloat16)

    if looped:

        @pl.loop(0, len(js))
        def _(n):
            for i in range(2):
                one_block(2 * (js[0] + n) + i, qds[0].at[n, i], dqs[0].at[n, i])
    else:
        for j, qd, dq in zip(js, qds, dqs):
            for i in range(2):
                one_block(2 * j + i, qd.at[i], dq.at[i])

    if last:
        local[...] = acc[:ways]
        for s in range(lay.spans):
            backs[s, 0] = (acc[ways + s, 0] * SCALE).astype(jnp.bfloat16)
            backs[s, 1] = acc[ways + s, 1].astype(jnp.bfloat16)
            for h in heads if lay.mem_rows else ():
                rows = pl.ds(s * lay.mem_rows, lay.mem_rows)
                at = pl.ds(h * lay.mem_rows, lay.mem_rows)
                backs[s, 2, at] = (dmk[rows, col(h)] * SCALE).astype(jnp.bfloat16)
                backs[s, 3, at] = dmv[rows, col(h)].astype(jnp.bfloat16)
        rows = slice(None)
        if lay.mem_rows:
            rows = pl.ds(pl.multiple_of(ctl[1] * lay.mem_rows, lay.mem_rows), lay.mem_rows)
        own_mem[0] = dmk[rows, :] * SCALE
        own_mem[1] = dmv[rows, :]


def attention(lay, js, ctl, qds, pool, slots, stats, mk, mv, before, last):
    blocks = lay.ways + lay.spans
    totals = [
        array((blocks, 2, BLOCK, HEAD_FEATURES), jnp.float32),
        array((BLOCK, lay.width), jnp.float32),
        array((BLOCK, lay.width), jnp.float32),
    ]
    scratch = [
        pltpu.VMEM((blocks, 3, BLOCK, HEAD_FEATURES), jnp.bfloat16),
        pltpu.VMEM((lay.heads, BLOCK, HEAD_FEATURES), jnp.bfloat16),
    ]
    pieces = [qds[j] for j in js]
    outs = [array((2, BLOCK, lay.width))] * len(js)
    looped = len(js) > MAX_PERMUTES // 2
    if looped:
        pieces = [jnp.stack(pieces)]
        outs = [array((len(js), 2, BLOCK, lay.width))]
    if last:
        outs += [
            array((lay.ways, 2, BLOCK, HEAD_FEATURES), jnp.float32),
            array((2, lay.mem_rows or BLOCK, lay.width), jnp.float32),
            array((lay.spans, 4 if lay.mem_rows else 2, BLOCK, HEAD_FEATURES)),
        ]
        scratch = [pltpu.VMEM(t.shape, t.dtype) for t in totals] + scratch
    else:
        outs += totals
    done = call(
        functools.partial(attention_kernel, lay, js, before is None, last),
        outs,
        ctl,
        *pieces,
        pool,
        slots,
        stats,
        mk,
        mv,
        *(before or []),
        scratch=scratch,
    )
    dq = done[0] if looped else done[: len(js)]
    return dict(zip(js, dq)), done[1 if looped else len(js) :]


def merge_kernel(lay, ctl, local, own_mem, backs, *refs):
    *pieces, mem_sum, total = refs
    for k in range(lay.ways):
        total[k, 0] = local[k, 0] * SCALE
        total[k, 1] = local[k, 1]
    mem = [own_mem[0], own_mem[1]]
    for s in range(lay.spans):

        @pl.when(s != ctl[1])
        def _():
            at = lay.send_index(ctl, s)
            for i in range(2):
                total[at, i] += backs[s, i].astype(jnp.float32)

        if lay.mem_rows:
            for i in range(2):
                term = [
                    backs[s, 2 + i, pl.ds(h * lay.mem_rows, lay.mem_rows)]
                    for h in range(lay.heads)
                ]
                term = jnp.concatenate(term, axis=1).astype(jnp.float32)
                mem[i] += jnp.where(s == ctl[1], 0.0, term)
    for s in range(mem_sum.shape[0]):
        for i in range(2):
            mem_sum[s, i] = mem[i]
    for j, piece in enumerate(pieces):
        for i in range(2):
            piece[i] = total[2 * j + i].astype(jnp.bfloat16)


def by_partner(refs):
    *pieces, others = refs
    for j, piece in enumerate(pieces):
        yield 2 * j, piece.at[0]
        yield 2 * j + 1, others.at[j]


def join_kernel(lay, ctl, *refs):
    *pieces, out = refs
    for k, piece in by_partner(pieces):
        out[:, col(partner(ctl[0], k, lay.ways), lay.width)] = piece[...]


def finish_kernel(lay, ctl, mem, *refs):
    *pieces, out_k, out_v, out_mk, out_mv = refs
    shared = lay.heads < GROUP
    if shared:
        out_k[...] = jnp.zeros_like(out_k)
        out_v[...] = jnp.zeros_like(out_v)
    for k, piece in by_partner(pieces):
        at = col(lay.key_head(partner(ctl[0], k, lay.ways)))
        for i, out in enumerate((out_k, out_v)):
            term = piece[i].astype(jnp.float32)
            out[:, at] = out[:, at] + term if shared else term
    for s in range(mem.shape[0]):
        rows = pl.ds(s * mem.shape[2], mem.shape[2])
        out_mk[rows, :] = mem[s, 0]
        out_mv[rows, :] = mem[s, 1]


def whole_exchange(pieces):
    ways = 2 * len(pieces)
    order = partner(lax.axis_index("uly"), jnp.arange(ways, dtype=jnp.int32), ways)
    sent = jnp.concatenate(pieces)[order]
    got = lax.all_to_all(sent, "uly", 0, 0, tiled=True)[order]
    got = got.reshape(len(pieces), 2, *got.shape[1:])
    return [*got, got[:, 1]]


def shards(
    queries, keys, values, grad_out, row_lse, row_delta, pattern, memory_keys, memory_values
):
    lay = Layout(lax.axis_size("uly"), lax.axis_size("blk"))
    chips = lay.ways // 2
    in_stages = staged(lay.ways)
    place = jnp.stack([lax.axis_index("uly"), lax.axis_index("blk")]).astype(jnp.int32)
    ctl = jnp.concatenate([place, pattern.reshape(-1)])

    qd = by_chip(lambda device: device, place, queries, grad_out, lay.width)
    late = place
    kv = by_chip(lay.key_head, late, keys, values, HEAD_FEATURES)
    steps = [range(chips)]
    if in_stages:
        half = max(1, chips // 2)
        steps = [range(half), *([j] for j in range(half, chips))]
        qd[half] = swap(qd[half], 2 * half)
        for j in [*range(half, chips), *range(1, half)]:
            kv[j] = swap(kv[j], 2 * j)
        kv[1:], qd[half + 1] = after(kv[1:], qd[half + 1])
        kv[1], qd[1] = after(kv[1], qd[1])
        qd[half + 1] = swap(qd[half + 1], 2 * half + 2)
        qd[1] = swap(qd[1], 2)
    pool, slots = call(
        functools.partial(pool_kernel, lay),
        [
            array((lay.ways, 3, BLOCK, HEAD_FEATURES)),
            array((lay.spans, 2, BLOCK, HEAD_FEATURES)),
        ],
        ctl,
        *kv,
    )
    slots = to_spans(slots)
    stats = jnp.concatenate([row_lse, row_delta], axis=1)
    stats = stats.reshape(lay.ways, BLOCK, 2 * lay.heads).transpose(0, 2, 1)

    totals, dq = None, {}
    for step in steps:
        last = step is steps[-1]
        step_dq, totals = attention(
            lay, step, ctl, qd, pool, slots, stats, memory_keys, memory_values, totals, last
        )
        dq |= step_dq
    local, own_mem, backs = totals
    backs = to_spans(backs)
    if in_stages:
        for j in [*range(half, chips), *range(1, half)]:
            dq[j] = swap(dq[j], 2 * j)
        pass
    *dkv, mem = call(
        functools.partial(merge_kernel, lay),
        [array((2, 2, BLOCK, HEAD_FEATURES))] * chips
        + [array((lay.spans if lay.mem_rows else 1, *own_mem.shape), jnp.float32)],
        ctl,
        local,
        own_mem,
        backs,
        scratch=[pltpu.VMEM((lay.ways, 2, BLOCK, HEAD_FEATURES), jnp.float32)],
    )
    mem = to_spans(mem) if lay.mem_rows else lax.psum(mem, "blk")
    dq = [dq[j] for j in range(chips)]
    if in_stages:
        for j in [*range(half, chips), *range(1, half)]:
            dkv[j] = swap(dkv[j], 2 * j)
        (dkv[1:], mem), dq = after((dkv[1:], mem), dq)
        dq.append(to_blocks(dq))
        dkv.append(to_blocks(dkv))
    else:
        dq = whole_exchange(dq)
        dkv = whole_exchange(dkv)
    (grad_q,) = call(functools.partial(join_kernel, lay), [array(queries.shape)], place, *dq)
    grad_k, grad_v, grad_mk, grad_mv = call(
        functools.partial(finish_kernel, lay),
        [array(keys.shape, jnp.float32)] * 2 + [array(memory_keys.shape, jnp.float32)] * 2,
        place,
        mem,
        *dkv,
    )
    return grad_q, grad_k, grad_v, grad_mk, grad_mv


def solution(mesh):
    in_specs = (
        P(("blk", "uly"), None),
        P(("blk", "uly"), None),
        P(("blk", "uly"), None),
        P(("blk", "uly"), None),
        P("blk", "uly"),
        P("blk", "uly"),
        P(),
        P(None, "uly"),
        P(None, "uly"),
    )
    out_specs = (
        P(("blk", "uly"), None),
        P(("blk", "uly"), None),
        P(("blk", "uly"), None),
        P(None, "uly"),
        P(None, "uly"),
    )
    return jax.shard_map(shards, mesh=mesh, in_specs=in_specs, out_specs=out_specs, check_vma=False)
```

time: 126 us -> 121 us (0.960)
  starting transfers between devices: 60.3 us -> 37.9 us
  waiting for transfers between devices: 39.2 us -> 52.2 us
  Pallas kernels: 19.9 us -> 25 us
    ppermute x37 -> x16, starting transfers between devices: 60.3 us -> 27 us  [swap(): lax.ppermute(piece, 'uly', [(i, i ^ k) for i in range(lax.axis_size('uly'...]
    all_to_all x0 -> x3, starting transfers between devices: none -> 10.9 us  [to_spans(): return lax.all_to_all(stacked, 'blk', 0, 0, tiled=True)]
    all_to_all x0 -> x3, waiting for transfers between devices: none -> 10.8 us  [to_spans(): return lax.all_to_all(stacked, 'blk', 0, 0, tiled=True)]
    pallas_call x9 -> x13, Pallas kernels: 19.9 us -> 25 us  [call(): pl.pallas_call(kernel, in_specs=[SMEM_SPEC] + [pl.BlockSpec(memory_space=...]
    ppermute x37 -> x16, waiting for transfers between devices: 39.2 us -> 41.5 us  [swap(): lax.ppermute(piece, 'uly', [(i, i ^ k) for i in range(lax.axis_size('uly'...]
    unnamed x17 -> x33, local copies, waits for them, and re-layouts: 5.13 us -> 4.08 us
  transfers between devices with their start and end apart: 37 -> 19, of which waited for: 8 -> 10; matrix products, arithmetic and copies ran while one was open for 0% -> 0% of each run, Pallas kernels for 14% -> 16%
where the time goes in v3:
time: 121 us; the launch traced here: 120 us
  waiting for transfers between devices  52.2 us (43%)
  starting transfers between devices  37.9 us (31%)
  Pallas kernels  25 us (21%)
  local copies, waits for them, and re-layouts  4.18 us (3%)
    ppermute x16, waiting for transfers between devices, swap(): lax.ppermute(piece, 'uly', [(i, i ^ k) for i in range(lax.axis_size('uly'...  41.5 us
    ppermute x16, starting transfers between devices, swap(): lax.ppermute(piece, 'uly', [(i, i ^ k) for i in range(lax.axis_size('uly'...  27 us
    pallas_call x13, Pallas kernels, call(): pl.pallas_call(kernel, in_specs=[SMEM_SPEC] + [pl.BlockSpec(memory_space=...  25 us
    all_to_all x3, starting transfers between devices, to_spans(): return lax.all_to_all(stacked, 'blk', 0, 0, tiled=True)  10.9 us
    all_to_all x3, waiting for transfers between devices, to_spans(): return lax.all_to_all(stacked, 'blk', 0, 0, tiled=True)  10.8 us
    unnamed x33, local copies, waits for them, and re-layouts  4.08 us
  transfers between devices with their start and end apart: 19, of which 10 were waited for; matrix products, arithmetic and copies ran while one was open for 0% of the time, Pallas kernels for 16%

profile of v3, /device:TPU:0, one launch (start us, length us, event | category | flops | bytes accessed | tf_op | source)
XLA Modules:
  0.0 120.2 jit_solution(1129467596194783790)
XLA Ops:
  7.6 3.0 %collective-permute-start.1 = (bf16[2,2,128,128]{3,2,1,0:T(8,128)(2,1)S(1)}, bf16[2,2,128,128]{3,2,1,0:T(8,128)(2,1)S(1)}, u32[]{:S(2)}, u32[]{:S(2)}) collective-permute-start(bf16[2,2,128,128]{3,2,1,0:T(8,128)(2,1)S(1)} %get-tuple-element.51), channel_id=1, source_target_pairs={{0,2},{1,3},{2,0},{3,1},{4,6},{5,7},{6,4},{7,5},{8,10},{9,11},{10,... | collective-permute-start | bytes 393224 | tf_op jit(solution)/shard_map/ppermute | solution.py:52
  10.6 2.6 %collective-permute-start.2 = (bf16[2,2,128,128]{3,2,1,0:T(8,128)(2,1)S(1)}, bf16[2,2,128,128]{3,2,1,0:T(8,128)(2,1)S(1)}, u32[]{:S(2)}, u32[]{:S(2)}) collective-permute-start(bf16[2,2,128,128]{3,2,1,0:T(8,128)(2,1)S(1)} %get-tuple-element.52), channel_id=1, source_target_pairs={{0,4},{1,5},{2,6},{3,7},{4,0},{5,1},{6,2},{7,3},{8,12},{9,13},{10,... | collective-permute-start | bytes 393224 | tf_op jit(solution)/shard_map/ppermute | solution.py:52
  13.4 1.8 %shard_map.131 = (bf16[2,2,128,512]{3,2,1,0:T(8,128)(2,1)S(1)}, bf16[2,2,128,512]{3,2,1,0:T(8,128)(2,1)}, bf16[2,2,128,512]{3,2,1,0:T(8,128)(2,1)}, bf16[2,2,128,512]{3,2,1,0:T(8,128)(2,1)}) custom-call(s32[2]{0:T(128)S(1)} %pad_add_fusion.ctl, bf16[128,4096]{1,0:T(8,128)(2,1)S(1)} %copy-done.1, bf16[128,4096]{1,0:T(8,128)(2,1)S(1)} %copy-done.3, ...), custom_call_target="tpu_custom_call" | custom-call | tf_op jit(solution)/shard_map/pallas_call | solution.py:65
  16.3 7.2 %collective-permute-done.2.refs_2_ = bf16[2,2,128,128]{3,2,1,0:T(8,128)(2,1)S(1)} collective-permute-done((bf16[2,2,128,128]{3,2,1,0:T(8,128)(2,1)S(1)}, bf16[2,2,128,128]{3,2,1,0:T(8,128)(2,1)S(1)}, u32[]{:S(2)}, u32[]{:S(2)}) %collective-permute-start.2) | collective-permute-done | bytes 131104 | tf_op jit(solution)/shard_map/ppermute | solution.py:52
  23.5 2.3 %collective-permute-start.7 = (bf16[2,2,128,512]{3,2,1,0:T(8,128)(2,1)}, bf16[2,2,128,512]{3,2,1,0:T(8,128)(2,1)}, u32[]{:S(2)}, u32[]{:S(2)}) collective-permute-start(bf16[2,2,128,512]{3,2,1,0:T(8,128)(2,1)} %get-tuple-element.66), channel_id=1, source_target_pairs={{0,2},{1,3},{2,0},{3,1},{4,6},{5,7},{6,4},{7,5},{8,10},{9,11},{10,... | collective-permute-start | bytes 1572872 | tf_op jit(solution)/shard_map/ppermute | solution.py:52
  28.6 2.0 %shard_map.132 = (bf16[8,3,128,128]{3,2,1,0:T(8,128)(2,1)S(1)}, bf16[4,2,128,128]{3,2,1,0:T(8,128)(2,1)}) custom-call(s32[66]{0:T(128)S(1)} %pad_add_fusion.1.ctl, bf16[2,2,128,128]{3,2,1,0:T(8,128)(2,1)S(1)} %get-tuple-element.56.refs_0_, bf16[2,2,128,128]{3,2,1,0:T(8,128)(2,1)S(1)} %collective-permute-done.1.refs_1_, ...), custom_call_target="tpu_custom_call" | custom-call | tf_op jit(solution)/shard_map/pallas_call | solution.py:65
  30.6 3.7 %all-to-all-start = ((bf16[4,2,128,128]{3,2,1,0:T(8,128)(2,1)}), bf16[4,2,128,128]{3,2,1,0:T(8,128)(2,1)S(1)}, u32[]{:S(2)}, u32[]{:S(2)}) async-start(bf16[4,2,128,128]{3,2,1,0:T(8,128)(2,1)} %get-tuple-element.63), calls=%async_computation | async-start | bytes 524288 | tf_op jit(solution)/shard_map/all_to_all | solution.py:56
  34.3 5.4 %all-to-all-done.refs_3_.refs_2_ = bf16[4,2,128,128]{3,2,1,0:T(8,128)(2,1)S(1)} async-done(((bf16[4,2,128,128]{3,2,1,0:T(8,128)(2,1)}), bf16[4,2,128,128]{3,2,1,0:T(8,128)(2,1)S(1)}, u32[]{:S(2)}, u32[]{:S(2)}) %all-to-all-start) | async-done | bytes 262176 | tf_op jit(solution)/shard_map/all_to_all | solution.py:56
  39.7 7.6 %collective-permute-done.7.refs_1_ = bf16[2,2,128,512]{3,2,1,0:T(8,128)(2,1)} collective-permute-done((bf16[2,2,128,512]{3,2,1,0:T(8,128)(2,1)}, bf16[2,2,128,512]{3,2,1,0:T(8,128)(2,1)}, u32[]{:S(2)}, u32[]{:S(2)}) %collective-permute-start.7) | collective-permute-done | bytes 524320 | tf_op jit(solution)/shard_map/ppermute | solution.py:52
  47.3 6.3 %shard_map.133 = (bf16[2,128,512]{2,1,0:T(8,128)(2,1)S(1)}, bf16[2,128,512]{2,1,0:T(8,128)(2,1)S(1)}, f32[12,2,128,128]{3,2,1,0:T(8,128)S(1)}, f32[128,512]{1,0:T(8,128)S(1)}, f32[128,512]{1,0:T(8,128)S(1)}) custom-call(s32[66]{0:T(128)S(1)} %pad_add_fusion.1.ctl, bf16[2,2,128,512]{3,2,1,0:T(8,128)(2,1)S(1)} %get-tuple-element.65.refs_0_, ...), custom_call_target="tpu_custom_call" | custom-call | tf_op jit(solution)/shard_map/pallas_call | solution.py:65
  53.6 10.6 %collective-permute-done.6.refs_0_ = bf16[2,2,128,512]{3,2,1,0:T(8,128)(2,1)S(1)} collective-permute-done((bf16[2,2,128,512]{3,2,1,0:T(8,128)(2,1)}, bf16[2,2,128,512]{3,2,1,0:T(8,128)(2,1)S(1)}, u32[]{:S(2)}, u32[]{:S(2)}) %collective-permute-start.6) | collective-permute-done | bytes 524320 | tf_op jit(solution)/shard_map/ppermute | solution.py:52
  64.3 4.0 %shard_map.134 = (bf16[2,128,512]{2,1,0:T(8,128)(2,1)}, f32[12,2,128,128]{3,2,1,0:T(8,128)S(1)}, f32[128,512]{1,0:T(8,128)S(1)}, f32[128,512]{1,0:T(8,128)S(1)}) custom-call(s32[66]{0:T(128)S(1)} %pad_add_fusion.1.ctl, bf16[2,2,128,512]{3,2,1,0:T(8,128)(2,1)S(1)} %collective-permute-done.6.refs_0_, ...), custom_call_target="tpu_custom_call" | custom-call | tf_op jit(solution)/shard_map/pallas_call | solution.py:65
  68.3 3.4 %shard_map.135 = (bf16[2,128,512]{2,1,0:T(8,128)(2,1)S(1)}, f32[8,2,128,128]{3,2,1,0:T(8,128)S(1)}, f32[2,32,512]{2,1,0:T(8,128)S(1)}, bf16[4,4,128,128]{3,2,1,0:T(8,128)(2,1)S(1)}) custom-call(s32[66]{0:T(128)S(1)} %pad_add_fusion.1.ctl, bf16[2,2,128,512]{3,2,1,0:T(8,128)(2,1)S(1)} %collective-permute-done.5.refs_0_, ...), custom_call_target="tpu_custom_call" | custom-call | tf_op jit(solution)/shard_map/pallas_call | solution.py:65
  73.2 3.7 %all-to-all-start.1 = ((bf16[4,4,128,128]{3,2,1,0:T(8,128)(2,1)}), bf16[4,4,128,128]{3,2,1,0:T(8,128)(2,1)S(1)}, u32[]{:S(2)}, u32[]{:S(2)}) async-start(bf16[4,4,128,128]{3,2,1,0:T(8,128)(2,1)} %copy-done.8), calls=%async_computation.1 | async-start | bytes 1048576 | tf_op jit(solution)/shard_map/all_to_all | solution.py:56
  77.0 2.5 %collective-permute-start.13 = (bf16[2,128,512]{2,1,0:T(8,128)(2,1)}, bf16[2,128,512]{2,1,0:T(8,128)(2,1)S(1)}, u32[]{:S(2)}, u32[]{:S(2)}) collective-permute-start(bf16[2,128,512]{2,1,0:T(8,128)(2,1)} %copy-done.11), channel_id=1, source_target_pairs={{0,6},{1,7},{2,4},{3,5},{4,2},{5,3},{6,0},{7,1},{8,14},{9,15},{10,... | collective-permute-start | bytes 786440 | tf_op jit(solution)/shard_map/ppermute | solution.py:52
  79.4 5.4 %all-to-all-done.1.backs = bf16[4,4,128,128]{3,2,1,0:T(8,128)(2,1)S(1)} async-done(((bf16[4,4,128,128]{3,2,1,0:T(8,128)(2,1)}), bf16[4,4,128,128]{3,2,1,0:T(8,128)(2,1)S(1)}, u32[]{:S(2)}, u32[]{:S(2)}) %all-to-all-start.1) | async-done | bytes 524320 | tf_op jit(solution)/shard_map/all_to_all | solution.py:56
  84.8 2.1 %shard_map.136 = (bf16[2,2,128,128]{3,2,1,0:T(8,128)(2,1)S(1)}, bf16[2,2,128,128]{3,2,1,0:T(8,128)(2,1)S(1)}, bf16[2,2,128,128]{3,2,1,0:T(8,128)(2,1)S(1)}, bf16...) custom-call(s32[66]{0:T(128)S(1)} %pad_add_fusion.1.ctl, f32[8,2,128,128]{3,2,1,0:T(8,128)S(1)} %get-tuple-element.73.local, ...), custom_call_target="tpu_custom_call" | custom-call | tf_op jit(solution)/shard_map/pallas_call | solution.py:65
  86.9 3.5 %all-to-all-start.2 = ((f32[4,2,32,512]{3,2,1,0:T(8,128)}), f32[4,2,32,512]{3,2,1,0:T(8,128)S(1)}, u32[]{:S(2)}, u32[]{:S(2)}) async-start(f32[4,2,32,512]{3,2,1,0:T(8,128)} %get-tuple-element.79), calls=%async_computation.2 | async-start | bytes 1048576 | tf_op jit(solution)/shard_map/all_to_all | solution.py:56
  90.4 8.1 %collective-permute-start.12 = (bf16[2,128,512]{2,1,0:T(8,128)(2,1)}, bf16[2,128,512]{2,1,0:T(8,128)(2,1)S(1)}, u32[]{:S(2)}, u32[]{:S(2)}) collective-permute-start(bf16[2,128,512]{2,1,0:T(8,128)(2,1)} %get-tuple-element.82), channel_id=1, source_target_pairs={{0,4},{1,5},{2,6},{3,7},{4,0},{5,1},{6,2},{7,3},{8,12},{9,13},{10,... | collective-permute-start | bytes 786440 | tf_op jit(solution)/shard_map/ppermute | solution.py:52
  98.5 2.0 %collective-permute-start.8 = (bf16[2,2,128,128]{3,2,1,0:T(8,128)(2,1)}, bf16[2,2,128,128]{3,2,1,0:T(8,128)(2,1)S(1)}, u32[]{:S(2)}, u32[]{:S(2)}) collective-permute-start(bf16[2,2,128,128]{3,2,1,0:T(8,128)(2,1)} %copy-done.12), channel_id=1, source_target_pairs={{0,2},{1,3},{2,0},{3,1},{4,6},{5,7},{6,4},{7,5},{8,10},{9,11},{10,... | collective-permute-start | bytes 393224 | tf_op jit(solution)/shard_map/ppermute | solution.py:52
  100.6 2.3 %collective-permute-start.10 = (bf16[2,2,128,128]{3,2,1,0:T(8,128)(2,1)S(1)}, bf16[2,2,128,128]{3,2,1,0:T(8,128)(2,1)S(1)}, u32[]{:S(2)}, u32[]{:S(2)}) collective-permute-start(bf16[2,2,128,128]{3,2,1,0:T(8,128)(2,1)S(1)} %get-tuple-element.78), channel_id=1, source_target_pairs={{0,6},{1,7},{2,4},{3,5},{4,2},{5,3},{6,0},{7,1},{8,14},{9,15},{10,... | collective-permute-start | bytes 393224 | tf_op jit(solution)/shard_map/ppermute | solution.py:52
  102.9 7.3 %collective-permute-done.12.refs_2_ = bf16[2,128,512]{2,1,0:T(8,128)(2,1)S(1)} collective-permute-done((bf16[2,128,512]{2,1,0:T(8,128)(2,1)}, bf16[2,128,512]{2,1,0:T(8,128)(2,1)S(1)}, u32[]{:S(2)}, u32[]{:S(2)}) %collective-permute-start.12) | collective-permute-done | bytes 262176 | tf_op jit(solution)/shard_map/ppermute | solution.py:52
  110.2 4.2 %collective-permute-done.9.refs_2_ = bf16[2,2,128,128]{3,2,1,0:T(8,128)(2,1)S(1)} collective-permute-done((bf16[2,2,128,128]{3,2,1,0:T(8,128)(2,1)S(1)}, bf16[2,2,128,128]{3,2,1,0:T(8,128)(2,1)S(1)}, u32[]{:S(2)}, u32[]{:S(2)}) %collective-permute-start.9) | collective-permute-done | bytes 131104 | tf_op jit(solution)/shard_map/ppermute | solution.py:52
  116.8 1.8 %shard_map.140 = (f32[128,1024]{1,0:T(8,128)}, f32[128,1024]{1,0:T(8,128)}, f32[128,512]{1,0:T(8,128)}, f32[128,512]{1,0:T(8,128)}) custom-call(s32[2]{0:T(128)S(1)} %pad_add_fusion.ctl, f32[4,2,32,512]{3,2,1,0:T(8,128)S(1)} %all-to-all-done.2.mem, bf16[2,2,128,128]{3,2,1,0:T(8,128)(2,1)S(1)} %get-tuple-element.89.refs_0_, ...), custom_call_target="tpu_custom_call" | custom-call | tf_op jit(solution)/shard_map/pallas_call | solution.py:65
  (64 shorter events, 16.5 us)
Async XLA Ops:
  3.8 9.5 %collective-permute-start.4 = (bf16[4,2,128,512]{3,2,1,0:T(8,128)(2,1)S(1)}, bf16[4,2,128,512]{3,2,1,0:T(8,128)(2,1)S(1)}, u32[]{:S(2)}, u32[]{:S(2)}) collective-permute-start(bf16[4,2,128,512]{3,2,1,0:T(8,128)(2,1)S(1)} %shard_map.130), channel_id=1, source_target_pairs={{0,1},{1,0},{2,3},{3,2},{4,5},{5,4},{6,7},{7,6},{8,9},{9,8},{10,11... | collective-permute-start | bytes 3145736 | tf_op jit(solution)/shard_map/ppermute | solution.py:52
  5.0 2.0 %collective-permute-start = (bf16[4,2,128,128]{3,2,1,0:T(8,128)(2,1)S(1)}, bf16[4,2,128,128]{3,2,1,0:T(8,128)(2,1)S(1)}, u32[]{:S(2)}, u32[]{:S(2)}) collective-permute-start(bf16[4,2,128,128]{3,2,1,0:T(8,128)(2,1)S(1)} %shard_map.128), channel_id=1, source_target_pairs={{0,1},{1,0},{2,3},{3,2},{4,5},{5,4},{6,7},{7,6},{8,9},{9,8},{10,11... | collective-permute-start | bytes 786440 | tf_op jit(solution)/shard_map/ppermute | solution.py:52
  7.6 8.7 %collective-permute-start.1 = (bf16[2,2,128,128]{3,2,1,0:T(8,128)(2,1)S(1)}, bf16[2,2,128,128]{3,2,1,0:T(8,128)(2,1)S(1)}, u32[]{:S(2)}, u32[]{:S(2)}) collective-permute-start(bf16[2,2,128,128]{3,2,1,0:T(8,128)(2,1)S(1)} %get-tuple-element.51), channel_id=1, source_target_pairs={{0,2},{1,3},{2,0},{3,1},{4,6},{5,7},{6,4},{7,5},{8,10},{9,11},{10,... | collective-permute-start | bytes 393224 | tf_op jit(solution)/shard_map/ppermute | solution.py:52
  10.6 12.9 %collective-permute-start.2 = (bf16[2,2,128,128]{3,2,1,0:T(8,128)(2,1)S(1)}, bf16[2,2,128,128]{3,2,1,0:T(8,128)(2,1)S(1)}, u32[]{:S(2)}, u32[]{:S(2)}) collective-permute-start(bf16[2,2,128,128]{3,2,1,0:T(8,128)(2,1)S(1)} %get-tuple-element.52), channel_id=1, source_target_pairs={{0,4},{1,5},{2,6},{3,7},{4,0},{5,1},{6,2},{7,3},{8,12},{9,13},{10,... | collective-permute-start | bytes 393224 | tf_op jit(solution)/shard_map/ppermute | solution.py:52
  13.2 21.1 %copy-start.13 = (f32[1024,4]{0,1:T(4,128)S(1)}, f32[1024,4]{0,1:T(4,128)}, u32[]{:S(2)}) copy-start(f32[1024,4]{0,1:T(4,128)} %param.14) | copy-start | bytes 49156
  13.2 21.1 %copy-start.14 = (f32[1024,4]{0,1:T(4,128)S(1)}, f32[1024,4]{0,1:T(4,128)}, u32[]{:S(2)}) copy-start(f32[1024,4]{0,1:T(4,128)} %param.13) | copy-start | bytes 49156
  13.2 34.1 %copy-start.4 = (bf16[128,512]{1,0:T(8,128)(2,1)S(1)}, bf16[128,512]{1,0:T(8,128)(2,1)}, u32[]{:S(2)}) copy-start(bf16[128,512]{1,0:T(8,128)(2,1)} %refs_4_.3) | copy-start | bytes 393220
  13.2 34.1 %copy-start.5 = (bf16[128,512]{1,0:T(8,128)(2,1)S(1)}, bf16[128,512]{1,0:T(8,128)(2,1)}, u32[]{:S(2)}) copy-start(bf16[128,512]{1,0:T(8,128)(2,1)} %refs_5_.5) | copy-start | bytes 393220
  13.2 10.3 %collective-permute-start.3 = (bf16[2,2,128,128]{3,2,1,0:T(8,128)(2,1)S(1)}, bf16[2,2,128,128]{3,2,1,0:T(8,128)(2,1)S(1)}, u32[]{:S(2)}, u32[]{:S(2)}) collective-permute-start(bf16[2,2,128,128]{3,2,1,0:T(8,128)(2,1)S(1)} %get-tuple-element.53), channel_id=1, source_target_pairs={{0,6},{1,7},{2,4},{3,5},{4,2},{5,3},{6,0},{7,1},{8,14},{9,15},{10,... | collective-permute-start | bytes 393224 | tf_op jit(solution)/shard_map/ppermute | solution.py:52
  23.5 23.8 %collective-permute-start.7 = (bf16[2,2,128,512]{3,2,1,0:T(8,128)(2,1)}, bf16[2,2,128,512]{3,2,1,0:T(8,128)(2,1)}, u32[]{:S(2)}, u32[]{:S(2)}) collective-permute-start(bf16[2,2,128,512]{3,2,1,0:T(8,128)(2,1)} %get-tuple-element.66), channel_id=1, source_target_pairs={{0,2},{1,3},{2,0},{3,1},{4,6},{5,7},{6,4},{7,5},{8,10},{9,11},{10,... | collective-permute-start | bytes 1572872 | tf_op jit(solution)/shard_map/ppermute | solution.py:52
  25.8 38.4 %collective-permute-start.6 = (bf16[2,2,128,512]{3,2,1,0:T(8,128)(2,1)}, bf16[2,2,128,512]{3,2,1,0:T(8,128)(2,1)S(1)}, u32[]{:S(2)}, u32[]{:S(2)}) collective-permute-start(bf16[2,2,128,512]{3,2,1,0:T(8,128)(2,1)} %get-tuple-element.64), channel_id=1, source_target_pairs={{0,4},{1,5},{2,6},{3,7},{4,0},{5,1},{6,2},{7,3},{8,12},{9,13},{10,... | collective-permute-start | bytes 1572872 | tf_op jit(solution)/shard_map/ppermute | solution.py:52
  26.8 41.5 %collective-permute-start.5 = (bf16[2,2,128,512]{3,2,1,0:T(8,128)(2,1)}, bf16[2,2,128,512]{3,2,1,0:T(8,128)(2,1)S(1)}, u32[]{:S(2)}, u32[]{:S(2)}) collective-permute-start(bf16[2,2,128,512]{3,2,1,0:T(8,128)(2,1)} %get-tuple-element.55), channel_id=1, source_target_pairs={{0,6},{1,7},{2,4},{3,5},{4,2},{5,3},{6,0},{7,1},{8,14},{9,15},{10,... | collective-permute-start | bytes 1572872 | tf_op jit(solution)/shard_map/ppermute | solution.py:52
  30.6 9.1 %all-to-all-start = ((bf16[4,2,128,128]{3,2,1,0:T(8,128)(2,1)}), bf16[4,2,128,128]{3,2,1,0:T(8,128)(2,1)S(1)}, u32[]{:S(2)}, u32[]{:S(2)}) async-start(bf16[4,2,128,128]{3,2,1,0:T(8,128)(2,1)} %get-tuple-element.63), calls=%async_computation | async-start | bytes 524288 | tf_op jit(solution)/shard_map/all_to_all | solution.py:56
  73.2 11.6 %all-to-all-start.1 = ((bf16[4,4,128,128]{3,2,1,0:T(8,128)(2,1)}), bf16[4,4,128,128]{3,2,1,0:T(8,128)(2,1)S(1)}, u32[]{:S(2)}, u32[]{:S(2)}) async-start(bf16[4,4,128,128]{3,2,1,0:T(8,128)(2,1)} %copy-done.8), calls=%async_computation.1 | async-start | bytes 1048576 | tf_op jit(solution)/shard_map/all_to_all | solution.py:56
  77.0 21.6 %copy-start.10 = (bf16[2,128,512]{2,1,0:T(8,128)(2,1)S(1)}, bf16[2,128,512]{2,1,0:T(8,128)(2,1)}, u32[]{:S(2)}) copy-start(bf16[2,128,512]{2,1,0:T(8,128)(2,1)} %copy-done.9) | copy-start | bytes 786436
  77.0 23.7 %collective-permute-start.13 = (bf16[2,128,512]{2,1,0:T(8,128)(2,1)}, bf16[2,128,512]{2,1,0:T(8,128)(2,1)S(1)}, u32[]{:S(2)}, u32[]{:S(2)}) collective-permute-start(bf16[2,128,512]{2,1,0:T(8,128)(2,1)} %copy-done.11), channel_id=1, source_target_pairs={{0,6},{1,7},{2,4},{3,5},{4,2},{5,3},{6,0},{7,1},{8,14},{9,15},{10,... | collective-permute-start | bytes 786440 | tf_op jit(solution)/shard_map/ppermute | solution.py:52
  86.9 27.5 %all-to-all-start.2 = ((f32[4,2,32,512]{3,2,1,0:T(8,128)}), f32[4,2,32,512]{3,2,1,0:T(8,128)S(1)}, u32[]{:S(2)}, u32[]{:S(2)}) async-start(f32[4,2,32,512]{3,2,1,0:T(8,128)} %get-tuple-element.79), calls=%async_computation.2 | async-start | bytes 1048576 | tf_op jit(solution)/shard_map/all_to_all | solution.py:56
  90.4 19.8 %collective-permute-start.12 = (bf16[2,128,512]{2,1,0:T(8,128)(2,1)}, bf16[2,128,512]{2,1,0:T(8,128)(2,1)S(1)}, u32[]{:S(2)}, u32[]{:S(2)}) collective-permute-start(bf16[2,128,512]{2,1,0:T(8,128)(2,1)} %get-tuple-element.82), channel_id=1, source_target_pairs={{0,4},{1,5},{2,6},{3,7},{4,0},{5,1},{6,2},{7,3},{8,12},{9,13},{10,... | collective-permute-start | bytes 786440 | tf_op jit(solution)/shard_map/ppermute | solution.py:52
  98.5 11.7 %collective-permute-start.11 = (bf16[2,128,512]{2,1,0:T(8,128)(2,1)S(1)}, bf16[2,128,512]{2,1,0:T(8,128)(2,1)S(1)}, u32[]{:S(2)}, u32[]{:S(2)}) collective-permute-start(bf16[2,128,512]{2,1,0:T(8,128)(2,1)S(1)} %copy-done.10), channel_id=1, source_target_pairs={{0,2},{1,3},{2,0},{3,1},{4,6},{5,7},{6,4},{7,5},{8,10},{9,11},{10,... | collective-permute-start | bytes 786440 | tf_op jit(solution)/shard_map/ppermute | solution.py:52
  98.5 11.7 %collective-permute-start.8 = (bf16[2,2,128,128]{3,2,1,0:T(8,128)(2,1)}, bf16[2,2,128,128]{3,2,1,0:T(8,128)(2,1)S(1)}, u32[]{:S(2)}, u32[]{:S(2)}) collective-permute-start(bf16[2,2,128,128]{3,2,1,0:T(8,128)(2,1)} %copy-done.12), channel_id=1, source_target_pairs={{0,2},{1,3},{2,0},{3,1},{4,6},{5,7},{6,4},{7,5},{8,10},{9,11},{10,... | collective-permute-start | bytes 393224 | tf_op jit(solution)/shard_map/ppermute | solution.py:52
  100.5 13.9 %collective-permute-start.9 = (bf16[2,2,128,128]{3,2,1,0:T(8,128)(2,1)S(1)}, bf16[2,2,128,128]{3,2,1,0:T(8,128)(2,1)S(1)}, u32[]{:S(2)}, u32[]{:S(2)}) collective-permute-start(bf16[2,2,128,128]{3,2,1,0:T(8,128)(2,1)S(1)} %get-tuple-element.77), channel_id=1, source_target_pairs={{0,4},{1,5},{2,6},{3,7},{4,0},{5,1},{6,2},{7,3},{8,12},{9,13},{10,... | collective-permute-start | bytes 393224 | tf_op jit(solution)/shard_map/ppermute | solution.py:52
  100.6 13.8 %collective-permute-start.10 = (bf16[2,2,128,128]{3,2,1,0:T(8,128)(2,1)S(1)}, bf16[2,2,128,128]{3,2,1,0:T(8,128)(2,1)S(1)}, u32[]{:S(2)}, u32[]{:S(2)}) collective-permute-start(bf16[2,2,128,128]{3,2,1,0:T(8,128)(2,1)S(1)} %get-tuple-element.78), channel_id=1, source_target_pairs={{0,6},{1,7},{2,4},{3,5},{4,2},{5,3},{6,0},{7,1},{8,14},{9,15},{10,... | collective-permute-start | bytes 393224 | tf_op jit(solution)/shard_map/ppermute | solution.py:52
  114.4 4.2 %collective-permute-start.14 = (bf16[4,128,512]{2,1,0:T(8,128)(2,1)S(1)}, bf16[4,128,512]{2,1,0:T(8,128)(2,1)S(1)}, u32[]{:S(2)}, u32[]{:S(2)}) collective-permute-start(bf16[4,128,512]{2,1,0:T(8,128)(2,1)S(1)} %shard_map.137), channel_id=1, source_target_pairs={{0,1},{1,0},{2,3},{3,2},{4,5},{5,4},{6,7},{7,6},{8,9},{9,8},{10,11... | collective-permute-start | bytes 1572872 | tf_op jit(solution)/shard_map/ppermute | solution.py:52
  114.6 2.2 %collective-permute-start.15 = (bf16[4,2,128,128]{3,2,1,0:T(8,128)(2,1)S(1)}, bf16[4,2,128,128]{3,2,1,0:T(8,128)(2,1)S(1)}, u32[]{:S(2)}, u32[]{:S(2)}) collective-permute-start(bf16[4,2,128,128]{3,2,1,0:T(8,128)(2,1)S(1)} %shard_map.139), channel_id=1, source_target_pairs={{0,1},{1,0},{2,3},{3,2},{4,5},{5,4},{6,7},{7,6},{8,9},{9,8},{10,11... | collective-permute-start | bytes 786440 | tf_op jit(solution)/shard_map/ppermute | solution.py:52
  (11 other events, 59.2 us)

commit v4 on v3

--- a/solution.py
+++ b/solution.py
@@ -50,6 +50,15 @@
 
 def swap(piece, k):
     return lax.ppermute(piece, "uly", [(i, i ^ k) for i in range(lax.axis_size("uly"))])
+
+
+def across_spans(pieces):
+    spans = len(pieces)
+    if even(spans) and spans <= MAX_PERMUTES:
+        pairs = [[(i, i ^ k) for i in range(spans)] for k in range(spans)]
+        return pieces[:1] + [lax.ppermute(pieces[k], "blk", pairs[k]) for k in range(1, spans)]
+    order = partner(lax.axis_index("blk"), jnp.arange(spans, dtype=jnp.int32), spans)
+    return list(to_spans(jnp.stack(pieces)[order])[order])
 
 
 def to_spans(stacked):
@@ -198,7 +207,8 @@
         prev = take(3)
     dqs = take(1 if looped else len(js))
     if last:
-        local, own_mem, backs = take(3)
+        local, own_mem = take(2)
+        backs = take(lay.spans)
         acc, dmk, dmv, slot_pool, mkt = take(5)
     else:
         acc, dmk, dmv = take(3)
@@ -278,14 +288,15 @@
 
     if last:
         local[...] = acc[:ways]
-        for s in range(lay.spans):
-            backs[s, 0] = (acc[ways + s, 0] * SCALE).astype(jnp.bfloat16)
-            backs[s, 1] = acc[ways + s, 1].astype(jnp.bfloat16)
+        for k, back in enumerate(backs):
+            span = partner(ctl[1], k, lay.spans)
+            back[0] = (acc[ways + span, 0] * SCALE).astype(jnp.bfloat16)
+            back[1] = acc[ways + span, 1].astype(jnp.bfloat16)
             for h in heads if lay.mem_rows else ():
-                rows = pl.ds(s * lay.mem_rows, lay.mem_rows)
+                rows = pl.ds(pl.multiple_of(span * lay.mem_rows, lay.mem_rows), lay.mem_rows)
                 at = pl.ds(h * lay.mem_rows, lay.mem_rows)
-                backs[s, 2, at] = (dmk[rows, col(h)] * SCALE).astype(jnp.bfloat16)
-                backs[s, 3, at] = dmv[rows, col(h)].astype(jnp.bfloat16)
+                back[2, at] = (dmk[rows, col(h)] * SCALE).astype(jnp.bfloat16)
+                back[3, at] = dmv[rows, col(h)].astype(jnp.bfloat16)
         rows = slice(None)
         if lay.mem_rows:
             rows = pl.ds(pl.multiple_of(ctl[1] * lay.mem_rows, lay.mem_rows), lay.mem_rows)
@@ -314,8 +325,8 @@
         outs += [
             array((lay.ways, 2, BLOCK, HEAD_FEATURES), jnp.float32),
             array((2, lay.mem_rows or BLOCK, lay.width), jnp.float32),
-            array((lay.spans, 4 if lay.mem_rows else 2, BLOCK, HEAD_FEATURES)),
         ]
+        outs += [array((4 if lay.mem_rows else 2, BLOCK, HEAD_FEATURES))] * lay.spans
         scratch = [pltpu.VMEM(t.shape, t.dtype) for t in totals] + scratch
     else:
         outs += totals
@@ -336,28 +347,27 @@
     return dict(zip(js, dq)), done[1 if looped else len(js) :]
 
 
-def merge_kernel(lay, ctl, local, own_mem, backs, *refs):
-    *pieces, mem_sum, total = refs
+def merge_kernel(lay, ctl, local, own_mem, *refs):
+    backs = refs[: lay.spans]
+    *pieces, mem_sum, total = refs[lay.spans :]
     for k in range(lay.ways):
         total[k, 0] = local[k, 0] * SCALE
         total[k, 1] = local[k, 1]
     mem = [own_mem[0], own_mem[1]]
-    for s in range(lay.spans):
-
-        @pl.when(s != ctl[1])
+    for k, back in enumerate(backs):
+        span = partner(ctl[1], k, lay.spans)
+
+        @pl.when(span != ctl[1])
         def _():
-            at = lay.send_index(ctl, s)
+            at = lay.send_index(ctl, span)
             for i in range(2):
-                total[at, i] += backs[s, i].astype(jnp.float32)
+                total[at, i] += back[i].astype(jnp.float32)
 
         if lay.mem_rows:
             for i in range(2):
-                term = [
-                    backs[s, 2 + i, pl.ds(h * lay.mem_rows, lay.mem_rows)]
-                    for h in range(lay.heads)
-                ]
-                term = jnp.concatenate(term, axis=1).astype(jnp.float32)
-                mem[i] += jnp.where(s == ctl[1], 0.0, term)
+                rows = [pl.ds(h * lay.mem_rows, lay.mem_rows) for h in range(lay.heads)]
+                term = jnp.concatenate([back[2 + i, r] for r in rows], axis=1)
+                mem[i] += jnp.where(span == ctl[1], 0.0, term.astype(jnp.float32))
     for s in range(mem_sum.shape[0]):
         for i in range(2):
             mem_sum[s, i] = mem[i]
@@ -373,14 +383,11 @@
         yield 2 * j + 1, others.at[j]
 
 
-def join_kernel(lay, ctl, *refs):
-    *pieces, out = refs
-    for k, piece in by_partner(pieces):
-        out[:, col(partner(ctl[0], k, lay.ways), lay.width)] = piece[...]
-
-
 def finish_kernel(lay, ctl, mem, *refs):
-    *pieces, out_k, out_v, out_mk, out_mv = refs
+    *pieces, out_q, out_k, out_v, out_mk, out_mv = refs
+    pieces, query_pieces = pieces[: len(pieces) // 2], pieces[len(pieces) // 2 :]
+    for k, piece in by_partner(query_pieces):
+        out_q[:, col(partner(ctl[0], k, lay.ways), lay.width)] = piece[...]
     shared = lay.heads < GROUP
     if shared:
         out_k[...] = jnp.zeros_like(out_k)
@@ -421,13 +428,14 @@
     if in_stages:
         half = max(1, chips // 2)
         steps = [range(half), *([j] for j in range(half, chips))]
-        qd[half] = swap(qd[half], 2 * half)
         for j in [*range(half, chips), *range(1, half)]:
             kv[j] = swap(kv[j], 2 * j)
+        qd[half] = swap(qd[half], 2 * half)
+        qd[1] = swap(qd[1], 2)
         kv[1:], qd[half + 1] = after(kv[1:], qd[half + 1])
-        kv[1], qd[1] = after(kv[1], qd[1])
         qd[half + 1] = swap(qd[half + 1], 2 * half + 2)
-        qd[1] = swap(qd[1], 2)
+        first = (qd[1], qd[half])
+        (qd[1], qd[half]), kv[0] = after(first, kv[0])
     pool, slots = call(
         functools.partial(pool_kernel, lay),
         [
@@ -448,12 +456,12 @@
             lay, step, ctl, qd, pool, slots, stats, memory_keys, memory_values, totals, last
         )
         dq |= step_dq
-    local, own_mem, backs = totals
-    backs = to_spans(backs)
+    local, own_mem, *backs = totals
+    backs = across_spans(backs)
     if in_stages:
         for j in [*range(half, chips), *range(1, half)]:
             dq[j] = swap(dq[j], 2 * j)
-        pass
+        dq[half], backs = after(dq[half], backs)
     *dkv, mem = call(
         functools.partial(merge_kernel, lay),
         [array((2, 2, BLOCK, HEAD_FEATURES))] * chips
@@ -461,12 +469,13 @@
         ctl,
         local,
         own_mem,
-        backs,
+        *backs,
         scratch=[pltpu.VMEM((lay.ways, 2, BLOCK, HEAD_FEATURES), jnp.float32)],
     )
     mem = to_spans(mem) if lay.mem_rows else lax.psum(mem, "blk")
     dq = [dq[j] for j in range(chips)]
     if in_stages:
+        (dq[1], dq[half + 1]), dkv = after((dq[1], dq[half + 1]), dkv)
         for j in [*range(half, chips), *range(1, half)]:
             dkv[j] = swap(dkv[j], 2 * j)
         (dkv[1:], mem), dq = after((dkv[1:], mem), dq)
@@ -475,15 +484,14 @@
     else:
         dq = whole_exchange(dq)
         dkv = whole_exchange(dkv)
-    (grad_q,) = call(functools.partial(join_kernel, lay), [array(queries.shape)], place, *dq)
-    grad_k, grad_v, grad_mk, grad_mv = call(
+    return tuple(call(
         functools.partial(finish_kernel, lay),
-        [array(keys.shape, jnp.float32)] * 2 + [array(memory_keys.shape, jnp.float32)] * 2,
+        [array(queries.shape)] + [array(keys.shape, jnp.float32)] * 2 + [array(memory_keys.shape, jnp.float32)] * 2,
         place,
         mem,
         *dkv,
-    )
-    return grad_q, grad_k, grad_v, grad_mk, grad_mv
+        *dq,
+    ))
 
 
 def solution(mesh):

time: 121 us -> 113 us (0.934)
  waiting for transfers between devices: 52.2 us -> 47.4 us
  starting transfers between devices: 37.9 us -> 33.6 us
  local copies, waits for them, and re-layouts: 4.18 us -> 6.1 us
  Pallas kernels: 25 us -> 23.3 us
    all_to_all x3 -> x2, waiting for transfers between devices: 10.8 us -> 4.63 us  [to_spans(): return lax.all_to_all(stacked, 'blk', 0, 0, tiled=True)]
    ppermute x16, starting transfers between devices: 27 us -> 22.9 us  [swap(): lax.ppermute(piece, 'uly', [(i, i ^ k) for i in range(lax.axis_size('uly'...]
    all_to_all x3 -> x2, starting transfers between devices: 10.9 us -> 7.19 us  [to_spans(): return lax.all_to_all(stacked, 'blk', 0, 0, tiled=True)]
    ppermute x0 -> x3, starting transfers between devices: none -> 3.49 us  [across_spans(): lax.ppermute(pieces[k], 'blk', pairs[k])]
    unnamed x33 -> x27, local copies, waits for them, and re-layouts: 4.08 us -> 6 us
    pallas_call x13 -> x12, Pallas kernels: 25 us -> 23.3 us  [call(): pl.pallas_call(kernel, in_specs=[SMEM_SPEC] + [pl.BlockSpec(memory_space=...]
  transfers between devices with their start and end apart: 19 -> 21, of which waited for: 10 -> 10; matrix products, arithmetic and copies ran while one was open for 0% -> 1% of each run, Pallas kernels for 16% -> 18%
where the time goes in v4:
time: 113 us; the launch traced here: 112 us
  waiting for transfers between devices  47.4 us (42%)
  starting transfers between devices  33.6 us (30%)
  Pallas kernels  23.3 us (21%)
  local copies, waits for them, and re-layouts  6.1 us (5%)
    ppermute x16, waiting for transfers between devices, swap(): lax.ppermute(piece, 'uly', [(i, i ^ k) for i in range(lax.axis_size('uly'...  41.7 us
    pallas_call x12, Pallas kernels, call(): pl.pallas_call(kernel, in_specs=[SMEM_SPEC] + [pl.BlockSpec(memory_space=...  23.3 us
    ppermute x16, starting transfers between devices, swap(): lax.ppermute(piece, 'uly', [(i, i ^ k) for i in range(lax.axis_size('uly'...  22.9 us
    all_to_all x2, starting transfers between devices, to_spans(): return lax.all_to_all(stacked, 'blk', 0, 0, tiled=True)  7.19 us
    unnamed x27, local copies, waits for them, and re-layouts  6 us
    all_to_all x2, waiting for transfers between devices, to_spans(): return lax.all_to_all(stacked, 'blk', 0, 0, tiled=True)  4.63 us
    ppermute x3, starting transfers between devices, across_spans(): lax.ppermute(pieces[k], 'blk', pairs[k])  3.49 us
  transfers between devices with their start and end apart: 21, of which 10 were waited for; matrix products, arithmetic and copies ran while one was open for 1% of the time, Pallas kernels for 18%

profile of v4, /device:TPU:0, one launch (start us, length us, event | category | flops | bytes accessed | tf_op | source)
XLA Modules:
  0.0 112.1 jit_solution(13490394959657539622)
XLA Ops:
  6.6 1.7 %shard_map.129 = (bf16[2,2,128,512]{3,2,1,0:T(8,128)(2,1)S(1)}, bf16[2,2,128,512]{3,2,1,0:T(8,128)(2,1)}, bf16[2,2,128,512]{3,2,1,0:T(8,128)(2,1)S(1)}, bf16[2,2,128,512]{3,2,1,0:T(8,128)(2,1)}) custom-call(s32[2]{0:T(128)S(1)} %pad_add_fusion.ctl, bf16[128,4096]{1,0:T(8,128)(2,1)S(1)} %copy-done.1, bf16[128,4096]{1,0:T(8,128)(2,1)S(1)} %copy-done.2, ...), custom_call_target="tpu_custom_call" | custom-call | tf_op jit(solution)/shard_map/pallas_call | solution.py:74
  8.3 2.9 %collective-permute-start.1 = (bf16[2,2,128,512]{3,2,1,0:T(8,128)(2,1)}, bf16[2,2,128,512]{3,2,1,0:T(8,128)(2,1)S(1)}, u32[]{:S(2)}, u32[]{:S(2)}) collective-permute-start(bf16[2,2,128,512]{3,2,1,0:T(8,128)(2,1)} %get-tuple-element.63), channel_id=1, source_target_pairs={{0,2},{1,3},{2,0},{3,1},{4,6},{5,7},{6,4},{7,5},{8,10},{9,11},{10,... | collective-permute-start | bytes 1572872 | tf_op jit(solution)/shard_map/ppermute | solution.py:52
  11.2 2.6 %collective-permute-start.2 = (bf16[2,2,128,512]{3,2,1,0:T(8,128)(2,1)S(1)}, bf16[2,2,128,512]{3,2,1,0:T(8,128)(2,1)S(1)}, u32[]{:S(2)}, u32[]{:S(2)}) collective-permute-start(bf16[2,2,128,512]{3,2,1,0:T(8,128)(2,1)S(1)} %get-tuple-element.64), channel_id=1, source_target_pairs={{0,4},{1,5},{2,6},{3,7},{4,0},{5,1},{6,2},{7,3},{8,12},{9,13},{10,... | collective-permute-start | bytes 1572872 | tf_op jit(solution)/shard_map/ppermute | solution.py:52
  15.0 3.9 %collective-permute-start.6 = (bf16[2,2,128,128]{3,2,1,0:T(8,128)(2,1)S(1)}, bf16[2,2,128,128]{3,2,1,0:T(8,128)(2,1)S(1)}, u32[]{:S(2)}, u32[]{:S(2)}) collective-permute-start(bf16[2,2,128,128]{3,2,1,0:T(8,128)(2,1)S(1)} %get-tuple-element.70), channel_id=1, source_target_pairs={{0,6},{1,7},{2,4},{3,5},{4,2},{5,3},{6,0},{7,1},{8,14},{9,15},{10,... | collective-permute-start | bytes 393224 | tf_op jit(solution)/shard_map/ppermute | solution.py:52
  18.9 20.8 %collective-permute-done.4.refs_1_ = bf16[2,2,128,128]{3,2,1,0:T(8,128)(2,1)S(1)} collective-permute-done((bf16[2,2,128,128]{3,2,1,0:T(8,128)(2,1)S(1)}, bf16[2,2,128,128]{3,2,1,0:T(8,128)(2,1)S(1)}, u32[]{:S(2)}, u32[]{:S(2)}) %collective-permute-start.4) | collective-permute-done | bytes 131104 | tf_op jit(solution)/shard_map/ppermute | solution.py:52
  39.7 6.9 %collective-permute-done.5.refs_2_ = bf16[2,2,128,128]{3,2,1,0:T(8,128)(2,1)S(1)} collective-permute-done((bf16[2,2,128,128]{3,2,1,0:T(8,128)(2,1)S(1)}, bf16[2,2,128,128]{3,2,1,0:T(8,128)(2,1)S(1)}, u32[]{:S(2)}, u32[]{:S(2)}) %collective-permute-start.5) | collective-permute-done | bytes 131104 | tf_op jit(solution)/shard_map/ppermute | solution.py:52
  47.2 2.5 %collective-permute-start.8 = (bf16[2,2,128,512]{3,2,1,0:T(8,128)(2,1)}, bf16[2,2,128,512]{3,2,1,0:T(8,128)(2,1)S(1)}, u32[]{:S(2)}, u32[]{:S(2)}) collective-permute-start(bf16[2,2,128,512]{3,2,1,0:T(8,128)(2,1)} %get-tuple-element.78), channel_id=1, source_target_pairs={{0,6},{1,7},{2,4},{3,5},{4,2},{5,3},{6,0},{7,1},{8,14},{9,15},{10,... | collective-permute-start | bytes 1572872 | tf_op jit(solution)/shard_map/ppermute | solution.py:52
  51.1 1.3 %shard_map.132 = (bf16[8,3,128,128]{3,2,1,0:T(8,128)(2,1)S(1)}, bf16[4,2,128,128]{3,2,1,0:T(8,128)(2,1)S(1)}) custom-call(s32[66]{0:T(128)S(1)} %pad_add_fusion.1.ctl, bf16[2,2,128,128]{3,2,1,0:T(8,128)(2,1)S(1)} %get-tuple-element.67.refs_0_, bf16[2,2,128,128]{3,2,1,0:T(8,128)(2,1)S(1)} %collective-permute-done.4.refs_1_, ...), custom_call_target="tpu_custom_call" | custom-call | tf_op jit(solution)/shard_map/pallas_call | solution.py:74
  53.1 3.7 %all-to-all-start = ((bf16[4,2,128,128]{3,2,1,0:T(8,128)(2,1)}), bf16[4,2,128,128]{3,2,1,0:T(8,128)(2,1)S(1)}, u32[]{:S(2)}, u32[]{:S(2)}) async-start(bf16[4,2,128,128]{3,2,1,0:T(8,128)(2,1)} %copy-done.9), calls=%async_computation | async-start | bytes 524288 | tf_op jit(solution)/shard_map/all_to_all | solution.py:65
  57.6 4.6 %all-to-all-done.refs_3_.refs_2_ = bf16[4,2,128,128]{3,2,1,0:T(8,128)(2,1)S(1)} async-done(((bf16[4,2,128,128]{3,2,1,0:T(8,128)(2,1)}), bf16[4,2,128,128]{3,2,1,0:T(8,128)(2,1)S(1)}, u32[]{:S(2)}, u32[]{:S(2)}) %all-to-all-start) | async-done | bytes 262176 | tf_op jit(solution)/shard_map/all_to_all | solution.py:65
  63.3 6.5 %shard_map.133 = (bf16[2,128,512]{2,1,0:T(8,128)(2,1)S(1)}, bf16[2,128,512]{2,1,0:T(8,128)(2,1)}, f32[12,2,128,128]{3,2,1,0:T(8,128)S(1)}, f32[128,512]{1,0:T(8,128)S(1)}, f32[128,512]{1,0:T(8,128)S(1)}) custom-call(s32[66]{0:T(128)S(1)} %pad_add_fusion.1.ctl, bf16[2,2,128,512]{3,2,1,0:T(8,128)(2,1)S(1)} %get-tuple-element.62.refs_0_, ...), custom_call_target="tpu_custom_call" | custom-call | tf_op jit(solution)/shard_map/pallas_call | solution.py:74
  69.8 3.4 %shard_map.134 = (bf16[2,128,512]{2,1,0:T(8,128)(2,1)S(1)}, f32[12,2,128,128]{3,2,1,0:T(8,128)S(1)}, f32[128,512]{1,0:T(8,128)S(1)}, f32[128,512]{1,0:T(8,128)S(1)}) custom-call(s32[66]{0:T(128)S(1)} %pad_add_fusion.1.ctl, bf16[2,2,128,512]{3,2,1,0:T(8,128)(2,1)S(1)} %collective-permute-done.2.refs_0_, ...), custom_call_target="tpu_custom_call" | custom-call | tf_op jit(solution)/shard_map/pallas_call | solution.py:74
  74.5 4.2 %shard_map.135 = (bf16[2,128,512]{2,1,0:T(8,128)(2,1)}, f32[8,2,128,128]{3,2,1,0:T(8,128)S(1)}, f32[2,32,512]{2,1,0:T(8,128)S(1)}, bf16[4,128,128]{2,1,0:T(8,128...) custom-call(s32[66]{0:T(128)S(1)} %pad_add_fusion.1.ctl, ...), custom_call_target="tpu_custom_call" | custom-call | tf_op jit(solution)/shard_map/pallas_call | solution.py:74
  80.5 1.6 %collective-permute-start.13 = (bf16[4,128,128]{2,1,0:T(8,128)(2,1)S(1)}, bf16[4,128,128]{2,1,0:T(8,128)(2,1)S(1)}, u32[]{:S(2)}, u32[]{:S(2)}) collective-permute-start(bf16[4,128,128]{2,1,0:T(8,128)(2,1)S(1)} %get-tuple-element.93), channel_id=1, source_target_pairs={{0,24},{8,16},{16,8},{24,0},{1,25},{9,17},{17,9},{25,1},{2,26},{10... | collective-permute-start | bytes 393224 | tf_op jit(solution)/shard_map/ppermute | solution.py:59
  83.6 2.5 %collective-permute-start.9 = (bf16[2,128,512]{2,1,0:T(8,128)(2,1)}, bf16[2,128,512]{2,1,0:T(8,128)(2,1)S(1)}, u32[]{:S(2)}, u32[]{:S(2)}) collective-permute-start(bf16[2,128,512]{2,1,0:T(8,128)(2,1)} %get-tuple-element.86), channel_id=1, source_target_pairs={{0,6},{1,7},{2,4},{3,5},{4,2},{5,3},{6,0},{7,1},{8,14},{9,15},{10,... | collective-permute-start | bytes 786440 | tf_op jit(solution)/shard_map/ppermute | solution.py:52
  86.4 2.1 %shard_map.136 = (bf16[2,2,128,128]{3,2,1,0:T(8,128)(2,1)S(1)}, bf16[2,2,128,128]{3,2,1,0:T(8,128)(2,1)S(1)}, bf16[2,2,128,128]{3,2,1,0:T(8,128)(2,1)S(1)}, bf16...) custom-call(s32[66]{0:T(128)S(1)} %pad_add_fusion.1.ctl, f32[8,2,128,128]{3,2,1,0:T(8,128)S(1)} %get-tuple-element.87.local, ...), custom_call_target="tpu_custom_call" | custom-call | tf_op jit(solution)/shard_map/pallas_call | solution.py:74
  88.5 3.5 %all-to-all-start.1 = ((f32[4,2,32,512]{3,2,1,0:T(8,128)}), f32[4,2,32,512]{3,2,1,0:T(8,128)S(1)}, u32[]{:S(2)}, u32[]{:S(2)}) async-start(f32[4,2,32,512]{3,2,1,0:T(8,128)} %get-tuple-element.105), calls=%async_computation.1 | async-start | bytes 1048576 | tf_op jit(solution)/shard_map/all_to_all | solution.py:65
  91.9 4.1 %collective-permute-done.7.refs_1_.refs_6_ = bf16[2,128,512]{2,1,0:T(8,128)(2,1)S(1)} collective-permute-done((bf16[2,128,512]{2,1,0:T(8,128)(2,1)}, bf16[2,128,512]{2,1,0:T(8,128)(2,1)S(1)}, u32[]{:S(2)}, u32[]{:S(2)}) %collective-permute-start.7) | collective-permute-done | bytes 262176 | tf_op jit(solution)/shard_map/ppermute | solution.py:52
  96.0 2.2 %collective-permute-start.15 = (bf16[2,2,128,128]{3,2,1,0:T(8,128)(2,1)S(1)}, bf16[2,2,128,128]{3,2,1,0:T(8,128)(2,1)S(1)}, u32[]{:S(2)}, u32[]{:S(2)}) collective-permute-start(bf16[2,2,128,128]{3,2,1,0:T(8,128)(2,1)S(1)} %get-tuple-element.103), channel_id=1, source_target_pairs={{0,4},{1,5},{2,6},{3,7},{4,0},{5,1},{6,2},{7,3},{8,12},{9,13},{10,... | collective-permute-start | bytes 393224 | tf_op jit(solution)/shard_map/ppermute | solution.py:52
  98.2 2.2 %collective-permute-start.16 = (bf16[2,2,128,128]{3,2,1,0:T(8,128)(2,1)S(1)}, bf16[2,2,128,128]{3,2,1,0:T(8,128)(2,1)S(1)}, u32[]{:S(2)}, u32[]{:S(2)}) collective-permute-start(bf16[2,2,128,128]{3,2,1,0:T(8,128)(2,1)S(1)} %get-tuple-element.104), channel_id=1, source_target_pairs={{0,6},{1,7},{2,4},{3,5},{4,2},{5,3},{6,0},{7,1},{8,14},{9,15},{10,... | collective-permute-start | bytes 393224 | tf_op jit(solution)/shard_map/ppermute | solution.py:52
  100.4 2.0 %collective-permute-done.14.refs_1_ = bf16[2,2,128,128]{3,2,1,0:T(8,128)(2,1)S(1)} collective-permute-done((bf16[2,2,128,128]{3,2,1,0:T(8,128)(2,1)S(1)}, bf16[2,2,128,128]{3,2,1,0:T(8,128)(2,1)S(1)}, u32[]{:S(2)}, u32[]{:S(2)}) %collective-permute-start.14) | collective-permute-done | bytes 131104 | tf_op jit(solution)/shard_map/ppermute | solution.py:52
  102.4 5.0 %collective-permute-done.15.refs_2_ = bf16[2,2,128,128]{3,2,1,0:T(8,128)(2,1)S(1)} collective-permute-done((bf16[2,2,128,128]{3,2,1,0:T(8,128)(2,1)S(1)}, bf16[2,2,128,128]{3,2,1,0:T(8,128)(2,1)S(1)}, u32[]{:S(2)}, u32[]{:S(2)}) %collective-permute-start.15) | collective-permute-done | bytes 131104 | tf_op jit(solution)/shard_map/ppermute | solution.py:52
  108.1 1.7 %collective-permute-done.17.refs_4_ = bf16[4,2,128,128]{3,2,1,0:T(8,128)(2,1)S(1)} collective-permute-done((bf16[4,2,128,128]{3,2,1,0:T(8,128)(2,1)S(1)}, bf16[4,2,128,128]{3,2,1,0:T(8,128)(2,1)S(1)}, u32[]{:S(2)}, u32[]{:S(2)}) %collective-permute-start.17) | collective-permute-done | bytes 262176 | tf_op jit(solution)/shard_map/ppermute | solution.py:52
  109.8 2.2 %shard_map.139 = (bf16[128,4096]{1,0:T(8,128)(2,1)}, f32[128,1024]{1,0:T(8,128)}, f32[128,1024]{1,0:T(8,128)}, f32[128,512]{1,0:T(8,128)}, f32[128,512]{1,0:T(8,128)}) custom-call(s32[2]{0:T(128)S(1)} %pad_add_fusion.ctl, f32[4,2,32,512]{3,2,1,0:T(8,128)S(1)} %all-to-all-done.1.mem, bf16[2,2,128,128]{3,2,1,0:T(8,128)(2,1)S(1)} %get-tuple-element.111.refs_0_, ...), custom_call_target="tpu_custom_call" | custom-call | tf_op jit(solution)/shard_map/pallas_call | solution.py:74
  (61 shorter events, 17.1 us)
Async XLA Ops:
  3.8 2.8 %collective-permute-start = (bf16[4,2,128,512]{3,2,1,0:T(8,128)(2,1)S(1)}, bf16[4,2,128,512]{3,2,1,0:T(8,128)(2,1)S(1)}, u32[]{:S(2)}, u32[]{:S(2)}) collective-permute-start(bf16[4,2,128,512]{3,2,1,0:T(8,128)(2,1)S(1)} %shard_map.128), channel_id=1, source_target_pairs={{0,1},{1,0},{2,3},{3,2},{4,5},{5,4},{6,7},{7,6},{8,9},{9,8},{10,11... | collective-permute-start | bytes 3145736 | tf_op jit(solution)/shard_map/ppermute | solution.py:52
  4.9 44.8 %copy-start.12 = (s32[32,2]{0,1:T(2,128)S(1)}, s32[32,2]{0,1:T(2,128)}, u32[]{:S(2)}) copy-start(s32[32,2]{0,1:T(2,128)} %param.15) | copy-start | bytes 772
  5.0 8.8 %collective-permute-start.3 = (bf16[4,2,128,128]{3,2,1,0:T(8,128)(2,1)S(1)}, bf16[4,2,128,128]{3,2,1,0:T(8,128)(2,1)S(1)}, u32[]{:S(2)}, u32[]{:S(2)}) collective-permute-start(bf16[4,2,128,128]{3,2,1,0:T(8,128)(2,1)S(1)} %shard_map.130), channel_id=1, source_target_pairs={{0,1},{1,0},{2,3},{3,2},{4,5},{5,4},{6,7},{7,6},{8,9},{9,8},{10,11... | collective-permute-start | bytes 786440 | tf_op jit(solution)/shard_map/ppermute | solution.py:52
  8.3 54.0 %copy-start.3 = (bf16[128,512]{1,0:T(8,128)(2,1)S(1)}, bf16[128,512]{1,0:T(8,128)(2,1)}, u32[]{:S(2)}) copy-start(bf16[128,512]{1,0:T(8,128)(2,1)} %refs_4_.3) | copy-start | bytes 393220
  8.3 54.0 %copy-start.4 = (bf16[128,512]{1,0:T(8,128)(2,1)S(1)}, bf16[128,512]{1,0:T(8,128)(2,1)}, u32[]{:S(2)}) copy-start(bf16[128,512]{1,0:T(8,128)(2,1)} %refs_5_.5) | copy-start | bytes 393220
  8.3 41.8 %collective-permute-start.1 = (bf16[2,2,128,512]{3,2,1,0:T(8,128)(2,1)}, bf16[2,2,128,512]{3,2,1,0:T(8,128)(2,1)S(1)}, u32[]{:S(2)}, u32[]{:S(2)}) collective-permute-start(bf16[2,2,128,512]{3,2,1,0:T(8,128)(2,1)} %get-tuple-element.63), channel_id=1, source_target_pairs={{0,2},{1,3},{2,0},{3,1},{4,6},{5,7},{6,4},{7,5},{8,10},{9,11},{10,... | collective-permute-start | bytes 1572872 | tf_op jit(solution)/shard_map/ppermute | solution.py:52
  11.2 38.8 %collective-permute-start.2 = (bf16[2,2,128,512]{3,2,1,0:T(8,128)(2,1)S(1)}, bf16[2,2,128,512]{3,2,1,0:T(8,128)(2,1)S(1)}, u32[]{:S(2)}, u32[]{:S(2)}) collective-permute-start(bf16[2,2,128,512]{3,2,1,0:T(8,128)(2,1)S(1)} %get-tuple-element.64), channel_id=1, source_target_pairs={{0,4},{1,5},{2,6},{3,7},{4,0},{5,1},{6,2},{7,3},{8,12},{9,13},{10,... | collective-permute-start | bytes 1572872 | tf_op jit(solution)/shard_map/ppermute | solution.py:52
  14.4 25.3 %collective-permute-start.4 = (bf16[2,2,128,128]{3,2,1,0:T(8,128)(2,1)S(1)}, bf16[2,2,128,128]{3,2,1,0:T(8,128)(2,1)S(1)}, u32[]{:S(2)}, u32[]{:S(2)}) collective-permute-start(bf16[2,2,128,128]{3,2,1,0:T(8,128)(2,1)S(1)} %get-tuple-element.68), channel_id=1, source_target_pairs={{0,2},{1,3},{2,0},{3,1},{4,6},{5,7},{6,4},{7,5},{8,10},{9,11},{10,... | collective-permute-start | bytes 393224 | tf_op jit(solution)/shard_map/ppermute | solution.py:52
  14.9 31.6 %collective-permute-start.5 = (bf16[2,2,128,128]{3,2,1,0:T(8,128)(2,1)S(1)}, bf16[2,2,128,128]{3,2,1,0:T(8,128)(2,1)S(1)}, u32[]{:S(2)}, u32[]{:S(2)}) collective-permute-start(bf16[2,2,128,128]{3,2,1,0:T(8,128)(2,1)S(1)} %get-tuple-element.69), channel_id=1, source_target_pairs={{0,4},{1,5},{2,6},{3,7},{4,0},{5,1},{6,2},{7,3},{8,12},{9,13},{10,... | collective-permute-start | bytes 393224 | tf_op jit(solution)/shard_map/ppermute | solution.py:52
  15.0 31.6 %collective-permute-start.6 = (bf16[2,2,128,128]{3,2,1,0:T(8,128)(2,1)S(1)}, bf16[2,2,128,128]{3,2,1,0:T(8,128)(2,1)S(1)}, u32[]{:S(2)}, u32[]{:S(2)}) collective-permute-start(bf16[2,2,128,128]{3,2,1,0:T(8,128)(2,1)S(1)} %get-tuple-element.70), channel_id=1, source_target_pairs={{0,6},{1,7},{2,4},{3,5},{4,2},{5,3},{6,0},{7,1},{8,14},{9,15},{10,... | collective-permute-start | bytes 393224 | tf_op jit(solution)/shard_map/ppermute | solution.py:52
  47.2 27.2 %collective-permute-start.8 = (bf16[2,2,128,512]{3,2,1,0:T(8,128)(2,1)}, bf16[2,2,128,512]{3,2,1,0:T(8,128)(2,1)S(1)}, u32[]{:S(2)}, u32[]{:S(2)}) collective-permute-start(bf16[2,2,128,512]{3,2,1,0:T(8,128)(2,1)} %get-tuple-element.78), channel_id=1, source_target_pairs={{0,6},{1,7},{2,4},{3,5},{4,2},{5,3},{6,0},{7,1},{8,14},{9,15},{10,... | collective-permute-start | bytes 1572872 | tf_op jit(solution)/shard_map/ppermute | solution.py:52
  53.1 9.1 %all-to-all-start = ((bf16[4,2,128,128]{3,2,1,0:T(8,128)(2,1)}), bf16[4,2,128,128]{3,2,1,0:T(8,128)(2,1)S(1)}, u32[]{:S(2)}, u32[]{:S(2)}) async-start(bf16[4,2,128,128]{3,2,1,0:T(8,128)(2,1)} %copy-done.9), calls=%async_computation | async-start | bytes 524288 | tf_op jit(solution)/shard_map/all_to_all | solution.py:65
  73.2 13.2 %collective-permute-start.10 = (bf16[2,128,512]{2,1,0:T(8,128)(2,1)S(1)}, bf16[2,128,512]{2,1,0:T(8,128)(2,1)S(1)}, u32[]{:S(2)}, u32[]{:S(2)}) collective-permute-start(bf16[2,128,512]{2,1,0:T(8,128)(2,1)S(1)} %get-tuple-element.89), channel_id=1, source_target_pairs={{0,4},{1,5},{2,6},{3,7},{4,0},{5,1},{6,2},{7,3},{8,12},{9,13},{10,... | collective-permute-start | bytes 786440 | tf_op jit(solution)/shard_map/ppermute | solution.py:52
  78.6 5.0 %collective-permute-start.11 = (bf16[4,128,128]{2,1,0:T(8,128)(2,1)S(1)}, bf16[4,128,128]{2,1,0:T(8,128)(2,1)S(1)}, u32[]{:S(2)}, u32[]{:S(2)}) collective-permute-start(bf16[4,128,128]{2,1,0:T(8,128)(2,1)S(1)} %get-tuple-element.91), channel_id=1, source_target_pairs={{0,8},{8,0},{16,24},{24,16},{1,9},{9,1},{17,25},{25,17},{2,10},{10... | collective-permute-start | bytes 393224 | tf_op jit(solution)/shard_map/ppermute | solution.py:59
  79.9 6.2 %collective-permute-start.12 = (bf16[4,128,128]{2,1,0:T(8,128)(2,1)S(1)}, bf16[4,128,128]{2,1,0:T(8,128)(2,1)S(1)}, u32[]{:S(2)}, u32[]{:S(2)}) collective-permute-start(bf16[4,128,128]{2,1,0:T(8,128)(2,1)S(1)} %get-tuple-element.92), channel_id=1, source_target_pairs={{0,16},{8,24},{16,0},{24,8},{1,17},{9,25},{17,1},{25,9},{2,18},{10... | collective-permute-start | bytes 393224 | tf_op jit(solution)/shard_map/ppermute | solution.py:59
  80.5 5.9 %collective-permute-start.13 = (bf16[4,128,128]{2,1,0:T(8,128)(2,1)S(1)}, bf16[4,128,128]{2,1,0:T(8,128)(2,1)S(1)}, u32[]{:S(2)}, u32[]{:S(2)}) collective-permute-start(bf16[4,128,128]{2,1,0:T(8,128)(2,1)S(1)} %get-tuple-element.93), channel_id=1, source_target_pairs={{0,24},{8,16},{16,8},{24,0},{1,25},{9,17},{17,9},{25,1},{2,26},{10... | collective-permute-start | bytes 393224 | tf_op jit(solution)/shard_map/ppermute | solution.py:59
  82.1 13.9 %collective-permute-start.7 = (bf16[2,128,512]{2,1,0:T(8,128)(2,1)}, bf16[2,128,512]{2,1,0:T(8,128)(2,1)S(1)}, u32[]{:S(2)}, u32[]{:S(2)}) collective-permute-start(bf16[2,128,512]{2,1,0:T(8,128)(2,1)} %get-tuple-element.77), channel_id=1, source_target_pairs={{0,2},{1,3},{2,0},{3,1},{4,6},{5,7},{6,4},{7,5},{8,10},{9,11},{10,... | collective-permute-start | bytes 786440 | tf_op jit(solution)/shard_map/ppermute | solution.py:52
  83.6 12.4 %collective-permute-start.9 = (bf16[2,128,512]{2,1,0:T(8,128)(2,1)}, bf16[2,128,512]{2,1,0:T(8,128)(2,1)S(1)}, u32[]{:S(2)}, u32[]{:S(2)}) collective-permute-start(bf16[2,128,512]{2,1,0:T(8,128)(2,1)} %get-tuple-element.86), channel_id=1, source_target_pairs={{0,6},{1,7},{2,4},{3,5},{4,2},{5,3},{6,0},{7,1},{8,14},{9,15},{10,... | collective-permute-start | bytes 786440 | tf_op jit(solution)/shard_map/ppermute | solution.py:52
  88.5 19.0 %all-to-all-start.1 = ((f32[4,2,32,512]{3,2,1,0:T(8,128)}), f32[4,2,32,512]{3,2,1,0:T(8,128)S(1)}, u32[]{:S(2)}, u32[]{:S(2)}) async-start(f32[4,2,32,512]{3,2,1,0:T(8,128)} %get-tuple-element.105), calls=%async_computation.1 | async-start | bytes 1048576 | tf_op jit(solution)/shard_map/all_to_all | solution.py:65
  96.0 6.4 %collective-permute-start.14 = (bf16[2,2,128,128]{3,2,1,0:T(8,128)(2,1)S(1)}, bf16[2,2,128,128]{3,2,1,0:T(8,128)(2,1)S(1)}, u32[]{:S(2)}, u32[]{:S(2)}) collective-permute-start(bf16[2,2,128,128]{3,2,1,0:T(8,128)(2,1)S(1)} %get-tuple-element.102), channel_id=1, source_target_pairs={{0,2},{1,3},{2,0},{3,1},{4,6},{5,7},{6,4},{7,5},{8,10},{9,11},{10,... | collective-permute-start | bytes 393224 | tf_op jit(solution)/shard_map/ppermute | solution.py:52
  96.0 11.4 %collective-permute-start.15 = (bf16[2,2,128,128]{3,2,1,0:T(8,128)(2,1)S(1)}, bf16[2,2,128,128]{3,2,1,0:T(8,128)(2,1)S(1)}, u32[]{:S(2)}, u32[]{:S(2)}) collective-permute-start(bf16[2,2,128,128]{3,2,1,0:T(8,128)(2,1)S(1)} %get-tuple-element.103), channel_id=1, source_target_pairs={{0,4},{1,5},{2,6},{3,7},{4,0},{5,1},{6,2},{7,3},{8,12},{9,13},{10,... | collective-permute-start | bytes 393224 | tf_op jit(solution)/shard_map/ppermute | solution.py:52
  98.2 9.2 %collective-permute-start.16 = (bf16[2,2,128,128]{3,2,1,0:T(8,128)(2,1)S(1)}, bf16[2,2,128,128]{3,2,1,0:T(8,128)(2,1)S(1)}, u32[]{:S(2)}, u32[]{:S(2)}) collective-permute-start(bf16[2,2,128,128]{3,2,1,0:T(8,128)(2,1)S(1)} %get-tuple-element.104), channel_id=1, source_target_pairs={{0,6},{1,7},{2,4},{3,5},{4,2},{5,3},{6,0},{7,1},{8,14},{9,15},{10,... | collective-permute-start | bytes 393224 | tf_op jit(solution)/shard_map/ppermute | solution.py:52
  107.5 2.4 %collective-permute-start.18 = (bf16[4,128,512]{2,1,0:T(8,128)(2,1)S(1)}, bf16[4,128,512]{2,1,0:T(8,128)(2,1)S(1)}, u32[]{:S(2)}, u32[]{:S(2)}) collective-permute-start(bf16[4,128,512]{2,1,0:T(8,128)(2,1)S(1)} %shard_map.138), channel_id=1, source_target_pairs={{0,1},{1,0},{2,3},{3,2},{4,5},{5,4},{6,7},{7,6},{8,9},{9,8},{10,11... | collective-permute-start | bytes 1572872 | tf_op jit(solution)/shard_map/ppermute | solution.py:52
  107.6 2.2 %collective-permute-start.17 = (bf16[4,2,128,128]{3,2,1,0:T(8,128)(2,1)S(1)}, bf16[4,2,128,128]{3,2,1,0:T(8,128)(2,1)S(1)}, u32[]{:S(2)}, u32[]{:S(2)}) collective-permute-start(bf16[4,2,128,128]{3,2,1,0:T(8,128)(2,1)S(1)} %shard_map.137), channel_id=1, source_target_pairs={{0,1},{1,0},{2,3},{3,2},{4,5},{5,4},{6,7},{7,6},{8,9},{9,8},{10,11... | collective-permute-start | bytes 786440 | tf_op jit(solution)/shard_map/ppermute | solution.py:52
  (10 other events, 23.9 us)

commit v5 on v4

--- a/solution.py
+++ b/solution.py
@@ -20,7 +20,6 @@
 FAR = 1e30
 MAX_PERMUTES = 8
 VMEM_LIMIT = 24 * 1024 * 1024
-WIDE_LIMIT = 60 * 1024 * 1024
 NN = (((1,), (0,)), ((), ()))
 NT = (((1,), (1,)), ((), ()))
 SMEM_SPEC = pl.BlockSpec(memory_space=pltpu.SMEM)
@@ -45,7 +44,7 @@
 
 
 def staged(n):
-    return even(n) and n <= MAX_PERMUTES
+    return n == 8
 
 
 def swap(piece, k):
@@ -202,32 +201,33 @@
     take = lambda n: [refs.pop(0) for _ in range(n)]
     looped = len(js) > MAX_PERMUTES // 2
     qds = take(1 if looped else len(js))
-    pool, slots, stats, mk, mv = take(5)
-    if not first:
+    if first:
+        pool, slots, stats, mk, mv = take(5)
+    else:
+        slot_pool, mkt, stats, mk, mv = take(5)
         prev = take(3)
     dqs = take(1 if looped else len(js))
+    acc, dmk, dmv = take(3)
+    if first:
+        slot_pool, mkt = take(2)
     if last:
-        local, own_mem = take(2)
+        (own_mem,) = take(1)
         backs = take(lay.spans)
-        acc, dmk, dmv, slot_pool, mkt = take(5)
-    else:
-        acc, dmk, dmv = take(3)
-        slot_pool, mkt = take(2)
     heads = range(lay.heads)
     ways = lay.ways
     if first:
         for total in (acc, dmk, dmv):
             total[...] = jnp.zeros_like(total)
+        slot_pool[:ways] = pool[...]
+        for s in range(lay.spans):
+            slot_pool[ways + s, 0] = slots[s, 0]
+            slot_pool[ways + s, 1] = slots[s, 1]
+            slot_pool[ways + s, 2] = slots[s, 0].T
+        for h in heads:
+            mkt[h] = mk[:, col(h)].T
     else:
         for total, before in zip((acc, dmk, dmv), prev):
             total[...] = before[...]
-    slot_pool[:ways] = pool[...]
-    for s in range(lay.spans):
-        slot_pool[ways + s, 0] = slots[s, 0]
-        slot_pool[ways + s, 1] = slots[s, 1]
-        slot_pool[ways + s, 2] = slots[s, 0].T
-    for h in heads:
-        mkt[h] = mk[:, col(h)].T
 
     def one_block(k, qd, dq):
         index, far = lay.pairs(ctl, k)
@@ -287,7 +287,6 @@
                 one_block(2 * j + i, qd.at[i], dq.at[i])
 
     if last:
-        local[...] = acc[:ways]
         for k, back in enumerate(backs):
             span = partner(ctl[1], k, lay.spans)
             back[0] = (acc[ways + span, 0] * SCALE).astype(jnp.bfloat16)
@@ -304,55 +303,49 @@
         own_mem[1] = dmv[rows, :]
 
 
-def attention(lay, js, ctl, qds, pool, slots, stats, mk, mv, before, last):
+def attention(lay, js, ctl, qds, pools, stats, mk, mv, before, last):
     blocks = lay.ways + lay.spans
+    pieces = [qds[j] for j in js]
+    dq = [array((2, BLOCK, lay.width))] * len(js)
+    if len(js) > MAX_PERMUTES // 2:
+        pieces = [jnp.stack(pieces)]
+        dq = [array((len(js), 2, BLOCK, lay.width))]
     totals = [
         array((blocks, 2, BLOCK, HEAD_FEATURES), jnp.float32),
         array((BLOCK, lay.width), jnp.float32),
         array((BLOCK, lay.width), jnp.float32),
     ]
-    scratch = [
-        pltpu.VMEM((blocks, 3, BLOCK, HEAD_FEATURES), jnp.bfloat16),
-        pltpu.VMEM((lay.heads, BLOCK, HEAD_FEATURES), jnp.bfloat16),
+    whole = [
+        array((blocks, 3, BLOCK, HEAD_FEATURES)),
+        array((lay.heads, BLOCK, HEAD_FEATURES)),
     ]
-    pieces = [qds[j] for j in js]
-    outs = [array((2, BLOCK, lay.width))] * len(js)
-    looped = len(js) > MAX_PERMUTES // 2
-    if looped:
-        pieces = [jnp.stack(pieces)]
-        outs = [array((len(js), 2, BLOCK, lay.width))]
-    if last:
-        outs += [
-            array((lay.ways, 2, BLOCK, HEAD_FEATURES), jnp.float32),
-            array((2, lay.mem_rows or BLOCK, lay.width), jnp.float32),
-        ]
-        outs += [array((4 if lay.mem_rows else 2, BLOCK, HEAD_FEATURES))] * lay.spans
-        scratch = [pltpu.VMEM(t.shape, t.dtype) for t in totals] + scratch
-    else:
-        outs += totals
+    sent = [array((2, lay.mem_rows or BLOCK, lay.width), jnp.float32)]
+    sent += [array((4 if lay.mem_rows else 2, BLOCK, HEAD_FEATURES))] * lay.spans
+    first = before is None
     done = call(
-        functools.partial(attention_kernel, lay, js, before is None, last),
-        outs,
+        functools.partial(attention_kernel, lay, js, first, last),
+        dq + totals + (whole if first else []) + (sent if last else []),
         ctl,
         *pieces,
-        pool,
-        slots,
+        *pools,
         stats,
         mk,
         mv,
         *(before or []),
-        scratch=scratch,
     )
-    dq = done[0] if looped else done[: len(js)]
-    return dict(zip(js, dq)), done[1 if looped else len(js) :]
-
-
-def merge_kernel(lay, ctl, local, own_mem, *refs):
+    dq, done = done[: len(dq)], done[len(dq) :]
+    totals, done = done[:3], done[3:]
+    if first:
+        pools, done = done[:2], done[2:]
+    return dict(zip(js, dq if len(dq) == len(js) else dq[0])), totals, pools, done
+
+
+def merge_kernel(lay, ctl, acc, own_mem, *refs):
     backs = refs[: lay.spans]
     *pieces, mem_sum, total = refs[lay.spans :]
     for k in range(lay.ways):
-        total[k, 0] = local[k, 0] * SCALE
-        total[k, 1] = local[k, 1]
+        total[k, 0] = acc[k, 0] * SCALE
+        total[k, 1] = acc[k, 1]
     mem = [own_mem[0], own_mem[1]]
     for k, back in enumerate(backs):
         span = partner(ctl[1], k, lay.spans)
@@ -422,20 +415,19 @@
     ctl = jnp.concatenate([place, pattern.reshape(-1)])
 
     qd = by_chip(lambda device: device, place, queries, grad_out, lay.width)
-    late = place
-    kv = by_chip(lay.key_head, late, keys, values, HEAD_FEATURES)
+    kv = by_chip(lay.key_head, place, keys, values, HEAD_FEATURES)
     steps = [range(chips)]
     if in_stages:
         half = max(1, chips // 2)
-        steps = [range(half), *([j] for j in range(half, chips))]
-        for j in [*range(half, chips), *range(1, half)]:
+        far, last_far = 3, 2
+        steps = [range(half), [far], [last_far]]
+        for j in [far, last_far, 1]:
             kv[j] = swap(kv[j], 2 * j)
-        qd[half] = swap(qd[half], 2 * half)
+        qd[far] = swap(qd[far], 2 * far)
         qd[1] = swap(qd[1], 2)
-        kv[1:], qd[half + 1] = after(kv[1:], qd[half + 1])
-        qd[half + 1] = swap(qd[half + 1], 2 * half + 2)
-        first = (qd[1], qd[half])
-        (qd[1], qd[half]), kv[0] = after(first, kv[0])
+        kv[1:], qd[last_far] = after(kv[1:], qd[last_far])
+        qd[last_far] = swap(qd[last_far], 2 * last_far)
+        (qd[1], qd[far]), kv[0] = after((qd[1], qd[far]), kv[0])
     pool, slots = call(
         functools.partial(pool_kernel, lay),
         [
@@ -449,25 +441,25 @@
     stats = jnp.concatenate([row_lse, row_delta], axis=1)
     stats = stats.reshape(lay.ways, BLOCK, 2 * lay.heads).transpose(0, 2, 1)
 
-    totals, dq = None, {}
+    totals, pools, dq = None, (pool, slots), {}
     for step in steps:
         last = step is steps[-1]
-        step_dq, totals = attention(
-            lay, step, ctl, qd, pool, slots, stats, memory_keys, memory_values, totals, last
+        step_dq, totals, pools, sent = attention(
+            lay, step, ctl, qd, pools, stats, memory_keys, memory_values, totals, last
         )
         dq |= step_dq
-    local, own_mem, *backs = totals
+    own_mem, *backs = sent
     backs = across_spans(backs)
     if in_stages:
-        for j in [*range(half, chips), *range(1, half)]:
+        for j in [far, last_far, 1]:
             dq[j] = swap(dq[j], 2 * j)
-        dq[half], backs = after(dq[half], backs)
+        dq[far], backs = after(dq[far], backs)
     *dkv, mem = call(
         functools.partial(merge_kernel, lay),
         [array((2, 2, BLOCK, HEAD_FEATURES))] * chips
         + [array((lay.spans if lay.mem_rows else 1, *own_mem.shape), jnp.float32)],
         ctl,
-        local,
+        totals[0],
         own_mem,
         *backs,
         scratch=[pltpu.VMEM((lay.ways, 2, BLOCK, HEAD_FEATURES), jnp.float32)],
@@ -475,8 +467,8 @@
     mem = to_spans(mem) if lay.mem_rows else lax.psum(mem, "blk")
     dq = [dq[j] for j in range(chips)]
     if in_stages:
-        (dq[1], dq[half + 1]), dkv = after((dq[1], dq[half + 1]), dkv)
-        for j in [*range(half, chips), *range(1, half)]:
+        (dq[1], dq[last_far]), dkv = after((dq[1], dq[last_far]), dkv)
+        for j in [far, last_far, 1]:
             dkv[j] = swap(dkv[j], 2 * j)
         (dkv[1:], mem), dq = after((dkv[1:], mem), dq)
         dq.append(to_blocks(dq))
@@ -484,14 +476,10 @@
     else:
         dq = whole_exchange(dq)
         dkv = whole_exchange(dkv)
-    return tuple(call(
-        functools.partial(finish_kernel, lay),
-        [array(queries.shape)] + [array(keys.shape, jnp.float32)] * 2 + [array(memory_keys.shape, jnp.float32)] * 2,
-        place,
-        mem,
-        *dkv,
-        *dq,
-    ))
+    outs = [queries.shape, keys.shape, keys.shape, memory_keys.shape, memory_keys.shape]
+    kinds = [jnp.bfloat16] + [jnp.float32] * 4
+    outs = [array(shape, kind) for shape, kind in zip(outs, kinds)]
+    return tuple(call(functools.partial(finish_kernel, lay), outs, place, mem, *dkv, *dq))
 
 
 def solution(mesh):

time: 113 us -> 112 us (level)
    ppermute x3, waiting for transfers between devices: 1.07 us -> 2.43 us  [across_spans(): lax.ppermute(pieces[k], 'blk', pairs[k])]
    ppermute x16, waiting for transfers between devices: 41.7 us -> 40.4 us  [swap(): lax.ppermute(piece, 'uly', [(i, i ^ k) for i in range(lax.axis_size('uly'...]
    unnamed x27 -> x33, local copies, waits for them, and re-layouts: 6 us -> 6.87 us
  transfers between devices with their start and end apart: 21 -> 21, of which waited for: 10 -> 10; matrix products, arithmetic and copies ran while one was open for 1% -> 0% of each run, Pallas kernels for 18% -> 18%
where the time goes in v5:
time: 112 us
  waiting for transfers between devices  48.2 us (43%)
  starting transfers between devices  32.6 us (29%)
  Pallas kernels  23.2 us (21%)
  local copies, waits for them, and re-layouts  6.97 us (6%)
    ppermute x16, waiting for transfers between devices, swap(): lax.ppermute(piece, 'uly', [(i, i ^ k) for i in range(lax.axis_size('uly'...  40.4 us
    pallas_call x12, Pallas kernels, call(): pl.pallas_call(kernel, in_specs=[SMEM_SPEC] + [pl.BlockSpec(memory_space=...  23.2 us
    ppermute x16, starting transfers between devices, swap(): lax.ppermute(piece, 'uly', [(i, i ^ k) for i in range(lax.axis_size('uly'...  21.9 us
    all_to_all x2, starting transfers between devices, to_spans(): return lax.all_to_all(stacked, 'blk', 0, 0, tiled=True)  7.19 us
    unnamed x33, local copies, waits for them, and re-layouts  6.87 us
    all_to_all x2, waiting for transfers between devices, to_spans(): return lax.all_to_all(stacked, 'blk', 0, 0, tiled=True)  5.35 us
    ppermute x3, starting transfers between devices, across_spans(): lax.ppermute(pieces[k], 'blk', pairs[k])  3.49 us
    ppermute x3, waiting for transfers between devices, across_spans(): lax.ppermute(pieces[k], 'blk', pairs[k])  2.43 us
  transfers between devices with their start and end apart: 21, of which 10 were waited for; matrix products, arithmetic and copies ran while one was open for 0% of the time, Pallas kernels for 18%

profile of v5, /device:TPU:0, one launch (start us, length us, event | category | flops | bytes accessed | tf_op | source)
XLA Modules:
  0.0 111.9 jit_solution(6169646924881676554)
XLA Ops:
  6.6 1.7 %shard_map.129 = (bf16[2,2,128,512]{3,2,1,0:T(8,128)(2,1)S(1)}, bf16[2,2,128,512]{3,2,1,0:T(8,128)(2,1)}, bf16[2,2,128,512]{3,2,1,0:T(8,128)(2,1)}, bf16[2,2,128,512]{3,2,1,0:T(8,128)(2,1)S(1)}) custom-call(s32[2]{0:T(128)S(1)} %pad_add_fusion.ctl, bf16[128,4096]{1,0:T(8,128)(2,1)S(1)} %copy-done.1, bf16[128,4096]{1,0:T(8,128)(2,1)S(1)} %copy-done.2, ...), custom_call_target="tpu_custom_call" | custom-call | tf_op jit(solution)/shard_map/pallas_call | solution.py:73
  8.3 3.0 %collective-permute-start.1 = (bf16[2,2,128,512]{3,2,1,0:T(8,128)(2,1)}, bf16[2,2,128,512]{3,2,1,0:T(8,128)(2,1)S(1)}, u32[]{:S(2)}, u32[]{:S(2)}) collective-permute-start(bf16[2,2,128,512]{3,2,1,0:T(8,128)(2,1)} %get-tuple-element.65), channel_id=1, source_target_pairs={{0,2},{1,3},{2,0},{3,1},{4,6},{5,7},{6,4},{7,5},{8,10},{9,11},{10,... | collective-permute-start | bytes 1572872 | tf_op jit(solution)/shard_map/ppermute | solution.py:51
  11.3 2.5 %collective-permute-start.2 = (bf16[2,2,128,512]{3,2,1,0:T(8,128)(2,1)S(1)}, bf16[2,2,128,512]{3,2,1,0:T(8,128)(2,1)S(1)}, u32[]{:S(2)}, u32[]{:S(2)}) collective-permute-start(bf16[2,2,128,512]{3,2,1,0:T(8,128)(2,1)S(1)} %get-tuple-element.66), channel_id=1, source_target_pairs={{0,6},{1,7},{2,4},{3,5},{4,2},{5,3},{6,0},{7,1},{8,14},{9,15},{10,... | collective-permute-start | bytes 1572872 | tf_op jit(solution)/shard_map/ppermute | solution.py:51
  16.4 2.5 %collective-permute-start.6 = (bf16[2,2,128,128]{3,2,1,0:T(8,128)(2,1)S(1)}, bf16[2,2,128,128]{3,2,1,0:T(8,128)(2,1)S(1)}, u32[]{:S(2)}, u32[]{:S(2)}) collective-permute-start(bf16[2,2,128,128]{3,2,1,0:T(8,128)(2,1)S(1)} %get-tuple-element.72), channel_id=1, source_target_pairs={{0,6},{1,7},{2,4},{3,5},{4,2},{5,3},{6,0},{7,1},{8,14},{9,15},{10,... | collective-permute-start | bytes 393224 | tf_op jit(solution)/shard_map/ppermute | solution.py:51
  18.8 21.2 %collective-permute-done.4.refs_1_ = bf16[2,2,128,128]{3,2,1,0:T(8,128)(2,1)S(1)} collective-permute-done((bf16[2,2,128,128]{3,2,1,0:T(8,128)(2,1)S(1)}, bf16[2,2,128,128]{3,2,1,0:T(8,128)(2,1)S(1)}, u32[]{:S(2)}, u32[]{:S(2)}) %collective-permute-start.4) | collective-permute-done | bytes 131104 | tf_op jit(solution)/shard_map/ppermute | solution.py:51
  40.1 6.2 %collective-permute-done.5.refs_2_ = bf16[2,2,128,128]{3,2,1,0:T(8,128)(2,1)S(1)} collective-permute-done((bf16[2,2,128,128]{3,2,1,0:T(8,128)(2,1)S(1)}, bf16[2,2,128,128]{3,2,1,0:T(8,128)(2,1)S(1)}, u32[]{:S(2)}, u32[]{:S(2)}) %collective-permute-start.5) | collective-permute-done | bytes 131104 | tf_op jit(solution)/shard_map/ppermute | solution.py:51
  47.6 3.1 %collective-permute-start.8 = (bf16[2,2,128,512]{3,2,1,0:T(8,128)(2,1)}, bf16[2,2,128,512]{3,2,1,0:T(8,128)(2,1)S(1)}, u32[]{:S(2)}, u32[]{:S(2)}) collective-permute-start(bf16[2,2,128,512]{3,2,1,0:T(8,128)(2,1)} %get-tuple-element.80), channel_id=1, source_target_pairs={{0,4},{1,5},{2,6},{3,7},{4,0},{5,1},{6,2},{7,3},{8,12},{9,13},{10,... | collective-permute-start | bytes 1572872 | tf_op jit(solution)/shard_map/ppermute | solution.py:51
  52.9 2.0 %shard_map.132 = (bf16[8,3,128,128]{3,2,1,0:T(8,128)(2,1)S(1)}, bf16[4,2,128,128]{3,2,1,0:T(8,128)(2,1)}) custom-call(s32[66]{0:T(128)S(1)} %pad_add_fusion.1.ctl, bf16[2,2,128,128]{3,2,1,0:T(8,128)(2,1)S(1)} %get-tuple-element.69.refs_0_, bf16[2,2,128,128]{3,2,1,0:T(8,128)(2,1)S(1)} %collective-permute-done.4.refs_1_, ...), custom_call_target="tpu_custom_call" | custom-call | tf_op jit(solution)/shard_map/pallas_call | solution.py:73
  55.0 3.7 %all-to-all-start = ((bf16[4,2,128,128]{3,2,1,0:T(8,128)(2,1)}), bf16[4,2,128,128]{3,2,1,0:T(8,128)(2,1)S(1)}, u32[]{:S(2)}, u32[]{:S(2)}) async-start(bf16[4,2,128,128]{3,2,1,0:T(8,128)(2,1)} %get-tuple-element.78), calls=%async_computation | async-start | bytes 524288 | tf_op jit(solution)/shard_map/all_to_all | solution.py:64
  58.7 5.4 %all-to-all-done.refs_3_ = bf16[4,2,128,128]{3,2,1,0:T(8,128)(2,1)S(1)} async-done(((bf16[4,2,128,128]{3,2,1,0:T(8,128)(2,1)}), bf16[4,2,128,128]{3,2,1,0:T(8,128)(2,1)S(1)}, u32[]{:S(2)}, u32[]{:S(2)}) %all-to-all-start) | async-done | bytes 262176 | tf_op jit(solution)/shard_map/all_to_all | solution.py:64
  65.1 5.8 %shard_map.133 = (bf16[2,128,512]{2,1,0:T(8,128)(2,1)S(1)}, bf16[2,128,512]{2,1,0:T(8,128)(2,1)S(1)}, f32[12,2,128,128]{3,2,1,0:T(8,128)S(1)}, f32[128,512]{1,0:...) custom-call(s32[66]{0:T(128)S(1)} %pad_add_fusion.1.ctl, ...), custom_call_target="tpu_custom_call" | custom-call | tf_op jit(solution)/shard_map/pallas_call | solution.py:73
  71.0 3.3 %shard_map.134 = (bf16[2,128,512]{2,1,0:T(8,128)(2,1)S(1)}, f32[12,2,128,128]{3,2,1,0:T(8,128)S(1)}, f32[128,512]{1,0:T(8,128)S(1)}, f32[128,512]{1,0:T(8,128)S(1)}) custom-call(s32[66]{0:T(128)S(1)} %pad_add_fusion.1.ctl, bf16[2,2,128,512]{3,2,1,0:T(8,128)(2,1)S(1)} %collective-permute-done.2.refs_0_, ...), custom_call_target="tpu_custom_call" | custom-call | tf_op jit(solution)/shard_map/pallas_call | solution.py:73
  75.5 4.1 %shard_map.135 = (bf16[2,128,512]{2,1,0:T(8,128)(2,1)S(1)}, f32[12,2,128,128]{3,2,1,0:T(8,128)S(1)}, f32[128,512]{1,0:T(8,128)}, f32[128,512]{1,0:T(8,128)}, f32...) custom-call(s32[66]{0:T(128)S(1)} %pad_add_fusion.1.ctl, ...), custom_call_target="tpu_custom_call" | custom-call | tf_op jit(solution)/shard_map/pallas_call | solution.py:73
  81.4 1.7 %collective-permute-start.13 = (bf16[4,128,128]{2,1,0:T(8,128)(2,1)S(1)}, bf16[4,128,128]{2,1,0:T(8,128)(2,1)S(1)}, u32[]{:S(2)}, u32[]{:S(2)}) collective-permute-start(bf16[4,128,128]{2,1,0:T(8,128)(2,1)S(1)} %get-tuple-element.97), channel_id=1, source_target_pairs={{0,24},{8,16},{16,8},{24,0},{1,25},{9,17},{17,9},{25,1},{2,26},{10... | collective-permute-start | bytes 393224 | tf_op jit(solution)/shard_map/ppermute | solution.py:58
  84.5 1.8 %collective-permute-start.9 = (bf16[2,128,512]{2,1,0:T(8,128)(2,1)S(1)}, bf16[2,128,512]{2,1,0:T(8,128)(2,1)S(1)}, u32[]{:S(2)}, u32[]{:S(2)}) collective-permute-start(bf16[2,128,512]{2,1,0:T(8,128)(2,1)S(1)} %get-tuple-element.90), channel_id=1, source_target_pairs={{0,4},{1,5},{2,6},{3,7},{4,0},{5,1},{6,2},{7,3},{8,12},{9,13},{10,... | collective-permute-start | bytes 786440 | tf_op jit(solution)/shard_map/ppermute | solution.py:51
  87.3 2.1 %shard_map.136 = (bf16[2,2,128,128]{3,2,1,0:T(8,128)(2,1)S(1)}, bf16[2,2,128,128]{3,2,1,0:T(8,128)(2,1)S(1)}, bf16[2,2,128,128]{3,2,1,0:T(8,128)(2,1)S(1)}, bf16...) custom-call(s32[66]{0:T(128)S(1)} %pad_add_fusion.1.ctl, f32[12,2,128,128]{3,2,1,0:T(8,128)S(1)} %get-tuple-element.91.acc, ...), custom_call_target="tpu_custom_call" | custom-call | tf_op jit(solution)/shard_map/pallas_call | solution.py:73
  89.4 3.5 %all-to-all-start.1 = ((f32[4,2,32,512]{3,2,1,0:T(8,128)}), f32[4,2,32,512]{3,2,1,0:T(8,128)S(1)}, u32[]{:S(2)}, u32[]{:S(2)}) async-start(f32[4,2,32,512]{3,2,1,0:T(8,128)} %get-tuple-element.109), calls=%async_computation.1 | async-start | bytes 1048576 | tf_op jit(solution)/shard_map/all_to_all | solution.py:64
  92.8 3.1 %collective-permute-done.9.refs_2_.refs_7_ = bf16[2,128,512]{2,1,0:T(8,128)(2,1)S(1)} collective-permute-done((bf16[2,128,512]{2,1,0:T(8,128)(2,1)S(1)}, bf16[2,128,512]{2,1,0:T(8,128)(2,1)S(1)}, u32[]{:S(2)}, u32[]{:S(2)}) %collective-permute-start.9) | collective-permute-done | bytes 262176 | tf_op jit(solution)/shard_map/ppermute | solution.py:51
  96.0 2.8 %collective-permute-start.15 = (bf16[2,2,128,128]{3,2,1,0:T(8,128)(2,1)S(1)}, bf16[2,2,128,128]{3,2,1,0:T(8,128)(2,1)S(1)}, u32[]{:S(2)}, u32[]{:S(2)}) collective-permute-start(bf16[2,2,128,128]{3,2,1,0:T(8,128)(2,1)S(1)} %get-tuple-element.107), channel_id=1, source_target_pairs={{0,4},{1,5},{2,6},{3,7},{4,0},{5,1},{6,2},{7,3},{8,12},{9,13},{10,... | collective-permute-start | bytes 393224 | tf_op jit(solution)/shard_map/ppermute | solution.py:51
  98.8 1.6 %collective-permute-start.16 = (bf16[2,2,128,128]{3,2,1,0:T(8,128)(2,1)S(1)}, bf16[2,2,128,128]{3,2,1,0:T(8,128)(2,1)S(1)}, u32[]{:S(2)}, u32[]{:S(2)}) collective-permute-start(bf16[2,2,128,128]{3,2,1,0:T(8,128)(2,1)S(1)} %get-tuple-element.108), channel_id=1, source_target_pairs={{0,6},{1,7},{2,4},{3,5},{4,2},{5,3},{6,0},{7,1},{8,14},{9,15},{10,... | collective-permute-start | bytes 393224 | tf_op jit(solution)/shard_map/ppermute | solution.py:51
  100.4 2.1 %collective-permute-done.14.refs_1_ = bf16[2,2,128,128]{3,2,1,0:T(8,128)(2,1)S(1)} collective-permute-done((bf16[2,2,128,128]{3,2,1,0:T(8,128)(2,1)S(1)}, bf16[2,2,128,128]{3,2,1,0:T(8,128)(2,1)S(1)}, u32[]{:S(2)}, u32[]{:S(2)}) %collective-permute-start.14) | collective-permute-done | bytes 131104 | tf_op jit(solution)/shard_map/ppermute | solution.py:51
  102.5 4.8 %collective-permute-done.15.refs_2_ = bf16[2,2,128,128]{3,2,1,0:T(8,128)(2,1)S(1)} collective-permute-done((bf16[2,2,128,128]{3,2,1,0:T(8,128)(2,1)S(1)}, bf16[2,2,128,128]{3,2,1,0:T(8,128)(2,1)S(1)}, u32[]{:S(2)}, u32[]{:S(2)}) %collective-permute-start.15) | collective-permute-done | bytes 131104 | tf_op jit(solution)/shard_map/ppermute | solution.py:51
  108.0 1.7 %collective-permute-done.17.refs_4_ = bf16[4,2,128,128]{3,2,1,0:T(8,128)(2,1)S(1)} collective-permute-done((bf16[4,2,128,128]{3,2,1,0:T(8,128)(2,1)S(1)}, bf16[4,2,128,128]{3,2,1,0:T(8,128)(2,1)S(1)}, u32[]{:S(2)}, u32[]{:S(2)}) %collective-permute-start.17) | collective-permute-done | bytes 262176 | tf_op jit(solution)/shard_map/ppermute | solution.py:51
  109.7 2.2 %shard_map.139 = (bf16[128,4096]{1,0:T(8,128)(2,1)}, f32[128,1024]{1,0:T(8,128)}, f32[128,1024]{1,0:T(8,128)}, f32[128,512]{1,0:T(8,128)}, f32[128,512]{1,0:T(8,128)}) custom-call(s32[2]{0:T(128)S(1)} %pad_add_fusion.ctl, f32[4,2,32,512]{3,2,1,0:T(8,128)S(1)} %all-to-all-done.1.mem, bf16[2,2,128,128]{3,2,1,0:T(8,128)(2,1)S(1)} %get-tuple-element.115.refs_0_, ...), custom_call_target="tpu_custom_call" | custom-call | tf_op jit(solution)/shard_map/pallas_call | solution.py:73
  (67 shorter events, 19.3 us)
Async XLA Ops:
  3.8 2.8 %collective-permute-start = (bf16[4,2,128,512]{3,2,1,0:T(8,128)(2,1)S(1)}, bf16[4,2,128,512]{3,2,1,0:T(8,128)(2,1)S(1)}, u32[]{:S(2)}, u32[]{:S(2)}) collective-permute-start(bf16[4,2,128,512]{3,2,1,0:T(8,128)(2,1)S(1)} %shard_map.128), channel_id=1, source_target_pairs={{0,1},{1,0},{2,3},{3,2},{4,5},{5,4},{6,7},{7,6},{8,9},{9,8},{10,11... | collective-permute-start | bytes 3145736 | tf_op jit(solution)/shard_map/ppermute | solution.py:51
  5.0 8.8 %collective-permute-start.3 = (bf16[4,2,128,128]{3,2,1,0:T(8,128)(2,1)S(1)}, bf16[4,2,128,128]{3,2,1,0:T(8,128)(2,1)S(1)}, u32[]{:S(2)}, u32[]{:S(2)}) collective-permute-start(bf16[4,2,128,128]{3,2,1,0:T(8,128)(2,1)S(1)} %shard_map.130), channel_id=1, source_target_pairs={{0,1},{1,0},{2,3},{3,2},{4,5},{5,4},{6,7},{7,6},{8,9},{9,8},{10,11... | collective-permute-start | bytes 786440 | tf_op jit(solution)/shard_map/ppermute | solution.py:51
  8.3 50.4 %copy-start.14 = (f32[1024,4]{0,1:T(4,128)S(1)}, f32[1024,4]{0,1:T(4,128)}, u32[]{:S(2)}) copy-start(f32[1024,4]{0,1:T(4,128)} %param.13) | copy-start | bytes 49156
  8.3 55.8 %copy-start.3 = (bf16[128,512]{1,0:T(8,128)(2,1)S(1)}, bf16[128,512]{1,0:T(8,128)(2,1)}, u32[]{:S(2)}) copy-start(bf16[128,512]{1,0:T(8,128)(2,1)} %refs_4_.3) | copy-start | bytes 393220
  8.3 55.8 %copy-start.4 = (bf16[128,512]{1,0:T(8,128)(2,1)S(1)}, bf16[128,512]{1,0:T(8,128)(2,1)}, u32[]{:S(2)}) copy-start(bf16[128,512]{1,0:T(8,128)(2,1)} %refs_5_.5) | copy-start | bytes 393220
  8.3 42.7 %collective-permute-start.1 = (bf16[2,2,128,512]{3,2,1,0:T(8,128)(2,1)}, bf16[2,2,128,512]{3,2,1,0:T(8,128)(2,1)S(1)}, u32[]{:S(2)}, u32[]{:S(2)}) collective-permute-start(bf16[2,2,128,512]{3,2,1,0:T(8,128)(2,1)} %get-tuple-element.65), channel_id=1, source_target_pairs={{0,2},{1,3},{2,0},{3,1},{4,6},{5,7},{6,4},{7,5},{8,10},{9,11},{10,... | collective-permute-start | bytes 1572872 | tf_op jit(solution)/shard_map/ppermute | solution.py:51
  11.3 39.7 %collective-permute-start.2 = (bf16[2,2,128,512]{3,2,1,0:T(8,128)(2,1)S(1)}, bf16[2,2,128,512]{3,2,1,0:T(8,128)(2,1)S(1)}, u32[]{:S(2)}, u32[]{:S(2)}) collective-permute-start(bf16[2,2,128,512]{3,2,1,0:T(8,128)(2,1)S(1)} %get-tuple-element.66), channel_id=1, source_target_pairs={{0,6},{1,7},{2,4},{3,5},{4,2},{5,3},{6,0},{7,1},{8,14},{9,15},{10,... | collective-permute-start | bytes 1572872 | tf_op jit(solution)/shard_map/ppermute | solution.py:51
  14.4 25.7 %collective-permute-start.4 = (bf16[2,2,128,128]{3,2,1,0:T(8,128)(2,1)S(1)}, bf16[2,2,128,128]{3,2,1,0:T(8,128)(2,1)S(1)}, u32[]{:S(2)}, u32[]{:S(2)}) collective-permute-start(bf16[2,2,128,128]{3,2,1,0:T(8,128)(2,1)S(1)} %get-tuple-element.70), channel_id=1, source_target_pairs={{0,2},{1,3},{2,0},{3,1},{4,6},{5,7},{6,4},{7,5},{8,10},{9,11},{10,... | collective-permute-start | bytes 393224 | tf_op jit(solution)/shard_map/ppermute | solution.py:51
  15.1 31.1 %collective-permute-start.5 = (bf16[2,2,128,128]{3,2,1,0:T(8,128)(2,1)S(1)}, bf16[2,2,128,128]{3,2,1,0:T(8,128)(2,1)S(1)}, u32[]{:S(2)}, u32[]{:S(2)}) collective-permute-start(bf16[2,2,128,128]{3,2,1,0:T(8,128)(2,1)S(1)} %get-tuple-element.71), channel_id=1, source_target_pairs={{0,4},{1,5},{2,6},{3,7},{4,0},{5,1},{6,2},{7,3},{8,12},{9,13},{10,... | collective-permute-start | bytes 393224 | tf_op jit(solution)/shard_map/ppermute | solution.py:51
  16.4 30.6 %collective-permute-start.6 = (bf16[2,2,128,128]{3,2,1,0:T(8,128)(2,1)S(1)}, bf16[2,2,128,128]{3,2,1,0:T(8,128)(2,1)S(1)}, u32[]{:S(2)}, u32[]{:S(2)}) collective-permute-start(bf16[2,2,128,128]{3,2,1,0:T(8,128)(2,1)S(1)} %get-tuple-element.72), channel_id=1, source_target_pairs={{0,6},{1,7},{2,4},{3,5},{4,2},{5,3},{6,0},{7,1},{8,14},{9,15},{10,... | collective-permute-start | bytes 393224 | tf_op jit(solution)/shard_map/ppermute | solution.py:51
  47.6 27.9 %collective-permute-start.8 = (bf16[2,2,128,512]{3,2,1,0:T(8,128)(2,1)}, bf16[2,2,128,512]{3,2,1,0:T(8,128)(2,1)S(1)}, u32[]{:S(2)}, u32[]{:S(2)}) collective-permute-start(bf16[2,2,128,512]{3,2,1,0:T(8,128)(2,1)} %get-tuple-element.80), channel_id=1, source_target_pairs={{0,4},{1,5},{2,6},{3,7},{4,0},{5,1},{6,2},{7,3},{8,12},{9,13},{10,... | collective-permute-start | bytes 1572872 | tf_op jit(solution)/shard_map/ppermute | solution.py:51
  55.0 9.1 %all-to-all-start = ((bf16[4,2,128,128]{3,2,1,0:T(8,128)(2,1)}), bf16[4,2,128,128]{3,2,1,0:T(8,128)(2,1)S(1)}, u32[]{:S(2)}, u32[]{:S(2)}) async-start(bf16[4,2,128,128]{3,2,1,0:T(8,128)(2,1)} %get-tuple-element.78), calls=%async_computation | async-start | bytes 524288 | tf_op jit(solution)/shard_map/all_to_all | solution.py:64
  74.3 13.0 %collective-permute-start.10 = (bf16[2,128,512]{2,1,0:T(8,128)(2,1)S(1)}, bf16[2,128,512]{2,1,0:T(8,128)(2,1)S(1)}, u32[]{:S(2)}, u32[]{:S(2)}) collective-permute-start(bf16[2,128,512]{2,1,0:T(8,128)(2,1)S(1)} %get-tuple-element.93), channel_id=1, source_target_pairs={{0,6},{1,7},{2,4},{3,5},{4,2},{5,3},{6,0},{7,1},{8,14},{9,15},{10,... | collective-permute-start | bytes 786440 | tf_op jit(solution)/shard_map/ppermute | solution.py:51
  79.6 5.0 %collective-permute-start.11 = (bf16[4,128,128]{2,1,0:T(8,128)(2,1)S(1)}, bf16[4,128,128]{2,1,0:T(8,128)(2,1)S(1)}, u32[]{:S(2)}, u32[]{:S(2)}) collective-permute-start(bf16[4,128,128]{2,1,0:T(8,128)(2,1)S(1)} %get-tuple-element.95), channel_id=1, source_target_pairs={{0,8},{8,0},{16,24},{24,16},{1,9},{9,1},{17,25},{25,17},{2,10},{10... | collective-permute-start | bytes 393224 | tf_op jit(solution)/shard_map/ppermute | solution.py:58
  80.8 5.5 %collective-permute-start.12 = (bf16[4,128,128]{2,1,0:T(8,128)(2,1)S(1)}, bf16[4,128,128]{2,1,0:T(8,128)(2,1)S(1)}, u32[]{:S(2)}, u32[]{:S(2)}) collective-permute-start(bf16[4,128,128]{2,1,0:T(8,128)(2,1)S(1)} %get-tuple-element.96), channel_id=1, source_target_pairs={{0,16},{8,24},{16,0},{24,8},{1,17},{9,25},{17,1},{25,9},{2,18},{10... | collective-permute-start | bytes 393224 | tf_op jit(solution)/shard_map/ppermute | solution.py:58
  81.4 5.9 %collective-permute-start.13 = (bf16[4,128,128]{2,1,0:T(8,128)(2,1)S(1)}, bf16[4,128,128]{2,1,0:T(8,128)(2,1)S(1)}, u32[]{:S(2)}, u32[]{:S(2)}) collective-permute-start(bf16[4,128,128]{2,1,0:T(8,128)(2,1)S(1)} %get-tuple-element.97), channel_id=1, source_target_pairs={{0,24},{8,16},{16,8},{24,0},{1,25},{9,17},{17,9},{25,1},{2,26},{10... | collective-permute-start | bytes 393224 | tf_op jit(solution)/shard_map/ppermute | solution.py:58
  83.0 9.8 %collective-permute-start.7 = (bf16[2,128,512]{2,1,0:T(8,128)(2,1)S(1)}, bf16[2,128,512]{2,1,0:T(8,128)(2,1)S(1)}, u32[]{:S(2)}, u32[]{:S(2)}) collective-permute-start(bf16[2,128,512]{2,1,0:T(8,128)(2,1)S(1)} %get-tuple-element.79), channel_id=1, source_target_pairs={{0,2},{1,3},{2,0},{3,1},{4,6},{5,7},{6,4},{7,5},{8,10},{9,11},{10,... | collective-permute-start | bytes 786440 | tf_op jit(solution)/shard_map/ppermute | solution.py:51
  84.5 11.4 %collective-permute-start.9 = (bf16[2,128,512]{2,1,0:T(8,128)(2,1)S(1)}, bf16[2,128,512]{2,1,0:T(8,128)(2,1)S(1)}, u32[]{:S(2)}, u32[]{:S(2)}) collective-permute-start(bf16[2,128,512]{2,1,0:T(8,128)(2,1)S(1)} %get-tuple-element.90), channel_id=1, source_target_pairs={{0,4},{1,5},{2,6},{3,7},{4,0},{5,1},{6,2},{7,3},{8,12},{9,13},{10,... | collective-permute-start | bytes 786440 | tf_op jit(solution)/shard_map/ppermute | solution.py:51
  89.4 17.9 %all-to-all-start.1 = ((f32[4,2,32,512]{3,2,1,0:T(8,128)}), f32[4,2,32,512]{3,2,1,0:T(8,128)S(1)}, u32[]{:S(2)}, u32[]{:S(2)}) async-start(f32[4,2,32,512]{3,2,1,0:T(8,128)} %get-tuple-element.109), calls=%async_computation.1 | async-start | bytes 1048576 | tf_op jit(solution)/shard_map/all_to_all | solution.py:64
  96.0 6.5 %collective-permute-start.14 = (bf16[2,2,128,128]{3,2,1,0:T(8,128)(2,1)S(1)}, bf16[2,2,128,128]{3,2,1,0:T(8,128)(2,1)S(1)}, u32[]{:S(2)}, u32[]{:S(2)}) collective-permute-start(bf16[2,2,128,128]{3,2,1,0:T(8,128)(2,1)S(1)} %get-tuple-element.106), channel_id=1, source_target_pairs={{0,2},{1,3},{2,0},{3,1},{4,6},{5,7},{6,4},{7,5},{8,10},{9,11},{10,... | collective-permute-start | bytes 393224 | tf_op jit(solution)/shard_map/ppermute | solution.py:51
  96.0 11.3 %collective-permute-start.15 = (bf16[2,2,128,128]{3,2,1,0:T(8,128)(2,1)S(1)}, bf16[2,2,128,128]{3,2,1,0:T(8,128)(2,1)S(1)}, u32[]{:S(2)}, u32[]{:S(2)}) collective-permute-start(bf16[2,2,128,128]{3,2,1,0:T(8,128)(2,1)S(1)} %get-tuple-element.107), channel_id=1, source_target_pairs={{0,4},{1,5},{2,6},{3,7},{4,0},{5,1},{6,2},{7,3},{8,12},{9,13},{10,... | collective-permute-start | bytes 393224 | tf_op jit(solution)/shard_map/ppermute | solution.py:51
  98.8 8.5 %collective-permute-start.16 = (bf16[2,2,128,128]{3,2,1,0:T(8,128)(2,1)S(1)}, bf16[2,2,128,128]{3,2,1,0:T(8,128)(2,1)S(1)}, u32[]{:S(2)}, u32[]{:S(2)}) collective-permute-start(bf16[2,2,128,128]{3,2,1,0:T(8,128)(2,1)S(1)} %get-tuple-element.108), channel_id=1, source_target_pairs={{0,6},{1,7},{2,4},{3,5},{4,2},{5,3},{6,0},{7,1},{8,14},{9,15},{10,... | collective-permute-start | bytes 393224 | tf_op jit(solution)/shard_map/ppermute | solution.py:51
  107.3 2.4 %collective-permute-start.18 = (bf16[4,128,512]{2,1,0:T(8,128)(2,1)S(1)}, bf16[4,128,512]{2,1,0:T(8,128)(2,1)S(1)}, u32[]{:S(2)}, u32[]{:S(2)}) collective-permute-start(bf16[4,128,512]{2,1,0:T(8,128)(2,1)S(1)} %shard_map.138), channel_id=1, source_target_pairs={{0,1},{1,0},{2,3},{3,2},{4,5},{5,4},{6,7},{7,6},{8,9},{9,8},{10,11... | collective-permute-start | bytes 1572872 | tf_op jit(solution)/shard_map/ppermute | solution.py:51
  107.4 2.2 %collective-permute-start.17 = (bf16[4,2,128,128]{3,2,1,0:T(8,128)(2,1)S(1)}, bf16[4,2,128,128]{3,2,1,0:T(8,128)(2,1)S(1)}, u32[]{:S(2)}, u32[]{:S(2)}) collective-permute-start(bf16[4,2,128,128]{3,2,1,0:T(8,128)(2,1)S(1)} %shard_map.137), channel_id=1, source_target_pairs={{0,1},{1,0},{2,3},{3,2},{4,5},{5,4},{6,7},{7,6},{8,9},{9,8},{10,11... | collective-permute-start | bytes 786440 | tf_op jit(solution)/shard_map/ppermute | solution.py:51
  (13 other events, 112.7 us)

commit v6 on v5

--- a/solution.py
+++ b/solution.py
@@ -184,16 +184,16 @@
 
 
 def pool_kernel(lay, ctl, *refs):
-    *pieces, pool, slots = refs
+    pieces, pool, slots = refs[: lay.ways // 2], refs[lay.ways // 2], refs[lay.ways // 2 + 1 :]
     for j, piece in enumerate(pieces):
         for i in range(2):
             pool[2 * j + i, 0] = piece[i, 0]
             pool[2 * j + i, 1] = piece[i, 1]
             pool[2 * j + i, 2] = piece[i, 0].T
-    for s in range(lay.spans):
-        at = lay.send_index(ctl, s)
-        slots[s, 0] = pool[at, 0]
-        slots[s, 1] = pool[at, 1]
+    for k, slot in enumerate(slots):
+        at = lay.send_index(ctl, partner(ctl[1], k, lay.spans))
+        slot[0] = pool[at, 0]
+        slot[1] = pool[at, 1]
 
 
 def attention_kernel(lay, js, first, last, ctl, *refs):
@@ -202,7 +202,9 @@
     looped = len(js) > MAX_PERMUTES // 2
     qds = take(1 if looped else len(js))
     if first:
-        pool, slots, stats, mk, mv = take(5)
+        (pool,) = take(1)
+        slots = take(lay.spans)
+        stats, mk, mv = take(3)
     else:
         slot_pool, mkt, stats, mk, mv = take(5)
         prev = take(3)
@@ -219,10 +221,11 @@
         for total in (acc, dmk, dmv):
             total[...] = jnp.zeros_like(total)
         slot_pool[:ways] = pool[...]
-        for s in range(lay.spans):
-            slot_pool[ways + s, 0] = slots[s, 0]
-            slot_pool[ways + s, 1] = slots[s, 1]
-            slot_pool[ways + s, 2] = slots[s, 0].T
+        for k, slot in enumerate(slots):
+            at = ways + partner(ctl[1], k, lay.spans)
+            slot_pool[at, 0] = slot[0]
+            slot_pool[at, 1] = slot[1]
+            slot_pool[at, 2] = slot[0].T
         for h in heads:
             mkt[h] = mk[:, col(h)].T
     else:
@@ -428,20 +431,20 @@
         kv[1:], qd[last_far] = after(kv[1:], qd[last_far])
         qd[last_far] = swap(qd[last_far], 2 * last_far)
         (qd[1], qd[far]), kv[0] = after((qd[1], qd[far]), kv[0])
-    pool, slots = call(
+    pool, *slots = call(
         functools.partial(pool_kernel, lay),
         [
             array((lay.ways, 3, BLOCK, HEAD_FEATURES)),
-            array((lay.spans, 2, BLOCK, HEAD_FEATURES)),
+            *[array((2, BLOCK, HEAD_FEATURES))] * lay.spans,
         ],
         ctl,
         *kv,
     )
-    slots = to_spans(slots)
+    slots = across_spans(slots)
     stats = jnp.concatenate([row_lse, row_delta], axis=1)
     stats = stats.reshape(lay.ways, BLOCK, 2 * lay.heads).transpose(0, 2, 1)
 
-    totals, pools, dq = None, (pool, slots), {}
+    totals, pools, dq = None, (pool, *slots), {}
     for step in steps:
         last = step is steps[-1]
         step_dq, totals, pools, sent = attention(

time: 112 us -> 117 us (1.045)
  waiting for transfers between devices: 48.2 us -> 57.5 us
  local copies, waits for them, and re-layouts: 6.97 us -> 2.68 us
    ppermute x16, waiting for transfers between devices: 40.4 us -> 48.9 us  [swap(): lax.ppermute(piece, 'uly', [(i, i ^ k) for i in range(lax.axis_size('uly'...]
    ppermute x3 -> x6, waiting for transfers between devices: 2.43 us -> 8.63 us  [across_spans(): lax.ppermute(pieces[k], 'blk', pairs[k])]
    all_to_all x2 -> x1, waiting for transfers between devices: 5.35 us -> 0.01 us  [to_spans(): return lax.all_to_all(stacked, 'blk', 0, 0, tiled=True)]
    unnamed x33 -> x21, local copies, waits for them, and re-layouts: 6.87 us -> 2.58 us
    all_to_all x2 -> x1, starting transfers between devices: 7.19 us -> 3.47 us  [to_spans(): return lax.all_to_all(stacked, 'blk', 0, 0, tiled=True)]
    ppermute x3 -> x6, starting transfers between devices: 3.49 us -> 7.04 us  [across_spans(): lax.ppermute(pieces[k], 'blk', pairs[k])]
  transfers between devices with their start and end apart: 21 -> 23, of which waited for: 10 -> 15; matrix products, arithmetic and copies ran while one was open for 0% -> 0% of each run, Pallas kernels for 18% -> 17%
where the time goes in v6:
time: 117 us
  waiting for transfers between devices  57.5 us (49%)
  starting transfers between devices  32.7 us (28%)
  Pallas kernels  23.2 us (20%)
  local copies, waits for them, and re-layouts  2.68 us (2%)
    ppermute x16, waiting for transfers between devices, swap(): lax.ppermute(piece, 'uly', [(i, i ^ k) for i in range(lax.axis_size('uly'...  48.9 us
    pallas_call x12, Pallas kernels, call(): pl.pallas_call(kernel, in_specs=[SMEM_SPEC] + [pl.BlockSpec(memory_space=...  23.2 us
    ppermute x16, starting transfers between devices, swap(): lax.ppermute(piece, 'uly', [(i, i ^ k) for i in range(lax.axis_size('uly'...  22.2 us
    ppermute x6, waiting for transfers between devices, across_spans(): lax.ppermute(pieces[k], 'blk', pairs[k])  8.63 us
    ppermute x6, starting transfers between devices, across_spans(): lax.ppermute(pieces[k], 'blk', pairs[k])  7.04 us
    all_to_all x1, starting transfers between devices, to_spans(): return lax.all_to_all(stacked, 'blk', 0, 0, tiled=True)  3.47 us
    unnamed x21, local copies, waits for them, and re-layouts  2.58 us
  transfers between devices with their start and end apart: 23, of which 15 were waited for; matrix products, arithmetic and copies ran while one was open for 0% of the time, Pallas kernels for 17%

profile of v6, /device:TPU:0, one launch (start us, length us, event | category | flops | bytes accessed | tf_op | source)
XLA Modules:
  0.0 117.1 jit_solution(1165898581374304820)
XLA Ops:
  6.6 1.7 %shard_map.129 = (bf16[2,2,128,512]{3,2,1,0:T(8,128)(2,1)S(1)}, bf16[2,2,128,512]{3,2,1,0:T(8,128)(2,1)}, bf16[2,2,128,512]{3,2,1,0:T(8,128)(2,1)S(1)}, bf16[2,2,128,512]{3,2,1,0:T(8,128)(2,1)}) custom-call(s32[2]{0:T(128)S(1)} %pad_add_fusion.ctl, bf16[128,4096]{1,0:T(8,128)(2,1)S(1)} %copy-done.1, bf16[128,4096]{1,0:T(8,128)(2,1)S(1)} %copy-done.2, ...), custom_call_target="tpu_custom_call" | custom-call | tf_op jit(solution)/shard_map/pallas_call | solution.py:73
  8.3 2.9 %collective-permute-start.1 = (bf16[2,2,128,512]{3,2,1,0:T(8,128)(2,1)}, bf16[2,2,128,512]{3,2,1,0:T(8,128)(2,1)S(1)}, u32[]{:S(2)}, u32[]{:S(2)}) collective-permute-start(bf16[2,2,128,512]{3,2,1,0:T(8,128)(2,1)} %get-tuple-element.68), channel_id=1, source_target_pairs={{0,2},{1,3},{2,0},{3,1},{4,6},{5,7},{6,4},{7,5},{8,10},{9,11},{10,... | collective-permute-start | bytes 1572872 | tf_op jit(solution)/shard_map/ppermute | solution.py:51
  11.2 2.5 %collective-permute-start.2 = (bf16[2,2,128,512]{3,2,1,0:T(8,128)(2,1)}, bf16[2,2,128,512]{3,2,1,0:T(8,128)(2,1)S(1)}, u32[]{:S(2)}, u32[]{:S(2)}) collective-permute-start(bf16[2,2,128,512]{3,2,1,0:T(8,128)(2,1)} %get-tuple-element.69), channel_id=1, source_target_pairs={{0,6},{1,7},{2,4},{3,5},{4,2},{5,3},{6,0},{7,1},{8,14},{9,15},{10,... | collective-permute-start | bytes 1572872 | tf_op jit(solution)/shard_map/ppermute | solution.py:51
  16.3 2.5 %collective-permute-start.6 = (bf16[2,2,128,128]{3,2,1,0:T(8,128)(2,1)S(1)}, bf16[2,2,128,128]{3,2,1,0:T(8,128)(2,1)S(1)}, u32[]{:S(2)}, u32[]{:S(2)}) collective-permute-start(bf16[2,2,128,128]{3,2,1,0:T(8,128)(2,1)S(1)} %get-tuple-element.75), channel_id=1, source_target_pairs={{0,6},{1,7},{2,4},{3,5},{4,2},{5,3},{6,0},{7,1},{8,14},{9,15},{10,... | collective-permute-start | bytes 393224 | tf_op jit(solution)/shard_map/ppermute | solution.py:51
  18.8 21.1 %collective-permute-done.4.refs_1_ = bf16[2,2,128,128]{3,2,1,0:T(8,128)(2,1)S(1)} collective-permute-done((bf16[2,2,128,128]{3,2,1,0:T(8,128)(2,1)S(1)}, bf16[2,2,128,128]{3,2,1,0:T(8,128)(2,1)S(1)}, u32[]{:S(2)}, u32[]{:S(2)}) %collective-permute-start.4) | collective-permute-done | bytes 131104 | tf_op jit(solution)/shard_map/ppermute | solution.py:51
  39.8 6.6 %collective-permute-done.5.refs_2_ = bf16[2,2,128,128]{3,2,1,0:T(8,128)(2,1)S(1)} collective-permute-done((bf16[2,2,128,128]{3,2,1,0:T(8,128)(2,1)S(1)}, bf16[2,2,128,128]{3,2,1,0:T(8,128)(2,1)S(1)}, u32[]{:S(2)}, u32[]{:S(2)}) %collective-permute-start.5) | collective-permute-done | bytes 131104 | tf_op jit(solution)/shard_map/ppermute | solution.py:51
  46.4 3.7 %collective-permute-start.11 = (bf16[2,2,128,512]{3,2,1,0:T(8,128)(2,1)S(1)}, bf16[2,2,128,512]{3,2,1,0:T(8,128)(2,1)S(1)}, u32[]{:S(2)}, u32[]{:S(2)}) collective-permute-start(bf16[2,2,128,512]{3,2,1,0:T(8,128)(2,1)S(1)} %get-tuple-element.86), channel_id=1, source_target_pairs={{0,4},{1,5},{2,6},{3,7},{4,0},{5,1},{6,2},{7,3},{8,12},{9,13},{10,... | collective-permute-start | bytes 1572872 | tf_op jit(solution)/shard_map/ppermute | solution.py:51
  51.9 1.6 %collective-permute-start.7 = (bf16[2,128,128]{2,1,0:T(8,128)(2,1)S(1)}, bf16[2,128,128]{2,1,0:T(8,128)(2,1)S(1)}, u32[]{:S(2)}, u32[]{:S(2)}) collective-permute-start(bf16[2,128,128]{2,1,0:T(8,128)(2,1)S(1)} %get-tuple-element.82), channel_id=1, source_target_pairs={{0,8},{8,0},{16,24},{24,16},{1,9},{9,1},{17,25},{25,17},{2,10},{10... | collective-permute-start | bytes 196616 | tf_op jit(solution)/shard_map/ppermute | solution.py:58
  53.4 1.5 %collective-permute-start.8 = (bf16[2,128,128]{2,1,0:T(8,128)(2,1)S(1)}, bf16[2,128,128]{2,1,0:T(8,128)(2,1)S(1)}, u32[]{:S(2)}, u32[]{:S(2)}) collective-permute-start(bf16[2,128,128]{2,1,0:T(8,128)(2,1)S(1)} %get-tuple-element.83), channel_id=1, source_target_pairs={{0,16},{8,24},{16,0},{24,8},{1,17},{9,25},{17,1},{25,9},{2,18},{10... | collective-permute-start | bytes 196616 | tf_op jit(solution)/shard_map/ppermute | solution.py:58
  58.2 1.9 %collective-permute-done.9.refs_6_ = bf16[2,128,128]{2,1,0:T(8,128)(2,1)S(1)} collective-permute-done((bf16[2,128,128]{2,1,0:T(8,128)(2,1)S(1)}, bf16[2,128,128]{2,1,0:T(8,128)(2,1)S(1)}, u32[]{:S(2)}, u32[]{:S(2)}) %collective-permute-start.9) | collective-permute-done | bytes 65568 | tf_op jit(solution)/shard_map/ppermute | solution.py:58
  60.1 6.5 %shard_map.133 = (bf16[2,128,512]{2,1,0:T(8,128)(2,1)S(1)}, bf16[2,128,512]{2,1,0:T(8,128)(2,1)}, f32[12,2,128,128]{3,2,1,0:T(8,128)S(1)}, f32[128,512]{1,0:T(8,...) custom-call(s32[66]{0:T(128)S(1)} %pad_add_fusion.1.ctl, ...), custom_call_target="tpu_custom_call" | custom-call | tf_op jit(solution)/shard_map/pallas_call | solution.py:73
  66.7 3.3 %shard_map.134 = (bf16[2,128,512]{2,1,0:T(8,128)(2,1)S(1)}, f32[12,2,128,128]{3,2,1,0:T(8,128)S(1)}, f32[128,512]{1,0:T(8,128)S(1)}, f32[128,512]{1,0:T(8,128)S(1)}) custom-call(s32[66]{0:T(128)S(1)} %pad_add_fusion.1.ctl, bf16[2,2,128,512]{3,2,1,0:T(8,128)(2,1)S(1)} %collective-permute-done.2.refs_0_, ...), custom_call_target="tpu_custom_call" | custom-call | tf_op jit(solution)/shard_map/pallas_call | solution.py:73
  71.2 8.3 %collective-permute-done.11.refs_0_ = bf16[2,2,128,512]{3,2,1,0:T(8,128)(2,1)S(1)} collective-permute-done((bf16[2,2,128,512]{3,2,1,0:T(8,128)(2,1)S(1)}, bf16[2,2,128,512]{3,2,1,0:T(8,128)(2,1)S(1)}, u32[]{:S(2)}, u32[]{:S(2)}) %collective-permute-start.11) | collective-permute-done | bytes 524320 | tf_op jit(solution)/shard_map/ppermute | solution.py:51
  79.5 4.1 %shard_map.135 = (bf16[2,128,512]{2,1,0:T(8,128)(2,1)S(1)}, f32[12,2,128,128]{3,2,1,0:T(8,128)S(1)}, f32[128,512]{1,0:T(8,128)}, f32[128,512]{1,0:T(8,128)}, f32...) custom-call(s32[66]{0:T(128)S(1)} %pad_add_fusion.1.ctl, ...), custom_call_target="tpu_custom_call" | custom-call | tf_op jit(solution)/shard_map/pallas_call | solution.py:73
  85.0 1.5 %collective-permute-start.15 = (bf16[4,128,128]{2,1,0:T(8,128)(2,1)S(1)}, bf16[4,128,128]{2,1,0:T(8,128)(2,1)S(1)}, u32[]{:S(2)}, u32[]{:S(2)}) collective-permute-start(bf16[4,128,128]{2,1,0:T(8,128)(2,1)S(1)} %get-tuple-element.102), channel_id=1, source_target_pairs={{0,16},{8,24},{16,0},{24,8},{1,17},{9,25},{17,1},{25,9},{2,18},{10... | collective-permute-start | bytes 393224 | tf_op jit(solution)/shard_map/ppermute | solution.py:58
  90.0 2.4 %collective-permute-done.16.refs_3_ = bf16[4,128,128]{2,1,0:T(8,128)(2,1)S(1)} collective-permute-done((bf16[4,128,128]{2,1,0:T(8,128)(2,1)S(1)}, bf16[4,128,128]{2,1,0:T(8,128)(2,1)S(1)}, u32[]{:S(2)}, u32[]{:S(2)}) %collective-permute-start.16) | collective-permute-done | bytes 131104 | tf_op jit(solution)/shard_map/ppermute | solution.py:58
  92.4 2.1 %shard_map.136 = (bf16[2,2,128,128]{3,2,1,0:T(8,128)(2,1)S(1)}, bf16[2,2,128,128]{3,2,1,0:T(8,128)(2,1)S(1)}, bf16[2,2,128,128]{3,2,1,0:T(8,128)(2,1)S(1)}, bf16...) custom-call(s32[66]{0:T(128)S(1)} %pad_add_fusion.1.ctl, f32[12,2,128,128]{3,2,1,0:T(8,128)S(1)} %get-tuple-element.97.acc, ...), custom_call_target="tpu_custom_call" | custom-call | tf_op jit(solution)/shard_map/pallas_call | solution.py:73
  94.5 3.5 %all-to-all-start = ((f32[4,2,32,512]{3,2,1,0:T(8,128)}), f32[4,2,32,512]{3,2,1,0:T(8,128)S(1)}, u32[]{:S(2)}, u32[]{:S(2)}) async-start(f32[4,2,32,512]{3,2,1,0:T(8,128)} %get-tuple-element.115), calls=%async_computation | async-start | bytes 1048576 | tf_op jit(solution)/shard_map/all_to_all | solution.py:64
  98.0 4.5 %collective-permute-done.12.refs_2_.refs_7_ = bf16[2,128,512]{2,1,0:T(8,128)(2,1)S(1)} collective-permute-done((bf16[2,128,512]{2,1,0:T(8,128)(2,1)S(1)}, bf16[2,128,512]{2,1,0:T(8,128)(2,1)S(1)}, u32[]{:S(2)}, u32[]{:S(2)}) %collective-permute-start.12) | collective-permute-done | bytes 262176 | tf_op jit(solution)/shard_map/ppermute | solution.py:51
  102.5 3.1 %collective-permute-start.18 = (bf16[2,2,128,128]{3,2,1,0:T(8,128)(2,1)S(1)}, bf16[2,2,128,128]{3,2,1,0:T(8,128)(2,1)S(1)}, u32[]{:S(2)}, u32[]{:S(2)}) collective-permute-start(bf16[2,2,128,128]{3,2,1,0:T(8,128)(2,1)S(1)} %get-tuple-element.113), channel_id=1, source_target_pairs={{0,4},{1,5},{2,6},{3,7},{4,0},{5,1},{6,2},{7,3},{8,12},{9,13},{10,... | collective-permute-start | bytes 393224 | tf_op jit(solution)/shard_map/ppermute | solution.py:51
  106.9 1.9 %collective-permute-done.17.refs_1_ = bf16[2,2,128,128]{3,2,1,0:T(8,128)(2,1)S(1)} collective-permute-done((bf16[2,2,128,128]{3,2,1,0:T(8,128)(2,1)S(1)}, bf16[2,2,128,128]{3,2,1,0:T(8,128)(2,1)S(1)}, u32[]{:S(2)}, u32[]{:S(2)}) %collective-permute-start.17) | collective-permute-done | bytes 131104 | tf_op jit(solution)/shard_map/ppermute | solution.py:51
  110.0 2.5 %collective-permute-done.19.refs_3_ = bf16[2,2,128,128]{3,2,1,0:T(8,128)(2,1)S(1)} collective-permute-done((bf16[2,2,128,128]{3,2,1,0:T(8,128)(2,1)S(1)}, bf16[2,2,128,128]{3,2,1,0:T(8,128)(2,1)S(1)}, u32[]{:S(2)}, u32[]{:S(2)}) %collective-permute-start.19) | collective-permute-done | bytes 131104 | tf_op jit(solution)/shard_map/ppermute | solution.py:51
  113.2 1.7 %collective-permute-done.20.refs_4_ = bf16[4,2,128,128]{3,2,1,0:T(8,128)(2,1)S(1)} collective-permute-done((bf16[4,2,128,128]{3,2,1,0:T(8,128)(2,1)S(1)}, bf16[4,2,128,128]{3,2,1,0:T(8,128)(2,1)S(1)}, u32[]{:S(2)}, u32[]{:S(2)}) %collective-permute-start.20) | collective-permute-done | bytes 262176 | tf_op jit(solution)/shard_map/ppermute | solution.py:51
  114.9 2.2 %shard_map.139 = (bf16[128,4096]{1,0:T(8,128)(2,1)}, f32[128,1024]{1,0:T(8,128)}, f32[128,1024]{1,0:T(8,128)}, f32[128,512]{1,0:T(8,128)}, f32[128,512]{1,0:T(8,128)}) custom-call(s32[2]{0:T(128)S(1)} %pad_add_fusion.ctl, f32[4,2,32,512]{3,2,1,0:T(8,128)S(1)} %all-to-all-done.mem, bf16[2,2,128,128]{3,2,1,0:T(8,128)(2,1)S(1)} %get-tuple-element.121.refs_0_, ...), custom_call_target="tpu_custom_call" | custom-call | tf_op jit(solution)/shard_map/pallas_call | solution.py:73
  (59 shorter events, 22.8 us)
Async XLA Ops:
  3.8 2.8 %collective-permute-start = (bf16[4,2,128,512]{3,2,1,0:T(8,128)(2,1)S(1)}, bf16[4,2,128,512]{3,2,1,0:T(8,128)(2,1)S(1)}, u32[]{:S(2)}, u32[]{:S(2)}) collective-permute-start(bf16[4,2,128,512]{3,2,1,0:T(8,128)(2,1)S(1)} %shard_map.128), channel_id=1, source_target_pairs={{0,1},{1,0},{2,3},{3,2},{4,5},{5,4},{6,7},{7,6},{8,9},{9,8},{10,11... | collective-permute-start | bytes 3145736 | tf_op jit(solution)/shard_map/ppermute | solution.py:51
  5.0 55.1 %copy-start.3 = (bf16[128,512]{1,0:T(8,128)(2,1)S(1)}, bf16[128,512]{1,0:T(8,128)(2,1)}, u32[]{:S(2)}) copy-start(bf16[128,512]{1,0:T(8,128)(2,1)} %refs_4_.3) | copy-start | bytes 393220
  5.0 8.7 %collective-permute-start.3 = (bf16[4,2,128,128]{3,2,1,0:T(8,128)(2,1)S(1)}, bf16[4,2,128,128]{3,2,1,0:T(8,128)(2,1)S(1)}, u32[]{:S(2)}, u32[]{:S(2)}) collective-permute-start(bf16[4,2,128,128]{3,2,1,0:T(8,128)(2,1)S(1)} %shard_map.130), channel_id=1, source_target_pairs={{0,1},{1,0},{2,3},{3,2},{4,5},{5,4},{6,7},{7,6},{8,9},{9,8},{10,11... | collective-permute-start | bytes 786440 | tf_op jit(solution)/shard_map/ppermute | solution.py:51
  8.3 42.2 %collective-permute-start.1 = (bf16[2,2,128,512]{3,2,1,0:T(8,128)(2,1)}, bf16[2,2,128,512]{3,2,1,0:T(8,128)(2,1)S(1)}, u32[]{:S(2)}, u32[]{:S(2)}) collective-permute-start(bf16[2,2,128,512]{3,2,1,0:T(8,128)(2,1)} %get-tuple-element.68), channel_id=1, source_target_pairs={{0,2},{1,3},{2,0},{3,1},{4,6},{5,7},{6,4},{7,5},{8,10},{9,11},{10,... | collective-permute-start | bytes 1572872 | tf_op jit(solution)/shard_map/ppermute | solution.py:51
  11.2 39.2 %collective-permute-start.2 = (bf16[2,2,128,512]{3,2,1,0:T(8,128)(2,1)}, bf16[2,2,128,512]{3,2,1,0:T(8,128)(2,1)S(1)}, u32[]{:S(2)}, u32[]{:S(2)}) collective-permute-start(bf16[2,2,128,512]{3,2,1,0:T(8,128)(2,1)} %get-tuple-element.69), channel_id=1, source_target_pairs={{0,6},{1,7},{2,4},{3,5},{4,2},{5,3},{6,0},{7,1},{8,14},{9,15},{10,... | collective-permute-start | bytes 1572872 | tf_op jit(solution)/shard_map/ppermute | solution.py:51
  14.3 25.5 %collective-permute-start.4 = (bf16[2,2,128,128]{3,2,1,0:T(8,128)(2,1)S(1)}, bf16[2,2,128,128]{3,2,1,0:T(8,128)(2,1)S(1)}, u32[]{:S(2)}, u32[]{:S(2)}) collective-permute-start(bf16[2,2,128,128]{3,2,1,0:T(8,128)(2,1)S(1)} %get-tuple-element.73), channel_id=1, source_target_pairs={{0,2},{1,3},{2,0},{3,1},{4,6},{5,7},{6,4},{7,5},{8,10},{9,11},{10,... | collective-permute-start | bytes 393224 | tf_op jit(solution)/shard_map/ppermute | solution.py:51
  15.1 31.4 %collective-permute-start.5 = (bf16[2,2,128,128]{3,2,1,0:T(8,128)(2,1)S(1)}, bf16[2,2,128,128]{3,2,1,0:T(8,128)(2,1)S(1)}, u32[]{:S(2)}, u32[]{:S(2)}) collective-permute-start(bf16[2,2,128,128]{3,2,1,0:T(8,128)(2,1)S(1)} %get-tuple-element.74), channel_id=1, source_target_pairs={{0,4},{1,5},{2,6},{3,7},{4,0},{5,1},{6,2},{7,3},{8,12},{9,13},{10,... | collective-permute-start | bytes 393224 | tf_op jit(solution)/shard_map/ppermute | solution.py:51
  16.3 30.1 %collective-permute-start.6 = (bf16[2,2,128,128]{3,2,1,0:T(8,128)(2,1)S(1)}, bf16[2,2,128,128]{3,2,1,0:T(8,128)(2,1)S(1)}, u32[]{:S(2)}, u32[]{:S(2)}) collective-permute-start(bf16[2,2,128,128]{3,2,1,0:T(8,128)(2,1)S(1)} %get-tuple-element.75), channel_id=1, source_target_pairs={{0,6},{1,7},{2,4},{3,5},{4,2},{5,3},{6,0},{7,1},{8,14},{9,15},{10,... | collective-permute-start | bytes 393224 | tf_op jit(solution)/shard_map/ppermute | solution.py:51
  46.4 33.1 %collective-permute-start.11 = (bf16[2,2,128,512]{3,2,1,0:T(8,128)(2,1)S(1)}, bf16[2,2,128,512]{3,2,1,0:T(8,128)(2,1)S(1)}, u32[]{:S(2)}, u32[]{:S(2)}) collective-permute-start(bf16[2,2,128,512]{3,2,1,0:T(8,128)(2,1)S(1)} %get-tuple-element.86), channel_id=1, source_target_pairs={{0,4},{1,5},{2,6},{3,7},{4,0},{5,1},{6,2},{7,3},{8,12},{9,13},{10,... | collective-permute-start | bytes 1572872 | tf_op jit(solution)/shard_map/ppermute | solution.py:51
  51.9 4.9 %collective-permute-start.7 = (bf16[2,128,128]{2,1,0:T(8,128)(2,1)S(1)}, bf16[2,128,128]{2,1,0:T(8,128)(2,1)S(1)}, u32[]{:S(2)}, u32[]{:S(2)}) collective-permute-start(bf16[2,128,128]{2,1,0:T(8,128)(2,1)S(1)} %get-tuple-element.82), channel_id=1, source_target_pairs={{0,8},{8,0},{16,24},{24,16},{1,9},{9,1},{17,25},{25,17},{2,10},{10... | collective-permute-start | bytes 196616 | tf_op jit(solution)/shard_map/ppermute | solution.py:58
  53.4 4.8 %collective-permute-start.8 = (bf16[2,128,128]{2,1,0:T(8,128)(2,1)S(1)}, bf16[2,128,128]{2,1,0:T(8,128)(2,1)S(1)}, u32[]{:S(2)}, u32[]{:S(2)}) collective-permute-start(bf16[2,128,128]{2,1,0:T(8,128)(2,1)S(1)} %get-tuple-element.83), channel_id=1, source_target_pairs={{0,16},{8,24},{16,0},{24,8},{1,17},{9,25},{17,1},{25,9},{2,18},{10... | collective-permute-start | bytes 196616 | tf_op jit(solution)/shard_map/ppermute | solution.py:58
  54.9 5.2 %collective-permute-start.9 = (bf16[2,128,128]{2,1,0:T(8,128)(2,1)S(1)}, bf16[2,128,128]{2,1,0:T(8,128)(2,1)S(1)}, u32[]{:S(2)}, u32[]{:S(2)}) collective-permute-start(bf16[2,128,128]{2,1,0:T(8,128)(2,1)S(1)} %get-tuple-element.84), channel_id=1, source_target_pairs={{0,24},{8,16},{16,8},{24,0},{1,25},{9,17},{17,9},{25,1},{2,26},{10... | collective-permute-start | bytes 196616 | tf_op jit(solution)/shard_map/ppermute | solution.py:58
  70.0 22.5 %collective-permute-start.13 = (bf16[2,128,512]{2,1,0:T(8,128)(2,1)S(1)}, bf16[2,128,512]{2,1,0:T(8,128)(2,1)S(1)}, u32[]{:S(2)}, u32[]{:S(2)}) collective-permute-start(bf16[2,128,512]{2,1,0:T(8,128)(2,1)S(1)} %get-tuple-element.99), channel_id=1, source_target_pairs={{0,6},{1,7},{2,4},{3,5},{4,2},{5,3},{6,0},{7,1},{8,14},{9,15},{10,... | collective-permute-start | bytes 786440 | tf_op jit(solution)/shard_map/ppermute | solution.py:51
  83.5 5.0 %collective-permute-start.14 = (bf16[4,128,128]{2,1,0:T(8,128)(2,1)S(1)}, bf16[4,128,128]{2,1,0:T(8,128)(2,1)S(1)}, u32[]{:S(2)}, u32[]{:S(2)}) collective-permute-start(bf16[4,128,128]{2,1,0:T(8,128)(2,1)S(1)} %get-tuple-element.101), channel_id=1, source_target_pairs={{0,8},{8,0},{16,24},{24,16},{1,9},{9,1},{17,25},{25,17},{2,10},{10... | collective-permute-start | bytes 393224 | tf_op jit(solution)/shard_map/ppermute | solution.py:58
  85.0 5.0 %collective-permute-start.15 = (bf16[4,128,128]{2,1,0:T(8,128)(2,1)S(1)}, bf16[4,128,128]{2,1,0:T(8,128)(2,1)S(1)}, u32[]{:S(2)}, u32[]{:S(2)}) collective-permute-start(bf16[4,128,128]{2,1,0:T(8,128)(2,1)S(1)} %get-tuple-element.102), channel_id=1, source_target_pairs={{0,16},{8,24},{16,0},{24,8},{1,17},{9,25},{17,1},{25,9},{2,18},{10... | collective-permute-start | bytes 393224 | tf_op jit(solution)/shard_map/ppermute | solution.py:58
  86.6 5.9 %collective-permute-start.16 = (bf16[4,128,128]{2,1,0:T(8,128)(2,1)S(1)}, bf16[4,128,128]{2,1,0:T(8,128)(2,1)S(1)}, u32[]{:S(2)}, u32[]{:S(2)}) collective-permute-start(bf16[4,128,128]{2,1,0:T(8,128)(2,1)S(1)} %get-tuple-element.103), channel_id=1, source_target_pairs={{0,24},{8,16},{16,8},{24,0},{1,25},{9,17},{17,9},{25,1},{2,26},{10... | collective-permute-start | bytes 393224 | tf_op jit(solution)/shard_map/ppermute | solution.py:58
  87.0 11.0 %collective-permute-start.10 = (bf16[2,128,512]{2,1,0:T(8,128)(2,1)}, bf16[2,128,512]{2,1,0:T(8,128)(2,1)S(1)}, u32[]{:S(2)}, u32[]{:S(2)}) collective-permute-start(bf16[2,128,512]{2,1,0:T(8,128)(2,1)} %get-tuple-element.85), channel_id=1, source_target_pairs={{0,2},{1,3},{2,0},{3,1},{4,6},{5,7},{6,4},{7,5},{8,10},{9,11},{10,... | collective-permute-start | bytes 786440 | tf_op jit(solution)/shard_map/ppermute | solution.py:51
  88.5 14.0 %collective-permute-start.12 = (bf16[2,128,512]{2,1,0:T(8,128)(2,1)S(1)}, bf16[2,128,512]{2,1,0:T(8,128)(2,1)S(1)}, u32[]{:S(2)}, u32[]{:S(2)}) collective-permute-start(bf16[2,128,512]{2,1,0:T(8,128)(2,1)S(1)} %get-tuple-element.96), channel_id=1, source_target_pairs={{0,4},{1,5},{2,6},{3,7},{4,0},{5,1},{6,2},{7,3},{8,12},{9,13},{10,... | collective-permute-start | bytes 786440 | tf_op jit(solution)/shard_map/ppermute | solution.py:51
  94.5 18.0 %all-to-all-start = ((f32[4,2,32,512]{3,2,1,0:T(8,128)}), f32[4,2,32,512]{3,2,1,0:T(8,128)S(1)}, u32[]{:S(2)}, u32[]{:S(2)}) async-start(f32[4,2,32,512]{3,2,1,0:T(8,128)} %get-tuple-element.115), calls=%async_computation | async-start | bytes 1048576 | tf_op jit(solution)/shard_map/all_to_all | solution.py:64
  102.5 6.3 %collective-permute-start.17 = (bf16[2,2,128,128]{3,2,1,0:T(8,128)(2,1)S(1)}, bf16[2,2,128,128]{3,2,1,0:T(8,128)(2,1)S(1)}, u32[]{:S(2)}, u32[]{:S(2)}) collective-permute-start(bf16[2,2,128,128]{3,2,1,0:T(8,128)(2,1)S(1)} %get-tuple-element.112), channel_id=1, source_target_pairs={{0,2},{1,3},{2,0},{3,1},{4,6},{5,7},{6,4},{7,5},{8,10},{9,11},{10,... | collective-permute-start | bytes 393224 | tf_op jit(solution)/shard_map/ppermute | solution.py:51
  102.5 7.5 %collective-permute-start.18 = (bf16[2,2,128,128]{3,2,1,0:T(8,128)(2,1)S(1)}, bf16[2,2,128,128]{3,2,1,0:T(8,128)(2,1)S(1)}, u32[]{:S(2)}, u32[]{:S(2)}) collective-permute-start(bf16[2,2,128,128]{3,2,1,0:T(8,128)(2,1)S(1)} %get-tuple-element.113), channel_id=1, source_target_pairs={{0,4},{1,5},{2,6},{3,7},{4,0},{5,1},{6,2},{7,3},{8,12},{9,13},{10,... | collective-permute-start | bytes 393224 | tf_op jit(solution)/shard_map/ppermute | solution.py:51
  105.6 6.9 %collective-permute-start.19 = (bf16[2,2,128,128]{3,2,1,0:T(8,128)(2,1)S(1)}, bf16[2,2,128,128]{3,2,1,0:T(8,128)(2,1)S(1)}, u32[]{:S(2)}, u32[]{:S(2)}) collective-permute-start(bf16[2,2,128,128]{3,2,1,0:T(8,128)(2,1)S(1)} %get-tuple-element.114), channel_id=1, source_target_pairs={{0,6},{1,7},{2,4},{3,5},{4,2},{5,3},{6,0},{7,1},{8,14},{9,15},{10,... | collective-permute-start | bytes 393224 | tf_op jit(solution)/shard_map/ppermute | solution.py:51
  112.5 2.4 %collective-permute-start.21 = (bf16[4,128,512]{2,1,0:T(8,128)(2,1)S(1)}, bf16[4,128,512]{2,1,0:T(8,128)(2,1)S(1)}, u32[]{:S(2)}, u32[]{:S(2)}) collective-permute-start(bf16[4,128,512]{2,1,0:T(8,128)(2,1)S(1)} %shard_map.138), channel_id=1, source_target_pairs={{0,1},{1,0},{2,3},{3,2},{4,5},{5,4},{6,7},{7,6},{8,9},{9,8},{10,11... | collective-permute-start | bytes 1572872 | tf_op jit(solution)/shard_map/ppermute | solution.py:51
  112.6 2.2 %collective-permute-start.20 = (bf16[4,2,128,128]{3,2,1,0:T(8,128)(2,1)S(1)}, bf16[4,2,128,128]{3,2,1,0:T(8,128)(2,1)S(1)}, u32[]{:S(2)}, u32[]{:S(2)}) collective-permute-start(bf16[4,2,128,128]{3,2,1,0:T(8,128)(2,1)S(1)} %shard_map.137), channel_id=1, source_target_pairs={{0,1},{1,0},{2,3},{3,2},{4,5},{5,4},{6,7},{7,6},{8,9},{9,8},{10,11... | collective-permute-start | bytes 786440 | tf_op jit(solution)/shard_map/ppermute | solution.py:51
  (9 other events, 209.4 us)
